TPU v7x, 256 devices: a whole 4x4x8 slice. The times are simulated.
256 devices in a mesh: front: 16 (over z, core), tile: 16 (over x, y).
Axes of the slice: x: 4, y: 4, z: 8, core: 2. Of those that a mesh axis runs over, the one named last changes fastest.
Arguments:
- child_front: float32 [16, 8192, 1536], P('front', 'tile')
- parent_front: float32 [16, 8192, 512], P('front', 'tile')
- child_map: int32 [16, 60], replicated, may hold values from 1 to 62, as said below
Outputs:
- child_panel: float32 [16, 8192, 512], P('front', 'tile')
- parent_result: float32 [16, 8192, 512], P('front', 'tile')
Inputs may be any that keep to these rules, and one draw needn't show every extreme that they name: child_map[f] is strictly increasing: each child's Schur tiles go, in order, to distinct parent tiles; parent tile 0 and the last parent tile receive nothing.
All inputs are finite; a program needn't handle non-finite values.
Results may differ from a plain program's by a relative error of at most 0.00028.
Values sent between devices are 32-bit elements; how exact they have to be, the bound alone decides.
No kernel may reach another device: no remote copies, remote signals or barrier semaphores. Data moves between devices by JAX's collectives and lax.ppermute only.
A program may use at most 64 MiB of HBM per device.

v0:
```python
import jax
import jax.numpy as jnp
from jax import lax
from jax.sharding import PartitionSpec as P

TILE_ROWS = 128
PIVOTS = 512
HALF_COLS = 512


def from_root(value, axis, source):
    kept = jnp.where(lax.axis_index(axis) == source, value, 0).astype(value.dtype)
    return lax.psum(kept, axis)


def shifted(x, axis, by):
    peers = lax.axis_size(axis)
    pairs = [(i, i + by) for i in range(peers) if 0 <= i + by < peers]
    return lax.ppermute(x, axis, pairs)


def from_partner(block, axis, stride):
    count = lax.axis_size(axis)
    route = []
    for low in range(count):
        high = low | 1 << stride
        if high != low and high < count:
            route += [(low, high), (high, low)]
    return lax.ppermute(block, axis, route)


def factor_block(block_vals):
    return jnp.linalg.cholesky(block_vals)


def panel_solve(columns, factor):
    return lax.linalg.triangular_solve(
        factor, columns, left_side=False, lower=True, transpose_a=True
    )


def times_rows(panel, top_rows):
    return lax.dot_general(
        panel, top_rows, (((1,), (1,)), ((), ())), precision=lax.Precision.HIGHEST
    )


def placing(child_map, child_idx, my_tile, per_dev, pivot_tiles):
    map_row = lax.dynamic_index_in_dim(child_map, child_idx, 0, keepdims=False)
    global_ids = my_tile * per_dev + jnp.arange(per_dev)
    schur_ids = global_ids - pivot_tiles
    targets = jnp.take(map_row, jnp.maximum(schur_ids, 0))
    valid = schur_ids >= 0
    places = targets - (my_tile - 1) * per_dev
    select = (places[None, :] == jnp.arange(2 * per_dev)[:, None]) & valid[None, :]
    return select.astype(jnp.float32)


def place_rows(select, row_vals):
    per_dev = select.shape[1]
    tiles = row_vals.reshape(per_dev, -1)
    return jnp.dot(select, tiles, precision=lax.Precision.HIGHEST)


def split_halves(buffer, per_dev, rows_here, width):
    lower = buffer[:per_dev].reshape(rows_here, width)
    upper = buffer[per_dev:].reshape(rows_here, width)
    return (lower, upper)


def local(child_front, parent_front, child_map):
    my_tile = lax.axis_index("tile")
    my_front = lax.axis_index("front")
    parity = my_front % 2
    half_idx = 1 - parity
    child_vals = child_front[0]
    parent_vals = parent_front[0]
    rows_here = child_vals.shape[0]
    width_all = child_vals.shape[1]
    tiles_here = rows_here // TILE_ROWS
    pivot_tiles = PIVOTS // TILE_ROWS
    child_block = from_root(child_vals[:PIVOTS, :PIVOTS], "tile", 0)
    child_factor = factor_block(child_block)
    child_panel = panel_solve(child_vals[:, :PIVOTS], child_factor)
    child_roots = -(-width_all // rows_here)

    def child_gather(counter, accum):
        arrived = from_root(child_panel, "tile", counter)
        return lax.dynamic_update_slice_in_dim(accum, arrived, counter * rows_here, 0)

    child_top = lax.fori_loop(
        0, child_roots, child_gather, jnp.zeros((child_roots * rows_here, PIVOTS), jnp.float32)
    )
    schur = child_vals[:, PIVOTS:] - times_rows(child_panel, child_top[PIVOTS:width_all])
    own_select = placing(child_map, my_front, my_tile, tiles_here, pivot_tiles)
    buffer = place_rows(own_select, schur)
    lower, upper = split_halves(buffer, tiles_here, rows_here, 2 * HALF_COLS)
    summed = upper + shifted(lower, "tile", -1)
    keep_half = lax.dynamic_slice_in_dim(summed, half_idx * HALF_COLS, HALF_COLS, 1)
    send_half = lax.dynamic_slice_in_dim(summed, parity * HALF_COLS, HALF_COLS, 1)
    contrib = keep_half + from_partner(send_half, "front", 0)
    assembled = parent_vals + contrib
    parent_block = from_root(assembled, "tile", 0)
    parent_factor = factor_block(parent_block)
    own_panel = panel_solve(assembled, parent_factor)
    moved_panel = shifted(own_panel, "front", -1)
    parent_panel = jnp.where(half_idx == 0, own_panel, moved_panel)
    parent_roots = -(-(2 * HALF_COLS) // rows_here)

    def parent_gather(counter, accum):
        arrived = from_root(parent_panel, "tile", counter)
        return lax.dynamic_update_slice_in_dim(accum, arrived, counter * rows_here, 0)

    parent_top = lax.fori_loop(
        0, parent_roots, parent_gather, jnp.zeros((parent_roots * rows_here, PIVOTS), jnp.float32)
    )
    needed_rows = lax.dynamic_slice_in_dim(parent_top, half_idx * HALF_COLS, HALF_COLS, 0)
    updated = assembled - times_rows(parent_panel, needed_rows)
    column_ids = half_idx * HALF_COLS + jnp.arange(HALF_COLS)
    result_vals = jnp.where(column_ids[None, :] < PIVOTS, parent_panel, updated)
    return (child_panel[None], result_vals[None])


def solution(mesh):
    return jax.shard_map(
        local,
        mesh=mesh,
        in_specs=(P("front", "tile", None), P("front", "tile", None), P()),
        out_specs=(P("front", "tile", None), P("front", "tile", None)),
        check_vma=False,
    )
```

profile of v0, /device:TPU:32, one launch (start us, length us, event | category | flops | bytes accessed | tf_op | source)
XLA Modules:
  0.0 1141.6 jit_solution(3679018719515833547)
XLA Ops:
  7.2 2.4 copy.15
  11.6 100.1 %all-reduce.6.cloned.1.call-done = f32[512,512]{0,1:T(8,128)} async-done(((f32[512,512]{0,1:T(8,128)}), f32[512,512]{0,1:T(8,128)}) %all-reduce.6.cloned.1.call-update) | async-done | bytes 1048592 | tf_op jit(solution)/shard_map/psum | solution.py:13
  111.7 2.5 copy.16
  114.2 1.8 fusion.7
  116.9 11.7 %cholesky.286 = f32[128,128]{1,0:T(8,128)S(1)} custom-call(f32[128,128]{1,0:T(8,128)S(1)} %cholesky.426), custom_call_target="Cholesky" | custom-call | tf_op jit(solution)/shard_map/jit(cholesky)/cholesky | solution.py:33
  129.8 9.8 custom-call.27
  139.6 1.9 constant_dynamic-update-slice_fusion.7
  142.8 11.7 %cholesky.305 = f32[128,128]{1,0:T(8,128)S(1)} custom-call(f32[128,128]{1,0:T(8,128)S(1)} %cholesky.430), custom_call_target="Cholesky" | custom-call | tf_op jit(solution)/shard_map/jit(cholesky)/cholesky | solution.py:33
  155.1 9.9 custom-call.28
  167.4 11.7 %cholesky.326 = f32[128,128]{1,0:T(8,128)S(1)} custom-call(f32[128,128]{1,0:T(8,128)S(1)} %cholesky.435), custom_call_target="Cholesky" | custom-call | tf_op jit(solution)/shard_map/jit(cholesky)/cholesky | solution.py:33
  179.8 9.8 custom-call.29
  191.9 11.7 %cholesky.343 = f32[128,128]{1,0:T(8,128)S(1)} custom-call(f32[128,128]{1,0:T(8,128)S(1)} %convolution_subtract_fusion.9), custom_call_target="Cholesky" | custom-call | tf_op jit(solution)/shard_map/jit(cholesky)/cholesky | solution.py:33
  208.9 2.3 select_select_fusion.1
  211.2 11.2 while.36
  211.8 2.2 bitcast_dynamic-update-slice_fusion.4
  214.6 2.2 bitcast_dynamic-update-slice_fusion.4
  217.4 2.2 bitcast_dynamic-update-slice_fusion.4
  220.3 2.1 bitcast_dynamic-update-slice_fusion.4
  222.4 39.9 %custom-call.30 = f32[4,128,128]{1,2,0:T(8,128)} custom-call(f32[4,128,128]{2,1,0:T(8,128)S(1)} %get-tuple-element.196), custom_call_target="InvertDiagBlocksLowerTriangular" | custom-call | tf_op jit(solution)/shard_map/triangular_solve/custom-call.3 | solution.py:37
  266.2 1.4 convolution_subtract_fusion.1
  268.1 1.7 convolution_subtract_fusion.3
  271.8 2.1 broadcast_in_dim.55
  273.9 309.8 %while.34 = (s32[]{:T(128)}, f32[1536,512]{1,0:T(8,128)}, f32[512,512]{1,0:T(8,128)S(1)}, s32[]{:T(128)}, u32[]{:T(128)}, /*index=5*/s32[]{:T(128)}, s32[]{:T(128)}, s32[]{:T(128)}) while((s32[]{:T(128)}, f32[1536,512]{1,0:T(8,128)}, f32[512,512]{1,0:T(8,128)S(1)}, s32[]{:T(128)}, u32[]{:T(128)}, /*index=5*/s32[]{:T(128)}, s32[]{:T(128)}, ...), condition=%wide.region_11.14_spmd, body=%wide.region_9.13_spmd.sunk | while | flops 524297 | bytes 10485973 | solution.py:91
  275.0 100.0 %all-reduce.10.cloned.1.call-done = f32[512,512]{1,0:T(8,128)} async-done(((f32[512,512]{1,0:T(8,128)}), f32[512,512]{1,0:T(8,128)}) %all-reduce.10.cloned.1.call-update) | async-done | bytes 1048592 | tf_op jit(solution)/shard_map/while/body/eval_jaxpr/psum | solution.py:13
  375.0 2.3 constant_dynamic-update-slice_fusion.12
  378.3 100.0 %all-reduce.10.cloned.1.call-done = f32[512,512]{1,0:T(8,128)} async-done(((f32[512,512]{1,0:T(8,128)}), f32[512,512]{1,0:T(8,128)}) %all-reduce.10.cloned.1.call-update) | async-done | bytes 1048592 | tf_op jit(solution)/shard_map/while/body/eval_jaxpr/psum | solution.py:13
  478.3 2.3 constant_dynamic-update-slice_fusion.12
  481.7 99.7 %all-reduce.10.cloned.1.call-done = f32[512,512]{1,0:T(8,128)} async-done(((f32[512,512]{1,0:T(8,128)}), f32[512,512]{1,0:T(8,128)}) %all-reduce.10.cloned.1.call-update) | async-done | bytes 1048592 | tf_op jit(solution)/shard_map/while/body/eval_jaxpr/psum | solution.py:13
  581.4 2.3 constant_dynamic-update-slice_fusion.12
  583.7 5.8 slice_subtract_fusion
  589.5 2.3 copy.20
  591.8 3.0 reshape.86
  594.8 2.2 fusion.67
  597.0 2.6 fusion.82
  599.7 3.0 reshape.88
  602.7 1.8 copy.21
  605.8 3.0 reshape.87
  608.9 1.9 copy.22
  610.7 41.8 %collective-permute-done = f32[512,1024]{0,1:T(8,128)} collective-permute-done((f32[512,1024]{0,1:T(8,128)}, f32[512,1024]{0,1:T(8,128)}, u32[]{:S(2)}, u32[]{:S(2)}) %collective-permute-start) | collective-permute-done | bytes 2097184 | tf_op jit(solution)/shard_map/ppermute | solution.py:19
  652.6 2.7 add.187
  655.6 2.5 copy.17
  658.4 2.9 broadcast_select_fusion.2
  661.3 98.5 %all-reduce.8.cloned.1.call-done = f32[512,512]{0,1:T(8,128)} async-done(((f32[512,512]{0,1:T(8,128)}), f32[512,512]{0,1:T(8,128)}) %all-reduce.8.cloned.1.call-update) | async-done | bytes 1048592 | tf_op jit(solution)/shard_map/psum | solution.py:13
  759.9 1.6 copy.23
  762.7 11.7 %cholesky.358 = f32[128,128]{1,0:T(8,128)S(1)} custom-call(f32[128,128]{1,0:T(8,128)S(1)} %cholesky.439), custom_call_target="Cholesky" | custom-call | tf_op jit(solution)/shard_map/jit(cholesky)/cholesky | solution.py:33
  774.6 9.8 custom-call.31
  786.9 11.7 %cholesky.377 = f32[128,128]{1,0:T(8,128)S(1)} custom-call(f32[128,128]{1,0:T(8,128)S(1)} %cholesky.443), custom_call_target="Cholesky" | custom-call | tf_op jit(solution)/shard_map/jit(cholesky)/cholesky | solution.py:33
  798.7 10.0 custom-call.32
  810.3 11.7 %cholesky.398 = f32[128,128]{1,0:T(8,128)S(1)} custom-call(f32[128,128]{1,0:T(8,128)S(1)} %cholesky.448), custom_call_target="Cholesky" | custom-call | tf_op jit(solution)/shard_map/jit(cholesky)/cholesky | solution.py:33
  822.0 9.8 custom-call.33
  833.3 11.9 %cholesky.415 = f32[128,128]{1,0:T(8,128)S(1)} custom-call(f32[128,128]{1,0:T(8,128)S(1)} %convolution_subtract_fusion.8), custom_call_target="Cholesky" | custom-call | tf_op jit(solution)/shard_map/jit(cholesky)/cholesky | solution.py:33
  850.6 8.5 while.37
  859.1 39.3 %custom-call.34 = f32[4,128,128]{1,2,0:T(8,128)S(1)} custom-call(f32[4,128,128]{2,1,0:T(8,128)S(1)} %get-tuple-element.197), custom_call_target="InvertDiagBlocksLowerTriangular" | custom-call | tf_op jit(solution)/shard_map/triangular_solve/custom-call.3 | solution.py:37
  901.4 1.7 fusion.14
  905.4 1.9 collective-permute-start.2
  908.7 11.3 collective-permute-done.2
  920.0 1.5 broadcast_select_fusion.3
  921.8 1.6 broadcast_in_dim.56
  923.4 206.5 %while.35 = (s32[]{:T(128)}, f32[1024,512]{1,0:T(8,128)}, f32[512,512]{1,0:T(8,128)S(1)}, s32[]{:T(128)}, u32[]{:T(128)}, /*index=5*/s32[]{:T(128)}, s32[]{:T(128)}, s32[]{:T(128)}) while((s32[]{:T(128)}, f32[1024,512]{1,0:T(8,128)}, f32[512,512]{1,0:T(8,128)S(1)}, s32[]{:T(128)}, u32[]{:T(128)}, /*index=5*/s32[]{:T(128)}, s32[]{:T(128)}, ...), condition=%wide.region_15.18_spmd, body=%wide.region_13.17_spmd.sunk | while | flops 524297 | bytes 10485973 | solution.py:114
  924.5 99.7 %all-reduce.12.cloned.1.call-done = f32[512,512]{1,0:T(8,128)} async-done(((f32[512,512]{1,0:T(8,128)}), f32[512,512]{1,0:T(8,128)}) %all-reduce.12.cloned.1.call-update) | async-done | bytes 1048592 | tf_op jit(solution)/shard_map/while/body/eval_jaxpr/psum | solution.py:13
  1024.2 2.3 constant_dynamic-update-slice_fusion.13
  1027.6 100.0 %all-reduce.12.cloned.1.call-done = f32[512,512]{1,0:T(8,128)} async-done(((f32[512,512]{1,0:T(8,128)}), f32[512,512]{1,0:T(8,128)}) %all-reduce.12.cloned.1.call-update) | async-done | bytes 1048592 | tf_op jit(solution)/shard_map/while/body/eval_jaxpr/psum | solution.py:13
  1127.5 2.3 constant_dynamic-update-slice_fusion.13
  1129.9 3.1 fusion.5
  (136 shorter events, 56.2 us)
Async XLA Ops:
  7.2 3.7 copy-start
  7.2 104.5 %all-reduce.6.cloned.1.call-start = ((), (), s32[]{:S(2)}) async-start(), calls=%async_computation | async-start | bytes 2097152 | tf_op jit(solution)/shard_map/psum | solution.py:13
  9.6 258.5 %copy-start.2 = (f32[1,512,1536]{1,2,0:T(8,128)}, f32[1,512,1536]{1,2,0:T(8,128)S(1)}, u32[]{:S(2)}) copy-start(f32[1,512,1536]{1,2,0:T(8,128)S(1)} %copy.15) | copy-start | bytes 9437188
  115.9 1.0 copy-start.10
  262.3 5.3 copy-start.12
  266.2 5.3 copy-start.3
  268.1 3.4 copy-start.7
  273.9 309.8 %copy-start.4 = (f32[512,128]{0,1:T(8,128)S(1)}, f32[512,128]{0,1:T(8,128)}, u32[]{:S(2)}) copy-start(f32[512,128]{0,1:T(8,128)} %copy-done.3) | copy-start | bytes 786436
  273.9 309.8 %copy-start.8 = (f32[512,128]{0,1:T(8,128)S(1)}, f32[512,128]{0,1:T(8,128)}, u32[]{:S(2)}) copy-start(f32[512,128]{0,1:T(8,128)} %copy-done.7) | copy-start | bytes 786436
  273.9 101.1 %all-reduce.10.cloned.1.call-start = ((), (), s32[]{:S(2)}) async-start(), calls=%async_computation.2 | async-start | bytes 2097152 | tf_op jit(solution)/shard_map/while/body/eval_jaxpr/psum | solution.py:13
  377.3 101.1 %all-reduce.10.cloned.1.call-start = ((), (), s32[]{:S(2)}) async-start(), calls=%async_computation.2 | async-start | bytes 2097152 | tf_op jit(solution)/shard_map/while/body/eval_jaxpr/psum | solution.py:13
  480.6 100.8 %all-reduce.10.cloned.1.call-start = ((), (), s32[]{:S(2)}) async-start(), calls=%async_computation.2 | async-start | bytes 2097152 | tf_op jit(solution)/shard_map/while/body/eval_jaxpr/psum | solution.py:13
  583.7 176.2 %all-reduce.8.cloned.1.call-start = ((), (), s32[]{:S(2)}) async-start(), calls=%async_computation.1 | async-start | bytes 2097152 | tf_op jit(solution)/shard_map/psum | solution.py:13
  604.5 48.1 %collective-permute-start = (f32[512,1024]{0,1:T(8,128)}, f32[512,1024]{0,1:T(8,128)}, u32[]{:S(2)}, u32[]{:S(2)}) collective-permute-start(f32[512,1024]{0,1:T(8,128)} %copy.21), channel_id=1, source_target_pairs={{1,0},{2,1},{3,2},{4,3},{5,4},{6,5},{7,6},{8,7},{9,8},{10,9},{11,1... | collective-permute-start | bytes 6291464 | tf_op jit(solution)/shard_map/ppermute | solution.py:19
  655.4 3.1 collective-permute-start.1
  759.9 1.7 copy-start.6
  761.7 1.0 copy-start.11
  859.1 39.8 %copy-start.9 = (f32[512,512]{1,0:T(8,128)}, f32[512,512]{1,0:T(8,128)S(1)}, u32[]{:S(2)}) copy-start(f32[512,512]{1,0:T(8,128)S(1)} %get-tuple-element.469) | copy-start | bytes 3145732
  898.4 2.6 copy-start.13
  901.4 5.9 copy-start.5
  905.4 14.5 %collective-permute-start.2 = (f32[512,512]{0,1:T(8,128)}, f32[512,512]{0,1:T(8,128)}, u32[]{:S(2)}, u32[]{:S(2)}) collective-permute-start(f32[512,512]{0,1:T(8,128)} %pad_maximum_fusion.1), channel_id=1, source_target_pairs={{16,0},{32,16},{48,32},{64,48},{80,64},{96,80},{112,96},{128,112},... | collective-permute-start | bytes 3145736 | tf_op jit(solution)/shard_map/ppermute | solution.py:19
  923.4 100.8 %all-reduce.12.cloned.1.call-start = ((), (), s32[]{:S(2)}) async-start(), calls=%async_computation.3 | async-start | bytes 2097152 | tf_op jit(solution)/shard_map/while/body/eval_jaxpr/psum | solution.py:13
  1026.5 101.1 %all-reduce.12.cloned.1.call-start = ((), (), s32[]{:S(2)}) async-start(), calls=%async_computation.3 | async-start | bytes 2097152 | tf_op jit(solution)/shard_map/while/body/eval_jaxpr/psum | solution.py:13
  1129.9 4.4 copy-start.1
Sparse Core Ops, SparseCore 0:
  11.8 99.7 all-reduce.5
  278.5 96.3 all-reduce.9
  381.9 96.3 all-reduce.9
  484.9 96.3 all-reduce.9
  661.5 98.3 all-reduce.7
  927.7 96.4 all-reduce.11
  1031.1 96.3 all-reduce.11
where the time goes:
time: 1150 us; the launch traced here: 1140 us
  waiting for transfers between devices  751 us (65%)
  other arithmetic  260 us (23%)
  local copies, waits for them, and re-layouts  68.7 us (6%)
  matrix products  38 us (3%)
  between operations  20.2 us (2%)
    psum x7, waiting for transfers between devices, from_root(): return lax.psum(kept, axis)  698 us
    another operation x29, other arithmetic, factor_block(): return jnp.linalg.cholesky(block_vals)  160 us
    another operation x7, other arithmetic, panel_solve(): lax.linalg.triangular_solve(factor, columns, left_side=False, lower=True,...  84 us
    ppermute x2, waiting for transfers between devices, shifted(): return lax.ppermute(x, axis, pairs)  53.1 us
  transfers between devices with their start and end apart: 10, of which 10 were waited for; matrix products, arithmetic and copies ran while one was open for 1% of the time, Pallas kernels for 0%

commit v1 on v0

v1 whole, which is shorter than its diff:
```python
import jax
import jax.numpy as jnp
from jax import lax
from jax.experimental import pallas as pl
from jax.experimental.pallas import tpu as pltpu
from jax.sharding import PartitionSpec as P

B = 128
N = 512
NT = ((1,), (1,))
NN = ((1,), (0,))
F32 = jnp.float32
VMEM = pl.BlockSpec(memory_space=pltpu.VMEM)
SMEM = pl.BlockSpec(memory_space=pltpu.SMEM)
PARAMS = pltpu.CompilerParams(vmem_limit_bytes=48 * 1024 * 1024)


def row_of(v, j):
    return jnp.broadcast_to(v[j : j + 1, :], v.shape)


def column_of(v, j):
    return jnp.broadcast_to(v[:, j : j + 1], (v.shape[0], B))


def inverse_factor(rows_at):
    sub = lax.broadcasted_iota(jnp.int32, (8, B), 0)
    lane = lax.broadcasted_iota(jnp.int32, (8, B), 1)
    left = [rows_at(q) for q in range(16)]
    right = [jnp.where(lane == sub + 8 * q, 1.0, 0.0).astype(F32) for q in range(16)]
    out = []
    for p in range(16):
        cols = [column_of(left[p], 8 * p + j) for j in range(8)]
        v, xv, xf = left[p], right[p], right[p]
        diag = jnp.zeros((8, B), F32)
        for j in range(8):
            pivot = row_of(cols[j], j)
            recip = 1.0 / pivot
            diag = jnp.where(sub == j, pivot, diag)
            scale = jnp.where(sub == j, 0.0, cols[j]) * recip
            below = jnp.where(sub > j, cols[j], 0.0) * recip
            for m in range(j + 1, 8):
                cm = row_of(cols[m], j)
                cols[m] = jnp.where(sub == j, cm * recip, cols[m] - scale * cm)
            vr, xr, fr = row_of(v, j), row_of(xv, j), row_of(xf, j)
            v = jnp.where(sub == j, vr * recip, v - scale * vr)
            xv = jnp.where(sub == j, xr * recip, xv - scale * xr)
            xf = xf - below * fr
        out.append(xf * lax.rsqrt(diag))
        if p < 15:
            w = [row_of(v, j) for j in range(8)]
            xw = [row_of(xv, j) for j in range(8)]
            for q in range(p + 1, 16):
                c = [column_of(left[q], 8 * p + j) for j in range(8)]
                s, x = c[0] * w[0], c[0] * xw[0]
                for j in range(1, 8):
                    s = s + c[j] * w[j]
                    x = x + c[j] * xw[j]
                left[q] = left[q] - s
                right[q] = right[q] - x
    return jnp.concatenate(out, axis=0)


def dot_f32(a, b, dims):
    return lax.dot_general(
        a, b, (dims, ((), ())), precision=lax.Precision.HIGHEST, preferred_element_type=F32
    )


def at(i):
    return pl.ds(pl.multiple_of(i * B, B), B)


def factor_kernel(rows, a_ref, x_ref, s_ref, l_ref):
    l_ref[...] = a_ref[:, :rows, :].reshape(N, N)
    for i in range(4):
        for j in range(i + 1):
            s_ref[i * B : (i + 1) * B, j * B : (j + 1) * B] = 0.5 * (
                l_ref[i * B : (i + 1) * B, j * B : (j + 1) * B]
                + l_ref[j * B : (j + 1) * B, i * B : (i + 1) * B].T
            )
    x_ref[...] = jnp.zeros_like(x_ref)

    def step(k, carry):
        k0 = pl.multiple_of(k * B, B)
        xk = inverse_factor(lambda q: s_ref[pl.ds(pl.multiple_of(k0 + 8 * q, 8), 8), at(k)])
        x_ref[at(k), at(k)] = xk

        def x_row(j, carry):
            def acc(m, t):
                return t + dot_f32(l_ref[at(k), at(m)], x_ref[at(m), at(j)], NN)

            t = lax.fori_loop(j, k, acc, jnp.zeros((B, B), F32))
            x_ref[at(k), at(j)] = -dot_f32(xk, t, NN)
            return carry

        lax.fori_loop(0, k, x_row, 0)

        def l_col(i, carry):
            l_ref[at(i), at(k)] = dot_f32(s_ref[at(i), at(k)], xk, NT)

            def update(j, carry):
                s_ref[at(i), at(j)] -= dot_f32(l_ref[at(i), at(k)], l_ref[at(j), at(k)], NT)
                return carry

            lax.fori_loop(k + 1, i + 1, update, 0)
            return carry

        lax.fori_loop(k + 1, 4, l_col, 0)
        return carry

    lax.fori_loop(0, 4, step, 0)


def inverse_of(block, rows):
    return pl.pallas_call(
        lambda *refs: factor_kernel(rows, *refs),
        out_shape=jax.ShapeDtypeStruct((N, N), F32),
        in_specs=[VMEM],
        out_specs=VMEM,
        scratch_shapes=[pltpu.VMEM((N, N), F32)] * 2,
        compiler_params=PARAMS,
        cost_estimate=pl.CostEstimate(flops=30_000_000_000, bytes_accessed=2**21, transcendentals=0),
    )(block)


def split(x):
    hi = x.astype(jnp.bfloat16)
    return hi, (x - hi.astype(F32)).astype(jnp.bfloat16)


def dot_split(a, b, dims=NT):
    def dot(u, v):
        return lax.dot_general(u, v, (dims, ((), ())), preferred_element_type=F32)

    return dot(a[0], b[0]) + (dot(a[0], b[1]) + dot(a[1], b[0]))


def child_kernel(ids, cmap, a_ref, x_ref, top_ref, panel_ref, keep_ref, send_ref):
    front, tile = ids[0], ids[1]
    parity = lax.rem(front, 2)
    x = split(x_ref[...])
    tops = [split(dot_split(split(top_ref[:, h].reshape(N, N)), x)) for h in range(2)]
    keep_ref[...] = jnp.zeros_like(keep_ref)
    send_ref[...] = jnp.zeros_like(send_ref)
    panel_ref[...] = dot_split(split(a_ref[0, :, :N]), x)
    for i in range(4):
        rows = slice(i * B, (i + 1) * B)
        panel = split(panel_ref[rows, :])
        place = cmap[front, jnp.maximum(4 * tile - 4 + i, 0)] - 4 * (tile - 1)
        first = a_ref[0, rows, N : 2 * N] - dot_split(panel, tops[0])
        second = a_ref[0, rows, 2 * N :] - dot_split(panel, tops[1])

        @pl.when(tile > 0)
        def _():
            keep_ref[at(place), :] = jnp.where(parity == 1, first, second)
            send_ref[at(place), :] = jnp.where(parity == 1, second, first)


def child_step(ids, cmap, front_vals, x, tops):
    return pl.pallas_call(
        child_kernel,
        out_shape=[jax.ShapeDtypeStruct((N, N), F32)] + [jax.ShapeDtypeStruct((2 * N, N), F32)] * 2,
        in_specs=[SMEM, SMEM, VMEM, VMEM, VMEM],
        out_specs=[VMEM] * 3,
        compiler_params=PARAMS,
        cost_estimate=pl.CostEstimate(flops=5_000_000_000, bytes_accessed=2**23, transcendentals=0),
    )(ids, cmap, front_vals, x, tops)


def parent_kernel(ids, own_ref, other_ref, x_ref, mine_ref, theirs_ref, out_ref):
    x = split(x_ref[...])
    parity = lax.rem(ids[0], 2)

    @pl.when(parity == 1)
    def _():
        out_ref[...] = dot_split(split(own_ref[...]), x)

    @pl.when(parity == 0)
    def _():
        top = jnp.concatenate([theirs_ref[...], mine_ref[:, 32:, :]], axis=1).reshape(N, N)
        top = split(dot_split(split(top), x))
        panel = split(dot_split(split(other_ref[...]), x))
        out_ref[...] = own_ref[...] - dot_split(panel, top)


def parent_step(ids, own, other, x, mine, theirs):
    return pl.pallas_call(
        parent_kernel,
        out_shape=jax.ShapeDtypeStruct((N, N), F32),
        in_specs=[SMEM] + [VMEM] * 5,
        out_specs=VMEM,
        compiler_params=PARAMS,
        cost_estimate=pl.CostEstimate(flops=5_000_000_000, bytes_accessed=2**23, transcendentals=0),
    )(ids, own, other, x, mine, theirs)


def scattered(x):
    return lax.all_to_all(x.reshape(16, 32, N), "tile", 0, 0)


def gathered(piece):
    return lax.all_to_all(jnp.broadcast_to(piece[None], (16,) + piece.shape), "tile", 0, 0)


def sibling(x):
    return lax.ppermute(x, "front", [(i, i ^ 1) for i in range(16)])


def local(child_front, parent_front, child_map):
    tile = lax.axis_index("tile")
    front = lax.axis_index("front")
    odd = front % 2 == 1
    ids = jnp.stack([front, tile]).astype(jnp.int32)
    parent_vals = parent_front[0]
    pivots_ahead = lax.ppermute(parent_vals, "tile", [(0, 1)])

    pieces = scattered(child_front[0, :, :N])
    tops = lax.all_gather(pieces[1:3], "tile")
    child_x = inverse_of(gathered(pieces[0]), 32)
    child_panel, keep, send = child_step(ids, child_map, child_front, child_x, tops)

    placed = keep + sibling(send)
    lower = placed[:N]
    upper = placed[N:] + parent_vals
    arrived = lax.ppermute(lower, "tile", [(i, i - 1) for i in range(1, 16)])
    outgoing = jnp.where(odd, lower + pivots_ahead, sibling(upper))
    parts = scattered(outgoing)
    mine = parts[1:3]
    theirs = sibling(mine)
    pivot_piece = jnp.where(odd, mine[0], theirs[0])
    top_piece = jnp.where(odd, mine[1] + theirs[0], theirs[1] + mine[0])
    top_half = jnp.where(odd, top_piece[:16], top_piece[16:])
    whole = gathered(jnp.concatenate([pivot_piece, top_half], axis=0))
    top_theirs = sibling(whole[:, 32:, :])
    assembled = upper + arrived
    other = sibling(assembled)
    parent_x = inverse_of(whole, 32)
    result = parent_step(ids, assembled, other, parent_x, whole, top_theirs)
    return (child_panel[None], result[None])


def solution(mesh):
    return jax.shard_map(
        local,
        mesh=mesh,
        in_specs=(P("front", "tile", None), P("front", "tile", None), P()),
        out_specs=(P("front", "tile", None), P("front", "tile", None)),
        check_vma=False,
    )
```

time: 1150 us -> 230 us (0.20)
  waiting for transfers between devices: 751 us -> 75.7 us
  other arithmetic: 260 us -> 5.05 us
  Pallas kernels: 0 us -> 67.9 us
  local copies, waits for them, and re-layouts: 68.7 us -> 4.44 us
  blocking collectives: 0 us -> 47.3 us
  matrix products: 38 us -> 0 us
    psum x7 -> x0, waiting for transfers between devices: 698 us -> none  [from_root(): return lax.psum(kept, axis)]
    another operation x36 -> x1, other arithmetic: 244 us -> 0.08 us  [local(): ids = jnp.stack([front, tile]).astype(jnp.int32)]
    pallas_call x0 -> x4, Pallas kernels: none -> 67.9 us  [the longest x2 52 us: inverse_of(): pl.pallas_call(lambda *refs: factor_kernel(rows, *refs), out_shape=jax.Sh...]
    all_to_all x0 -> x2, blocking collectives: none -> 47.3 us  [scattered(): return lax.all_to_all(x.reshape(16, 32, N), 'tile', 0, 0)]
    all_to_all x0 -> x2, waiting for transfers between devices: none -> 41.2 us  [gathered(): lax.all_to_all(jnp.broadcast_to(piece[None], (16,) + piece.shape), 'tile'...]
    another operation x26 -> x0, matrix products: 26.9 us -> none  [the longest x14 13.6 us: panel_solve(): lax.linalg.triangular_solve(factor, columns, left_side=False, lower=True,...]
    ppermute x3 -> x7, waiting for transfers between devices: 53.3 us -> 28.7 us  [the longest x1 20.3 us: local(): arrived = lax.ppermute(lower, 'tile', [(i, i - 1) for i in range(1, 16)])]
    another operation x35 -> x0, local copies, waits for them, and re-layouts: 20.8 us -> none  [the longest x27 19.5 us: panel_solve(): lax.linalg.triangular_solve(factor, columns, left_side=False, lower=True,...]
  transfers between devices with their start and end apart: 10 -> 10, of which waited for: 10 -> 7; matrix products, arithmetic and copies ran while one was open for 1% -> 2% of each run, Pallas kernels for 0% -> 23%
where the time goes in v1:
time: 230 us
  waiting for transfers between devices  75.7 us (33%)
  Pallas kernels  67.9 us (30%)
  blocking collectives  47.3 us (21%)
  starting transfers between devices  15 us (7%)
  between operations  14.2 us (6%)
  other arithmetic  5.05 us (2%)
  local copies, waits for them, and re-layouts  4.44 us (2%)
    pallas_call x2, Pallas kernels, inverse_of(): pl.pallas_call(lambda *refs: factor_kernel(rows, *refs), out_shape=jax.Sh...  52 us
    all_to_all x2, blocking collectives, scattered(): return lax.all_to_all(x.reshape(16, 32, N), 'tile', 0, 0)  47.3 us
    all_to_all x2, waiting for transfers between devices, gathered(): lax.all_to_all(jnp.broadcast_to(piece[None], (16,) + piece.shape), 'tile'...  41.2 us
    ppermute x1, waiting for transfers between devices, local(): arrived = lax.ppermute(lower, 'tile', [(i, i - 1) for i in range(1, 16)])  20.3 us
    pallas_call x1, Pallas kernels, child_step(): pl.pallas_call(child_kernel, out_shape=[jax.ShapeDtypeStruct((N, N), F32)...  10.8 us
    ppermute x5, waiting for transfers between devices, sibling(): return lax.ppermute(x, 'front', [(i, i ^ 1) for i in range(16)])  8.49 us
    all_to_all x2, starting transfers between devices, gathered(): lax.all_to_all(jnp.broadcast_to(piece[None], (16,) + piece.shape), 'tile'...  7.69 us
    all_gather x1, waiting for transfers between devices, local(): tops = lax.all_gather(pieces[1:3], 'tile')  5.75 us
  transfers between devices with their start and end apart: 10, of which 7 were waited for; matrix products, arithmetic and copies ran while one was open for 2% of the time, Pallas kernels for 23%

profile of v1, /device:TPU:32, one launch (start us, length us, event | category | flops | bytes accessed | tf_op | source)
XLA Modules:
  0.0 229.6 jit_solution(6934537694562630803)
XLA Ops:
  7.2 0.0 slice-start
  7.2 0.0 all-gather.3.cloned.1.call-start
  7.2 1.2 slice-done
  8.4 23.7 %all_to_all.20 = f32[16,32,512]{2,1,0:T(8,128)S(1)} all-to-all(f32[16,32,512]{2,1,0:T(8,128)S(1)} %bitcast.17), channel_id=1, replica_groups=mesh['front'=16,'tile'=16] {'tile'}, dimensions={0} | all-to-all | bytes 2097152 | tf_op jit(solution)/shard_map/all_to_all | solution.py:199
  32.1 0.7 slice.59
  32.7 0.0 all-gather.3.cloned.1.call-update
  32.8 1.1 broadcast_in_dim.20
  33.9 3.8 %all-to-all-start.1 = ((f32[16,32,512]{2,1,0:T(8,128)}), f32[16,32,512]{2,1,0:T(8,128)S(1)}, u32[]{:S(2)}, u32[]{:S(2)}) async-start(f32[16,32,512]{2,1,0:T(8,128)} %broadcast_in_dim.20), calls=%async_computation.1 | async-start | bytes 2097152 | tf_op jit(solution)/shard_map/all_to_all | solution.py:203
  37.7 0.1 pad_add_fusion.ids
  37.8 0.0 copy-start
  37.8 16.8 %all-to-all-done.1.refs_0_ = f32[16,32,512]{2,1,0:T(8,128)S(1)} async-done(((f32[16,32,512]{2,1,0:T(8,128)}), f32[16,32,512]{2,1,0:T(8,128)S(1)}, u32[]{:S(2)}, u32[]{:S(2)}) %all-to-all-start.1) | async-done | bytes 1048608 | tf_op jit(solution)/shard_map/all_to_all | solution.py:203
  54.6 26.0 %shard_map.50.x_ref = f32[512,512]{1,0:T(8,128)S(1)} custom-call(f32[16,32,512]{2,1,0:T(8,128)S(1)} %all-to-all-done.1.refs_0_), custom_call_target="tpu_custom_call" | custom-call | flops 30000001024 | bytes 2097152 | tf_op jit(solution)/shard_map/pallas_call | solution.py:116
  80.6 5.7 %all-gather.3.cloned.1.call-done = f32[32,32,512]{2,1,0:T(8,128)} async-done(((f32[2,32,512]{2,1,0:T(8,128)}), f32[32,32,512]{2,1,0:T(8,128)}) %all-gather.3.cloned.1.call-update) | async-done | bytes 2097168 | tf_op jit(solution)/shard_map/all_gather | solution.py:219
  86.3 0.0 copy-done
  86.3 10.8 %shard_map.51 = (f32[512,512]{1,0:T(8,128)}, f32[1024,512]{1,0:T(8,128)S(1)}, f32[1024,512]{1,0:T(8,128)S(1)}) custom-call(s32[2]{0:T(128)S(1)} %pad_add_fusion.ids, s32[16,60]{1,0:T(8,128)S(1)} %copy-done, f32[1,512,1536]{2,1,0:T(8,128)} %a_ref.1, f32[512,512]{1,0:T(8,128)S(1)} %shard_map.50.x_ref, f32[16,2,32,512]{3,2,1,0:T(8,128)} %bitcast.18), custom_call_target="tpu_custom_call" | custom-call | flops 5000000000 | bytes 8388608 | tf_op jit(solution)/shard_map/pallas_call | solution.py:161
  97.1 0.0 collective-permute-start
  97.1 4.2 %collective-permute-done = f32[1024,512]{1,0:T(8,128)S(1)} collective-permute-done((f32[1024,512]{1,0:T(8,128)S(1)}, f32[1024,512]{1,0:T(8,128)S(1)}, u32[]{:S(2)}, u32[]{:S(2)}) %collective-permute-start) | collective-permute-done | bytes 2097184 | tf_op jit(solution)/shard_map/ppermute | solution.py:207
  101.3 0.5 add.24
  101.8 0.1 slice.61
  101.8 1.3 collective-permute-start.1
  103.1 5.5 %collective-permute-start.3 = (f32[512,512]{1,0:T(8,128)}, f32[512,512]{1,0:T(8,128)}, u32[]{:S(2)}, u32[]{:S(2)}) collective-permute-start(f32[512,512]{1,0:T(8,128)} %bitcast.6), channel_id=1, source_target_pairs={{0,1},{16,17},{32,33},{48,49},{64,65},{80,81},{96,97},{112,113},{1... | collective-permute-start | bytes 3145736 | tf_op jit(solution)/shard_map/ppermute | solution.py:216
  108.7 20.3 %collective-permute-done.1 = f32[512,512]{1,0:T(8,128)S(1)} collective-permute-done((f32[512,512]{1,0:T(8,128)S(1)}, f32[512,512]{1,0:T(8,128)S(1)}, u32[]{:S(2)}, u32[]{:S(2)}) %collective-permute-start.1) | collective-permute-done | bytes 1048608 | tf_op jit(solution)/shard_map/ppermute | solution.py:226
  128.9 2.6 %fusion.2 = (f32[512,512]{1,0:T(8,128)S(1)}, f32[512,512]{1,0:T(8,128)}) fusion(f32[512,512]{1,0:T(8,128)S(1)} %collective-permute-done.1, f32[1,512,512]{2,1,0:T(8,128)} %param.4, f32[1024,512]{1,0:T(8,128)S(1)} %add.24), kind=kLoop, calls=%fused_computation.11 | loop fusion | flops 524288 | bytes 5242880 | tf_op jit(solution)/shard_map/add | solution.py:236
  131.5 0.0 collective-permute-start.4
  131.5 0.0 collective-permute-done.3
  131.5 3.0 %collective-permute-done.4 = f32[512,512]{1,0:T(8,128)} collective-permute-done((f32[512,512]{1,0:T(8,128)}, f32[512,512]{1,0:T(8,128)}, u32[]{:S(2)}, u32[]{:S(2)}) %collective-permute-start.4) | collective-permute-done | bytes 1048608 | tf_op jit(solution)/shard_map/ppermute | solution.py:207
  134.5 1.9 add_select_fusion
  136.4 23.7 %all_to_all.21 = f32[16,32,512]{2,1,0:T(8,128)S(1)} all-to-all(f32[16,32,512]{2,1,0:T(8,128)S(1)} %bitcast.16), channel_id=1, replica_groups=mesh['front'=16,'tile'=16] {'tile'}, dimensions={0} | all-to-all | bytes 2097152 | tf_op jit(solution)/shard_map/all_to_all | solution.py:199
  160.1 0.3 collective-permute-start.5
  160.3 1.3 collective-permute-done.5
  161.7 1.4 broadcast_in_dim.22
  163.1 3.8 %all-to-all-start.3 = ((f32[16,48,512]{2,1,0:T(8,128)}), f32[16,48,512]{2,1,0:T(8,128)S(1)}, u32[]{:S(2)}, u32[]{:S(2)}) async-start(f32[16,48,512]{2,1,0:T(8,128)} %broadcast_in_dim.22), calls=%async_computation.3 | async-start | bytes 3145728 | tf_op jit(solution)/shard_map/all_to_all | solution.py:203
  167.0 0.1 collective-permute-start.2
  167.1 24.4 %all-to-all-done.3.refs_0_.mine_ref = f32[16,48,512]{2,1,0:T(8,128)S(1)} async-done(((f32[16,48,512]{2,1,0:T(8,128)}), f32[16,48,512]{2,1,0:T(8,128)S(1)}, u32[]{:S(2)}, u32[]{:S(2)}) %all-to-all-start.3) | async-done | bytes 1572896 | tf_op jit(solution)/shard_map/all_to_all | solution.py:203
  191.5 0.1 collective-permute-start.6
  191.6 26.0 %shard_map.52.x_ref = f32[512,512]{1,0:T(8,128)S(1)} custom-call(f32[16,48,512]{2,1,0:T(8,128)S(1)} %all-to-all-done.3.refs_0_.mine_ref), custom_call_target="tpu_custom_call" | custom-call | flops 30000001024 | bytes 2097152 | tf_op jit(solution)/shard_map/pallas_call | solution.py:116
  217.6 0.0 collective-permute-done.2.other_ref
  217.6 0.0 collective-permute-done.6.theirs_ref
  217.6 5.1 %shard_map.53 = f32[512,512]{1,0:T(8,128)} custom-call(s32[2]{0:T(128)S(1)} %pad_add_fusion.ids, f32[512,512]{1,0:T(8,128)S(1)} %get-tuple-element.8.own_ref, f32[512,512]{1,0:T(8,128)} %collective-permute-done.2.other_ref, f32[512,512]{1,0:T(8,128)S(1)} %shard_map.52.x_ref, f32[16,48,512]{2,1,0:T(8,128)S(1)} %all-to-all-done.3.refs_0_.mine_ref, ...), custom_call_target="tpu_custom_call" | custom-call | flops 5000000000 | bytes 8388608 | tf_op jit(solution)/shard_map/pallas_call | solution.py:188
  (6 shorter events, 0.1 us)
Async XLA Ops:
  7.2 1.2 slice-start
  7.2 79.2 %all-gather.3.cloned.1.call-start = ((), (), s32[]{:S(2)}) async-start(), calls=%async_computation.4 | async-start | bytes 2228224 | tf_op jit(solution)/shard_map/all_gather | solution.py:219
  33.9 20.7 %all-to-all-start.1 = ((f32[16,32,512]{2,1,0:T(8,128)}), f32[16,32,512]{2,1,0:T(8,128)S(1)}, u32[]{:S(2)}, u32[]{:S(2)}) async-start(f32[16,32,512]{2,1,0:T(8,128)} %broadcast_in_dim.20), calls=%async_computation.1 | async-start | bytes 2097152 | tf_op jit(solution)/shard_map/all_to_all | solution.py:203
  37.8 48.5 %copy-start = (s32[16,60]{1,0:T(8,128)S(1)}, s32[16,60]{1,0:T(8,128)}, u32[]{:S(2)}) copy-start(s32[16,60]{1,0:T(8,128)} %cmap.1) | copy-start | bytes 11524
  97.1 4.2 %collective-permute-start = (f32[1024,512]{1,0:T(8,128)S(1)}, f32[1024,512]{1,0:T(8,128)S(1)}, u32[]{:S(2)}, u32[]{:S(2)}) collective-permute-start(f32[1024,512]{1,0:T(8,128)S(1)} %get-tuple-element.7), channel_id=1, source_target_pairs={{0,16},{16,0},{32,48},{48,32},{64,80},{80,64},{96,112},{112,96},{1... | collective-permute-start | bytes 6291464 | tf_op jit(solution)/shard_map/ppermute | solution.py:207
  101.8 27.1 %collective-permute-start.1 = (f32[512,512]{1,0:T(8,128)S(1)}, f32[512,512]{1,0:T(8,128)S(1)}, u32[]{:S(2)}, u32[]{:S(2)}) collective-permute-start(f32[512,512]{1,0:T(8,128)S(1)} %slice.61), channel_id=1, source_target_pairs={{1,0},{2,1},{3,2},{4,3},{5,4},{6,5},{7,6},{8,7},{9,8},{10,9},{11,1... | collective-permute-start | bytes 3145736 | tf_op jit(solution)/shard_map/ppermute | solution.py:226
  103.1 28.4 %collective-permute-start.3 = (f32[512,512]{1,0:T(8,128)}, f32[512,512]{1,0:T(8,128)}, u32[]{:S(2)}, u32[]{:S(2)}) collective-permute-start(f32[512,512]{1,0:T(8,128)} %bitcast.6), channel_id=1, source_target_pairs={{0,1},{16,17},{32,33},{48,49},{64,65},{80,81},{96,97},{112,113},{1... | collective-permute-start | bytes 3145736 | tf_op jit(solution)/shard_map/ppermute | solution.py:216
  131.5 3.0 %collective-permute-start.4 = (f32[512,512]{1,0:T(8,128)}, f32[512,512]{1,0:T(8,128)}, u32[]{:S(2)}, u32[]{:S(2)}) collective-permute-start(f32[512,512]{1,0:T(8,128)} %get-tuple-element.9), channel_id=1, source_target_pairs={{0,16},{16,0},{32,48},{48,32},{64,80},{80,64},{96,112},{112,96},{1... | collective-permute-start | bytes 3145736 | tf_op jit(solution)/shard_map/ppermute | solution.py:207
  160.1 1.6 collective-permute-start.5
  163.1 28.3 %all-to-all-start.3 = ((f32[16,48,512]{2,1,0:T(8,128)}), f32[16,48,512]{2,1,0:T(8,128)S(1)}, u32[]{:S(2)}, u32[]{:S(2)}) async-start(f32[16,48,512]{2,1,0:T(8,128)} %broadcast_in_dim.22), calls=%async_computation.3 | async-start | bytes 3145728 | tf_op jit(solution)/shard_map/all_to_all | solution.py:203
  167.0 50.6 %collective-permute-start.2 = (f32[512,512]{1,0:T(8,128)S(1)}, f32[512,512]{1,0:T(8,128)}, u32[]{:S(2)}, u32[]{:S(2)}) collective-permute-start(f32[512,512]{1,0:T(8,128)S(1)} %get-tuple-element.8.own_ref), channel_id=1, source_target_pairs={{0,16},{16,0},{32,48},{48,32},{64,80},{80,64},{96,112},{112,96},{1... | collective-permute-start | bytes 3145736 | tf_op jit(solution)/shard_map/ppermute | solution.py:207
  191.5 26.1 %collective-permute-start.6 = (f32[16,16,512]{2,1,0:T(8,128)S(1)}, f32[16,16,512]{2,1,0:T(8,128)S(1)}, u32[]{:S(2)}, u32[]{:S(2)}) collective-permute-start(f32[16,16,512]{2,1,0:T(8,128)S(1)} %slice.69), channel_id=1, source_target_pairs={{0,16},{16,0},{32,48},{48,32},{64,80},{80,64},{96,112},{112,96},{1... | collective-permute-start | bytes 1572872 | tf_op jit(solution)/shard_map/ppermute | solution.py:207
Sparse Core Ops, SparseCore 0:
  32.9 53.4 all-gather.2

commit v2 on v1

--- a/solution.py
+++ b/solution.py
@@ -71,16 +71,10 @@
     return pl.ds(pl.multiple_of(i * B, B), B)
 
 
-def factor_kernel(rows, a_ref, x_ref, s_ref, l_ref):
-    l_ref[...] = a_ref[:, :rows, :].reshape(N, N)
-    for i in range(4):
-        for j in range(i + 1):
-            s_ref[i * B : (i + 1) * B, j * B : (j + 1) * B] = 0.5 * (
-                l_ref[i * B : (i + 1) * B, j * B : (j + 1) * B]
-                + l_ref[j * B : (j + 1) * B, i * B : (i + 1) * B].T
-            )
-    x_ref[...] = jnp.zeros_like(x_ref)
-
+LOWER = [(i, j) for i in range(4) for j in range(i + 1)]
+
+
+def eliminate(steps, s_ref, l_ref, x_ref):
     def step(k, carry):
         k0 = pl.multiple_of(k * B, B)
         xk = inverse_factor(lambda q: s_ref[pl.ds(pl.multiple_of(k0 + 8 * q, 8), 8), at(k)])
@@ -109,19 +103,74 @@
         lax.fori_loop(k + 1, 4, l_col, 0)
         return carry
 
-    lax.fori_loop(0, 4, step, 0)
-
-
-def inverse_of(block, rows):
-    return pl.pallas_call(
-        lambda *refs: factor_kernel(rows, *refs),
-        out_shape=jax.ShapeDtypeStruct((N, N), F32),
+    lax.fori_loop(steps[0], steps[1], step, 0)
+
+
+def unpack(packed, s_ref):
+    for b, (i, j) in enumerate(LOWER):
+        s_ref[i * B : (i + 1) * B, j * B : (j + 1) * B] = packed[b * B : (b + 1) * B, :]
+
+
+def whole_kernel(a_ref, x_ref, s_ref, l_ref):
+    unpack(a_ref[...].reshape(1280, B), s_ref)
+    x_ref[...] = jnp.zeros_like(x_ref)
+    eliminate((0, 4), s_ref, l_ref, x_ref)
+
+
+def first_kernel(ids, mine_ref, theirs_ref, x_ref, s_ref, l_ref, p_ref):
+    parity = lax.rem(ids[0], 2)
+    p_ref[pl.ds(pl.multiple_of((1 - parity) * 640, 640), 640), :] = mine_ref[:, :40, :].reshape(640, B)
+    p_ref[pl.ds(pl.multiple_of(parity * 640, 640), 640), :] = theirs_ref[...].reshape(640, B)
+    unpack(p_ref, s_ref)
+    x_ref[...] = jnp.zeros_like(x_ref)
+    eliminate((0, 3), s_ref, l_ref, x_ref)
+
+
+def last_kernel(xin_ref, s_ref, l_ref, x_ref):
+    x_ref[...] = xin_ref[...]
+    eliminate((3, 4), s_ref, l_ref, x_ref)
+
+
+SQUARE = jax.ShapeDtypeStruct((N, N), F32)
+
+
+def cost(gflop):
+    return pl.CostEstimate(flops=int(gflop * 1e9), bytes_accessed=2**21, transcendentals=0)
+
+
+def inverse_whole(packed):
+    return pl.pallas_call(
+        whole_kernel,
+        out_shape=SQUARE,
         in_specs=[VMEM],
         out_specs=VMEM,
         scratch_shapes=[pltpu.VMEM((N, N), F32)] * 2,
         compiler_params=PARAMS,
-        cost_estimate=pl.CostEstimate(flops=30_000_000_000, bytes_accessed=2**21, transcendentals=0),
-    )(block)
+        cost_estimate=cost(25),
+    )(packed)
+
+
+def inverse_first(ids, mine, theirs):
+    return pl.pallas_call(
+        first_kernel,
+        out_shape=[SQUARE] * 3,
+        in_specs=[SMEM, VMEM, VMEM],
+        out_specs=[VMEM] * 3,
+        scratch_shapes=[pltpu.VMEM((1280, B), F32)],
+        compiler_params=PARAMS,
+        cost_estimate=cost(20),
+    )(ids, mine, theirs)
+
+
+def inverse_last(x, s, l):
+    return pl.pallas_call(
+        last_kernel,
+        out_shape=SQUARE,
+        in_specs=[VMEM] * 3,
+        out_specs=VMEM,
+        compiler_params=PARAMS,
+        cost_estimate=cost(6),
+    )(x, s, l)
 
 
 def split(x):
@@ -136,18 +185,104 @@
     return dot(a[0], b[0]) + (dot(a[0], b[1]) + dot(a[1], b[0]))
 
 
-def child_kernel(ids, cmap, a_ref, x_ref, top_ref, panel_ref, keep_ref, send_ref):
+def symmetric(ref, i, j):
+    return 0.5 * (
+        ref[i * B : (i + 1) * B, j * B : (j + 1) * B]
+        + ref[j * B : (j + 1) * B, i * B : (i + 1) * B].T
+    )
+
+
+def spread_kernel(ids, a_ref, out_ref, p_ref):
+    @pl.when(ids[1] > 0)
+    def _():
+        for c in range(4):
+            out_ref[:, 32 * c : 32 * c + 32, :] = a_ref[0, :, c * B : (c + 1) * B].reshape(16, 32, B)
+
+    @pl.when(ids[1] == 0)
+    def _():
+        for b, (i, j) in enumerate(LOWER):
+            p_ref[b * B : (b + 1) * B, :] = symmetric(a_ref.at[0], i, j)
+        out_ref[:, :80, :] = p_ref[...].reshape(16, 80, B)
+        out_ref[:, 80:, :] = jnp.zeros((16, 48, B), F32)
+
+
+def spread(ids, front_vals):
+    return pl.pallas_call(
+        spread_kernel,
+        grid=(1,),
+        out_shape=jax.ShapeDtypeStruct((16, B, B), F32),
+        in_specs=[SMEM, pl.BlockSpec((1, N, N), lambda i: (0, 0, 0))],
+        out_specs=pl.BlockSpec((16, B, B), lambda i: (0, 0, 0)),
+        scratch_shapes=[pltpu.VMEM((1280, B), F32)],
+        compiler_params=PARAMS,
+    )(ids, front_vals)
+
+
+def place_of(cmap, front, tile, i):
+    return cmap[front, jnp.maximum(4 * tile - 4 + i, 0)] - 4 * (tile - 1)
+
+
+def corner_kernel(
+    ids, cmap, a_ref, ahead_ref, x_ref, pp_ref, pf_ref, panel_ref, keep_ref, send_ref, b_ref, p_ref
+):
     front, tile = ids[0], ids[1]
     parity = lax.rem(front, 2)
     x = split(x_ref[...])
-    tops = [split(dot_split(split(top_ref[:, h].reshape(N, N)), x)) for h in range(2)]
+    panel_ref[...] = dot_split(split(a_ref[0, :, :N]), x)
+    top = split(dot_split(split(jnp.where(tile == 1, a_ref[0, :, :N], ahead_ref[...])), x))
+    b_ref[...] = jnp.zeros_like(b_ref)
+    for i in range(4):
+        rows = slice(i * B, (i + 1) * B)
+        first = a_ref[0, rows, N:] - dot_split(split(panel_ref[rows, :]), top)
+
+        @pl.when(tile > 0)
+        def _():
+            b_ref[at(place_of(cmap, front, tile, i)), :] = first
+
+    @pl.when((tile == 1) & (parity == 1))
+    def _():
+        b_ref[:N, :] += pp_ref[...]
+        b_ref[N:, :] += pf_ref[...]
+
+    for b, (i, j) in enumerate(LOWER):
+        p_ref[b * B : (b + 1) * B, :] = symmetric(b_ref, i, j)
+    base = jnp.where(tile == 1, N, 0)
+    for ref, half in ((keep_ref, 1 - parity), (send_ref, parity)):
+        ref[:, :40, :] = p_ref[pl.ds(pl.multiple_of(half * 640, 640), 640), :].reshape(16, 40, B)
+        rows = pl.ds(pl.multiple_of(base + half * 256, 256), 256)
+        for c in range(4):
+            ref[:, 40 + 16 * c : 56 + 16 * c, :] = b_ref[rows, c * B : (c + 1) * B].reshape(16, 16, B)
+
+
+def corner(ids, cmap, front_vals, ahead, x, pp, pf):
+    full = pl.BlockSpec((N, N), lambda i: (0, 0))
+    piece = pl.BlockSpec((16, 104, B), lambda i: (0, 0, 0))
+    return pl.pallas_call(
+        corner_kernel,
+        grid=(1,),
+        out_shape=[SQUARE] + [jax.ShapeDtypeStruct((16, 104, B), F32)] * 2,
+        in_specs=[SMEM, SMEM, pl.BlockSpec((1, N, 2 * N), lambda i: (0, 0, 0)), full, full, full, full],
+        out_specs=[full, piece, piece],
+        scratch_shapes=[pltpu.VMEM((2 * N, N), F32), pltpu.VMEM((1280, B), F32)],
+        compiler_params=PARAMS,
+        cost_estimate=cost(3),
+    )(ids, cmap, front_vals, ahead, x, pp, pf)
+
+
+def schur_kernel(ids, cmap, a_ref, panel_ref, x_ref, top_ref, keep_ref, send_ref):
+    front, tile = ids[0], ids[1]
+    parity = lax.rem(front, 2)
+    x = split(x_ref[...])
+    tops = []
+    for h in range(2):
+        raw = [top_ref[:, h, 32 * c : 32 * c + 32, :].reshape(N, B) for c in range(4)]
+        tops.append(split(dot_split(split(jnp.concatenate(raw, axis=1)), x)))
     keep_ref[...] = jnp.zeros_like(keep_ref)
     send_ref[...] = jnp.zeros_like(send_ref)
-    panel_ref[...] = dot_split(split(a_ref[0, :, :N]), x)
     for i in range(4):
         rows = slice(i * B, (i + 1) * B)
         panel = split(panel_ref[rows, :])
-        place = cmap[front, jnp.maximum(4 * tile - 4 + i, 0)] - 4 * (tile - 1)
+        place = place_of(cmap, front, tile, i)
         first = a_ref[0, rows, N : 2 * N] - dot_split(panel, tops[0])
         second = a_ref[0, rows, 2 * N :] - dot_split(panel, tops[1])
 
@@ -157,15 +292,15 @@
             send_ref[at(place), :] = jnp.where(parity == 1, second, first)
 
 
-def child_step(ids, cmap, front_vals, x, tops):
-    return pl.pallas_call(
-        child_kernel,
-        out_shape=[jax.ShapeDtypeStruct((N, N), F32)] + [jax.ShapeDtypeStruct((2 * N, N), F32)] * 2,
-        in_specs=[SMEM, SMEM, VMEM, VMEM, VMEM],
-        out_specs=[VMEM] * 3,
-        compiler_params=PARAMS,
-        cost_estimate=pl.CostEstimate(flops=5_000_000_000, bytes_accessed=2**23, transcendentals=0),
-    )(ids, cmap, front_vals, x, tops)
+def schur(ids, cmap, front_vals, panel, x, tops):
+    return pl.pallas_call(
+        schur_kernel,
+        out_shape=[jax.ShapeDtypeStruct((2 * N, N), F32)] * 2,
+        in_specs=[SMEM, SMEM, VMEM, VMEM, VMEM, VMEM],
+        out_specs=[VMEM] * 2,
+        compiler_params=PARAMS,
+        cost_estimate=cost(8),
+    )(ids, cmap, front_vals, panel, x, tops)
 
 
 def parent_kernel(ids, own_ref, other_ref, x_ref, mine_ref, theirs_ref, out_ref):
@@ -178,8 +313,17 @@
 
     @pl.when(parity == 0)
     def _():
-        top = jnp.concatenate([theirs_ref[...], mine_ref[:, 32:, :]], axis=1).reshape(N, N)
-        top = split(dot_split(split(top), x))
+        top = [
+            jnp.concatenate(
+                [
+                    theirs_ref[:, 16 * c : 16 * c + 16, :].reshape(256, B),
+                    mine_ref[:, 40 + 16 * c : 56 + 16 * c, :].reshape(256, B),
+                ],
+                axis=0,
+            )
+            for c in range(4)
+        ]
+        top = split(dot_split(split(jnp.concatenate(top, axis=1)), x))
         panel = split(dot_split(split(other_ref[...]), x))
         out_ref[...] = own_ref[...] - dot_split(panel, top)
 
@@ -187,20 +331,20 @@
 def parent_step(ids, own, other, x, mine, theirs):
     return pl.pallas_call(
         parent_kernel,
-        out_shape=jax.ShapeDtypeStruct((N, N), F32),
+        out_shape=SQUARE,
         in_specs=[SMEM] + [VMEM] * 5,
         out_specs=VMEM,
         compiler_params=PARAMS,
-        cost_estimate=pl.CostEstimate(flops=5_000_000_000, bytes_accessed=2**23, transcendentals=0),
+        cost_estimate=cost(4),
     )(ids, own, other, x, mine, theirs)
 
 
-def scattered(x):
-    return lax.all_to_all(x.reshape(16, 32, N), "tile", 0, 0)
+def exchanged(x):
+    return lax.all_to_all(x, "tile", 0, 0)
 
 
 def gathered(piece):
-    return lax.all_to_all(jnp.broadcast_to(piece[None], (16,) + piece.shape), "tile", 0, 0)
+    return exchanged(jnp.broadcast_to(piece[None], (16,) + piece.shape))
 
 
 def sibling(x):
@@ -210,33 +354,35 @@
 def local(child_front, parent_front, child_map):
     tile = lax.axis_index("tile")
     front = lax.axis_index("front")
-    odd = front % 2 == 1
     ids = jnp.stack([front, tile]).astype(jnp.int32)
     parent_vals = parent_front[0]
-    pivots_ahead = lax.ppermute(parent_vals, "tile", [(0, 1)])
-
-    pieces = scattered(child_front[0, :, :N])
+
+    pieces = exchanged(spread(ids, child_front))
     tops = lax.all_gather(pieces[1:3], "tile")
-    child_x = inverse_of(gathered(pieces[0]), 32)
-    child_panel, keep, send = child_step(ids, child_map, child_front, child_x, tops)
-
-    placed = keep + sibling(send)
-    lower = placed[:N]
-    upper = placed[N:] + parent_vals
-    arrived = lax.ppermute(lower, "tile", [(i, i - 1) for i in range(1, 16)])
-    outgoing = jnp.where(odd, lower + pivots_ahead, sibling(upper))
-    parts = scattered(outgoing)
-    mine = parts[1:3]
-    theirs = sibling(mine)
-    pivot_piece = jnp.where(odd, mine[0], theirs[0])
-    top_piece = jnp.where(odd, mine[1] + theirs[0], theirs[1] + mine[0])
-    top_half = jnp.where(odd, top_piece[:16], top_piece[16:])
-    whole = gathered(jnp.concatenate([pivot_piece, top_half], axis=0))
-    top_theirs = sibling(whole[:, 32:, :])
-    assembled = upper + arrived
+    pivot = gathered(pieces[0, :80])
+    columns, parents, pivot = lax.optimization_barrier((child_front[0, :, :N], parent_vals, pivot))
+    ahead = lax.ppermute(columns, "tile", [(1, 2)])
+    pivots_ahead = lax.ppermute(
+        parents, ("front", "tile"), [(f * 16, f * 16 + 1) for f in range(1, 16, 2)]
+    )
+    child_x = inverse_whole(pivot)
+    child_panel, keep, send = corner(
+        ids, child_map, child_front, ahead, child_x, pivots_ahead, parent_vals
+    )
+    parts = exchanged(keep + sibling(send))
+    piece = jnp.concatenate([parts[1, :40], parts[1, 40:] + parts[2, 40:]], axis=0)
+    mine = gathered(piece)
+    panel_later, _ = lax.optimization_barrier((child_panel, piece))
+    keep, send = schur(ids, child_map, child_front, panel_later, child_x, tops)
+    theirs = sibling(mine[:, :40])
+    top_theirs = sibling(mine[:, 40:])
+    own = keep + sibling(send)
+    arrived = lax.ppermute(own[:N], "tile", [(i, i - 1) for i in range(1, 16)])
+    x, s, l = inverse_first(ids, mine, theirs)
+    assembled, _ = lax.optimization_barrier((own[N:] + parent_vals + arrived, x))
     other = sibling(assembled)
-    parent_x = inverse_of(whole, 32)
-    result = parent_step(ids, assembled, other, parent_x, whole, top_theirs)
+    parent_x = inverse_last(x, s, l)
+    result = parent_step(ids, assembled, other, parent_x, mine, top_theirs)
     return (child_panel[None], result[None])
 
 

time: 230 us -> 184 us (0.80)
  waiting for transfers between devices: 75.7 us -> 17.1 us
  blocking collectives: 47.3 us -> 61.4 us
  Pallas kernels: 67.9 us -> 75.3 us
  starting transfers between devices: 15 us -> 7.7 us
  other arithmetic: 5.05 us -> 1.01 us
  local copies, waits for them, and re-layouts: 4.44 us -> 7.11 us
    all_to_all x2 -> x1, waiting for transfers between devices: 41.2 us -> 8.72 us  [exchanged(): return lax.all_to_all(x, 'tile', 0, 0)]
    ppermute x2 -> x3, waiting for transfers between devices: 20.3 us -> 6.1 us  [the longest x1 6.09 us: local(): arrived = lax.ppermute(own[:N], 'tile', [(i, i - 1) for i in range(1, 16)])]
    all_to_all x2 -> x3, blocking collectives: 47.3 us -> 61.4 us  [exchanged(): return lax.all_to_all(x, 'tile', 0, 0)]
    pallas_call x4 -> x7, Pallas kernels: 67.9 us -> 75.3 us  [the longest x1 25.8 us: inverse_whole(): pl.pallas_call(whole_kernel, out_shape=SQUARE, in_specs=[VMEM], out_specs...]
    ppermute x5, waiting for transfers between devices: 8.49 us -> 2.22 us  [sibling(): return lax.ppermute(x, 'front', [(i, i ^ 1) for i in range(16)])]
    all_gather x1, waiting for transfers between devices: 5.75 us -> 0.02 us  [local(): tops = lax.all_gather(pieces[1:3], 'tile')]
    ppermute x2 -> x3, starting transfers between devices: 6.83 us -> 2.87 us  [the longest x1 1.29 us: local(): arrived = lax.ppermute(own[:N], 'tile', [(i, i - 1) for i in range(1, 16)])]
    all_to_all x2 -> x1, starting transfers between devices: 7.69 us -> 3.84 us  [exchanged(): return lax.all_to_all(x, 'tile', 0, 0)]
  transfers between devices with their start and end apart: 10 -> 10, of which waited for: 7 -> 3; matrix products, arithmetic and copies ran while one was open for 2% -> 2% of each run, Pallas kernels for 23% -> 32%
where the time goes in v2:
time: 184 us
  Pallas kernels  75.3 us (41%)
  blocking collectives  61.4 us (33%)
  waiting for transfers between devices  17.1 us (9%)
  between operations  14.3 us (8%)
  starting transfers between devices  7.7 us (4%)
  local copies, waits for them, and re-layouts  7.11 us (4%)
    all_to_all x3, blocking collectives, exchanged(): return lax.all_to_all(x, 'tile', 0, 0)  61.4 us
    pallas_call x1, Pallas kernels, inverse_whole(): pl.pallas_call(whole_kernel, out_shape=SQUARE, in_specs=[VMEM], out_specs...  25.8 us
    pallas_call x1, Pallas kernels, inverse_first(): pl.pallas_call(first_kernel, out_shape=[SQUARE] * 3, in_specs=[SMEM, VMEM...  20 us
    pallas_call x1, Pallas kernels, schur(): pl.pallas_call(schur_kernel, out_shape=[jax.ShapeDtypeStruct((2 * N, N),...  10.6 us
    all_to_all x1, waiting for transfers between devices, exchanged(): return lax.all_to_all(x, 'tile', 0, 0)  8.72 us
    pallas_call x1, Pallas kernels, corner(): pl.pallas_call(corner_kernel, grid=(1,), out_shape=[SQUARE] + [jax.ShapeD...  7.33 us
    pallas_call x1, Pallas kernels, inverse_last(): pl.pallas_call(last_kernel, out_shape=SQUARE, in_specs=[VMEM] * 3, out_sp...  6.38 us
    ppermute x1, waiting for transfers between devices, local(): arrived = lax.ppermute(own[:N], 'tile', [(i, i - 1) for i in range(1, 16)])  6.09 us
  transfers between devices with their start and end apart: 10, of which 3 were waited for; matrix products, arithmetic and copies ran while one was open for 2% of the time, Pallas kernels for 32%

profile of v2, /device:TPU:32, one launch (start us, length us, event | category | flops | bytes accessed | tf_op | source)
XLA Modules:
  0.0 183.9 jit_solution(5108113105480370089)
XLA Ops:
  7.2 0.1 pad_add_fusion.ids
  7.2 0.0 copy-start
  7.2 1.9 %copy-done = f32[1,512,1536]{2,1,0:T(8,128)S(1)} copy-done((f32[1,512,1536]{2,1,0:T(8,128)S(1)}, f32[1,512,1536]{2,1,0:T(8,128)}, u32[]{:S(2)}) %copy-start) | copy-done | bytes 3145752
  9.1 0.8 shard_map.50
  9.9 23.5 %all_to_all.20 = f32[16,128,128]{2,1,0:T(8,128)S(1)} all-to-all(f32[16,128,128]{2,1,0:T(8,128)S(1)} %shard_map.50), channel_id=1, replica_groups=mesh['front'=16,'tile'=16] {'tile'}, dimensions={0} | all-to-all | bytes 2097152 | tf_op jit(solution)/shard_map/all_to_all | solution.py:343
  33.4 0.0 copy-start.1
  33.5 0.9 broadcast_in_dim.20
  34.3 3.8 %all-to-all-start.1 = ((f32[16,80,128]{2,1,0:T(8,128)}), f32[16,80,128]{2,1,0:T(8,128)S(1)}, u32[]{:S(2)}, u32[]{:S(2)}) async-start(f32[16,80,128]{2,1,0:T(8,128)} %broadcast_in_dim.20), calls=%async_computation.1 | async-start | bytes 1310720 | tf_op jit(solution)/shard_map/all_to_all | solution.py:343
  38.2 0.0 all-gather.3.cloned.1.call-start
  38.2 2.3 %slice_bitcast_fusion = f32[512,512]{1,0:T(8,128)} fusion(f32[1,512,1536]{2,1,0:T(8,128)} %a_ref.5), kind=kLoop, calls=%fused_computation.2 | loop fusion | bytes 2097152 | tf_op jit(solution)/shard_map/squeeze | solution.py:363
  40.5 0.6 slice.44
  41.1 0.0 all-gather.3.cloned.1.call-update
  41.2 8.7 %all-to-all-done.1.a_ref = f32[16,80,128]{2,1,0:T(8,128)S(1)} async-done(((f32[16,80,128]{2,1,0:T(8,128)}), f32[16,80,128]{2,1,0:T(8,128)S(1)}, u32[]{:S(2)}, u32[]{:S(2)}) %all-to-all-start.1) | async-done | bytes 655392 | tf_op jit(solution)/shard_map/all_to_all | solution.py:343
  49.9 0.0 copy-start.2
  49.9 0.8 collective-permute-start
  50.7 0.0 copy-done.1
  50.8 0.7 collective-permute-start.1
  51.5 25.8 %shard_map.51.x_ref = f32[512,512]{1,0:T(8,128)S(1)} custom-call(f32[16,80,128]{2,1,0:T(8,128)S(1)} %all-to-all-done.1.a_ref), custom_call_target="tpu_custom_call" | custom-call | flops 24999999488 | bytes 2097152 | tf_op jit(solution)/shard_map/pallas_call | solution.py:142
  77.3 0.0 copy-start.4
  77.4 0.0 collective-permute-done.ahead_ref
  77.4 0.0 collective-permute-done.1.pp_ref
  77.4 0.0 copy-done.2
  77.4 7.3 %shard_map.52 = (f32[512,512]{1,0:T(8,128)}, f32[16,104,128]{2,1,0:T(8,128)S(1)}, f32[16,104,128]{2,1,0:T(8,128)S(1)}) custom-call(s32[2]{0:T(128)S(1)} %pad_add_fusion.ids, s32[16,60]{1,0:T(8,128)S(1)} %copy-done.2, f32[1,512,1536]{2,1,0:T(8,128)} %a_ref.5, f32[512,512]{1,0:T(8,128)S(1)} %collective-permute-done.ahead_ref, f32[512,512]{1,0:T(8,128)S(1)} %shard_map.51.x_ref, ...), custom_call_target="tpu_custom_call" | custom-call | flops 3000000000 | bytes 2097152 | tf_op jit(solution)/shard_map/pallas_call | solution.py:260
  84.7 0.0 copy-done.4
  84.7 0.2 collective-permute-start.2
  84.9 2.2 %collective-permute-done.2 = f32[16,104,128]{2,1,0:T(8,128)S(1)} collective-permute-done((f32[16,104,128]{2,1,0:T(8,128)S(1)}, f32[16,104,128]{2,1,0:T(8,128)S(1)}, u32[]{:S(2)}, u32[]{:S(2)}) %collective-permute-start.2) | collective-permute-done | bytes 852000 | tf_op jit(solution)/shard_map/ppermute | solution.py:351
  87.1 0.0 copy-start.3
  87.1 0.1 add.18
  87.2 18.9 %all_to_all.21 = f32[16,104,128]{2,1,0:T(8,128)S(1)} all-to-all(f32[16,104,128]{2,1,0:T(8,128)S(1)} %add.18), channel_id=1, replica_groups=mesh['front'=16,'tile'=16] {'tile'}, dimensions={0} | all-to-all | bytes 1703936 | tf_op jit(solution)/shard_map/all_to_all | solution.py:343
  106.1 0.0 all-gather.3.cloned.1.call-done
  106.1 0.0 copy-done.3
  106.1 0.0 copy-start.5
  106.1 1.2 copy-done.5
  107.4 10.6 %shard_map.53 = (f32[1024,512]{1,0:T(8,128)S(1)}, f32[1024,512]{1,0:T(8,128)}) custom-call(s32[2]{0:T(128)S(1)} %pad_add_fusion.ids, s32[16,60]{1,0:T(8,128)S(1)} %copy-done.2, f32[1,512,1536]{2,1,0:T(8,128)} %a_ref.5, f32[512,512]{1,0:T(8,128)S(1)} %copy-done.3, f32[512,512]{1,0:T(8,128)S(1)} %copy-done.5, f32[16,2,128,128]{3,2,1,0:T(8,128)} %bitcast.18), custom_call_target="tpu_custom_call" | custom-call | flops 8000000000 | bytes 2097152 | tf_op jit(solution)/shard_map/pallas_call | solution.py:296
  117.9 0.0 collective-permute-start.3
  117.9 0.1 broadcast_in_dim.22
  118.0 19.0 %all_to_all.22.mine_ref = f32[16,104,128]{2,1,0:T(8,128)S(1)} all-to-all(f32[16,104,128]{2,1,0:T(8,128)S(1)} %broadcast_in_dim.22), channel_id=1, replica_groups=mesh['front'=16,'tile'=16] {'tile'}, dimensions={0} | all-to-all | bytes 1703936 | tf_op jit(solution)/shard_map/all_to_all | solution.py:343
  137.1 0.1 collective-permute-start.5
  137.2 0.0 collective-permute-done.3
  137.2 0.5 add.21
  137.7 0.1 slice.46
  137.7 1.3 collective-permute-start.4
  139.0 0.0 collective-permute-done.5.theirs_ref
  139.0 20.0 %shard_map.54 = (f32[512,512]{1,0:T(8,128)S(1)}, f32[512,512]{1,0:T(8,128)S(1)}, f32[512,512]{1,0:T(8,128)S(1)}) custom-call(s32[2]{0:T(128)S(1)} %pad_add_fusion.ids, f32[16,104,128]{2,1,0:T(8,128)S(1)} %all_to_all.22.mine_ref, f32[16,40,128]{2,1,0:T(8,128)S(1)} %collective-permute-done.5.theirs_ref), custom_call_target="tpu_custom_call" | custom-call | flops 20000000000 | bytes 2097152 | tf_op jit(solution)/shard_map/pallas_call | solution.py:154
  159.1 6.1 %collective-permute-done.4 = f32[512,512]{1,0:T(8,128)S(1)} collective-permute-done((f32[512,512]{1,0:T(8,128)S(1)}, f32[512,512]{1,0:T(8,128)S(1)}, u32[]{:S(2)}, u32[]{:S(2)}) %collective-permute-start.4) | collective-permute-done | bytes 1048608 | tf_op jit(solution)/shard_map/ppermute | solution.py:380
  165.2 0.3 fusion.own_ref
  165.5 0.1 collective-permute-start.6
  165.7 0.6 collective-permute-start.7
  166.3 6.4 %shard_map.55.x_ref = f32[512,512]{1,0:T(8,128)S(1)} custom-call(f32[512,512]{1,0:T(8,128)S(1)} %get-tuple-element.24.xin_ref, f32[512,512]{1,0:T(8,128)S(1)} %get-tuple-element.26.s_ref, f32[512,512]{1,0:T(8,128)S(1)} %get-tuple-element.27.l_ref), custom_call_target="tpu_custom_call" | custom-call | flops 6000000000 | bytes 2097152 | tf_op jit(solution)/shard_map/pallas_call | solution.py:166
  172.7 0.0 collective-permute-done.7.theirs_ref
  172.7 0.0 collective-permute-done.6.other_ref
  172.7 4.4 %shard_map.56 = f32[512,512]{1,0:T(8,128)} custom-call(s32[2]{0:T(128)S(1)} %pad_add_fusion.ids, f32[512,512]{1,0:T(8,128)S(1)} %fusion.own_ref, f32[512,512]{1,0:T(8,128)S(1)} %collective-permute-done.6.other_ref, f32[512,512]{1,0:T(8,128)S(1)} %shard_map.55.x_ref, f32[16,104,128]{2,1,0:T(8,128)S(1)} %all_to_all.22.mine_ref, ...), custom_call_target="tpu_custom_call" | custom-call | flops 4000000000 | bytes 2097152 | tf_op jit(solution)/shard_map/pallas_call | solution.py:332
  (6 shorter events, 0.1 us)
Async XLA Ops:
  7.2 1.9 %copy-start = (f32[1,512,1536]{2,1,0:T(8,128)S(1)}, f32[1,512,1536]{2,1,0:T(8,128)}, u32[]{:S(2)}) copy-start(f32[1,512,1536]{2,1,0:T(8,128)} %a_ref.5) | copy-start | bytes 9437188
  33.4 17.3 %copy-start.1 = (f32[1,512,512]{2,1,0:T(8,128)S(1)}, f32[1,512,512]{2,1,0:T(8,128)}, u32[]{:S(2)}) copy-start(f32[1,512,512]{2,1,0:T(8,128)} %param.4) | copy-start | bytes 3145732
  34.3 15.6 %all-to-all-start.1 = ((f32[16,80,128]{2,1,0:T(8,128)}), f32[16,80,128]{2,1,0:T(8,128)S(1)}, u32[]{:S(2)}, u32[]{:S(2)}) async-start(f32[16,80,128]{2,1,0:T(8,128)} %broadcast_in_dim.20), calls=%async_computation.1 | async-start | bytes 1310720 | tf_op jit(solution)/shard_map/all_to_all | solution.py:343
  38.2 67.9 %all-gather.3.cloned.1.call-start = ((), (), s32[]{:S(2)}) async-start(), calls=%async_computation.4 | async-start | bytes 2228224 | tf_op jit(solution)/shard_map/all_gather | solution.py:361
  49.9 27.5 %copy-start.2 = (s32[16,60]{1,0:T(8,128)S(1)}, s32[16,60]{1,0:T(8,128)}, u32[]{:S(2)}) copy-start(s32[16,60]{1,0:T(8,128)} %cmap.3) | copy-start | bytes 11524
  49.9 27.5 %collective-permute-start = (f32[512,512]{1,0:T(8,128)}, f32[512,512]{1,0:T(8,128)S(1)}, u32[]{:S(2)}, u32[]{:S(2)}) collective-permute-start(f32[512,512]{1,0:T(8,128)} %slice_bitcast_fusion), channel_id=1, source_target_pairs={{1,2},{17,18},{33,34},{49,50},{65,66},{81,82},{97,98},{113,114},{1... | collective-permute-start | bytes 3145736 | tf_op jit(solution)/shard_map/ppermute | solution.py:364
  50.8 26.6 %collective-permute-start.1 = (f32[512,512]{1,0:T(8,128)S(1)}, f32[512,512]{1,0:T(8,128)S(1)}, u32[]{:S(2)}, u32[]{:S(2)}) collective-permute-start(f32[512,512]{1,0:T(8,128)S(1)} %bitcast.15), channel_id=1, source_target_pairs={{16,17},{48,49},{80,81},{112,113},{144,145},{176,177},{208,209},{2... | collective-permute-start | bytes 3145736 | tf_op jit(solution)/shard_map/ppermute | solution.py:365
  77.3 7.4 %copy-start.4 = (f32[512,512]{1,0:T(8,128)}, f32[512,512]{1,0:T(8,128)S(1)}, u32[]{:S(2)}) copy-start(f32[512,512]{1,0:T(8,128)S(1)} %shard_map.51.x_ref) | copy-start | bytes 3145732
  84.7 2.4 %collective-permute-start.2 = (f32[16,104,128]{2,1,0:T(8,128)S(1)}, f32[16,104,128]{2,1,0:T(8,128)S(1)}, u32[]{:S(2)}, u32[]{:S(2)}) collective-permute-start(f32[16,104,128]{2,1,0:T(8,128)S(1)} %get-tuple-element.20), channel_id=1, source_target_pairs={{0,16},{16,0},{32,48},{48,32},{64,80},{80,64},{96,112},{112,96},{1... | collective-permute-start | bytes 2555912 | tf_op jit(solution)/shard_map/ppermute | solution.py:351
  87.1 19.0 %copy-start.3 = (f32[512,512]{1,0:T(8,128)S(1)}, f32[512,512]{1,0:T(8,128)}, u32[]{:S(2)}) copy-start(f32[512,512]{1,0:T(8,128)} %get-tuple-element.21.panel_ref) | copy-start | bytes 3145732
  106.1 1.2 copy-start.5
  117.9 19.2 %collective-permute-start.3 = (f32[1024,512]{1,0:T(8,128)}, f32[1024,512]{1,0:T(8,128)S(1)}, u32[]{:S(2)}, u32[]{:S(2)}) collective-permute-start(f32[1024,512]{1,0:T(8,128)} %get-tuple-element.23), channel_id=1, source_target_pairs={{0,16},{16,0},{32,48},{48,32},{64,80},{80,64},{96,112},{112,96},{1... | collective-permute-start | bytes 6291464 | tf_op jit(solution)/shard_map/ppermute | solution.py:351
  137.1 2.0 %collective-permute-start.5 = (f32[16,40,128]{2,1,0:T(8,128)S(1)}, f32[16,40,128]{2,1,0:T(8,128)S(1)}, u32[]{:S(2)}, u32[]{:S(2)}) collective-permute-start(f32[16,40,128]{2,1,0:T(8,128)S(1)} %slice.47), channel_id=1, source_target_pairs={{0,16},{16,0},{32,48},{48,32},{64,80},{80,64},{96,112},{112,96},{1... | collective-permute-start | bytes 983048 | tf_op jit(solution)/shard_map/ppermute | solution.py:351
  137.7 27.4 %collective-permute-start.4 = (f32[512,512]{1,0:T(8,128)S(1)}, f32[512,512]{1,0:T(8,128)S(1)}, u32[]{:S(2)}, u32[]{:S(2)}) collective-permute-start(f32[512,512]{1,0:T(8,128)S(1)} %slice.46), channel_id=1, source_target_pairs={{1,0},{2,1},{3,2},{4,3},{5,4},{6,5},{7,6},{8,7},{9,8},{10,9},{11,1... | collective-permute-start | bytes 3145736 | tf_op jit(solution)/shard_map/ppermute | solution.py:380
  165.5 7.1 %collective-permute-start.6 = (f32[512,512]{1,0:T(8,128)S(1)}, f32[512,512]{1,0:T(8,128)S(1)}, u32[]{:S(2)}, u32[]{:S(2)}) collective-permute-start(f32[512,512]{1,0:T(8,128)S(1)} %fusion.own_ref), channel_id=1, source_target_pairs={{0,16},{16,0},{32,48},{48,32},{64,80},{80,64},{96,112},{112,96},{1... | collective-permute-start | bytes 3145736 | tf_op jit(solution)/shard_map/ppermute | solution.py:351
  165.7 7.0 %collective-permute-start.7 = (f32[16,64,128]{2,1,0:T(8,128)S(1)}, f32[16,64,128]{2,1,0:T(8,128)S(1)}, u32[]{:S(2)}, u32[]{:S(2)}) collective-permute-start(f32[16,64,128]{2,1,0:T(8,128)S(1)} %slice.48), channel_id=1, source_target_pairs={{0,16},{16,0},{32,48},{48,32},{64,80},{80,64},{96,112},{112,96},{1... | collective-permute-start | bytes 1572872 | tf_op jit(solution)/shard_map/ppermute | solution.py:351
Sparse Core Ops, SparseCore 0:
  41.5 52.7 all-gather.2

commit v3 on v2

--- a/solution.py
+++ b/solution.py
@@ -31,40 +31,38 @@
     out = []
     for p in range(16):
         cols = [column_of(left[p], 8 * p + j) for j in range(8)]
-        v, xv, xf = left[p], right[p], right[p]
-        diag = jnp.zeros((8, B), F32)
+        v, xv = left[p], right[p]
+        xf = diag = None
+        pivot = row_of(cols[0], 0)
         for j in range(8):
-            pivot = row_of(cols[j], j)
             recip = 1.0 / pivot
-            diag = jnp.where(sub == j, pivot, diag)
-            scale = jnp.where(sub == j, 0.0, cols[j]) * recip
-            below = jnp.where(sub > j, cols[j], 0.0) * recip
-            for m in range(j + 1, 8):
-                cm = row_of(cols[m], j)
-                cols[m] = jnp.where(sub == j, cm * recip, cols[m] - scale * cm)
-            vr, xr, fr = row_of(v, j), row_of(xv, j), row_of(xf, j)
-            v = jnp.where(sub == j, vr * recip, v - scale * vr)
-            xv = jnp.where(sub == j, xr * recip, xv - scale * xr)
-            xf = xf - below * fr
+            hit = sub == j
+            diag = pivot if diag is None else jnp.where(hit, pivot, diag)
+            rows = [row_of(cols[m], j) for m in range(j + 1, 8)]
+            if j < 7:
+                pivot = row_of(cols[j + 1], j + 1) - (rows[0] * rows[0]) * recip
+            scale = jnp.where(hit, 0.0, cols[j]) * recip
+            for m, cm in zip(range(j + 1, 8), rows):
+                cols[m] = jnp.where(hit, cm * recip, cols[m] - scale * cm)
+            vr, xr = row_of(v, j), row_of(xv, j)
+            xf = xr if xf is None else jnp.where(hit, xr, xf)
+            v = jnp.where(hit, vr * recip, v - scale * vr)
+            xv = jnp.where(hit, xr * recip, xv - scale * xr)
         out.append(xf * lax.rsqrt(diag))
         if p < 15:
             w = [row_of(v, j) for j in range(8)]
             xw = [row_of(xv, j) for j in range(8)]
             for q in range(p + 1, 16):
                 c = [column_of(left[q], 8 * p + j) for j in range(8)]
-                s, x = c[0] * w[0], c[0] * xw[0]
-                for j in range(1, 8):
-                    s = s + c[j] * w[j]
-                    x = x + c[j] * xw[j]
-                left[q] = left[q] - s
-                right[q] = right[q] - x
+                left[q] = left[q] - total([c[j] * w[j] for j in range(8)])
+                right[q] = right[q] - total([c[j] * xw[j] for j in range(8)])
     return jnp.concatenate(out, axis=0)
 
 
-def dot_f32(a, b, dims):
-    return lax.dot_general(
-        a, b, (dims, ((), ())), precision=lax.Precision.HIGHEST, preferred_element_type=F32
-    )
+def total(terms):
+    while len(terms) > 1:
+        terms = [terms[i] + terms[i + 1] for i in range(0, len(terms), 2)]
+    return terms[0]
 
 
 def at(i):
@@ -79,28 +77,21 @@
         k0 = pl.multiple_of(k * B, B)
         xk = inverse_factor(lambda q: s_ref[pl.ds(pl.multiple_of(k0 + 8 * q, 8), 8), at(k)])
         x_ref[at(k), at(k)] = xk
-
-        def x_row(j, carry):
-            def acc(m, t):
-                return t + dot_f32(l_ref[at(k), at(m)], x_ref[at(m), at(j)], NN)
-
-            t = lax.fori_loop(j, k, acc, jnp.zeros((B, B), F32))
-            x_ref[at(k), at(j)] = -dot_f32(xk, t, NN)
-            return carry
-
-        lax.fori_loop(0, k, x_row, 0)
-
-        def l_col(i, carry):
-            l_ref[at(i), at(k)] = dot_f32(s_ref[at(i), at(k)], xk, NT)
-
-            def update(j, carry):
-                s_ref[at(i), at(j)] -= dot_f32(l_ref[at(i), at(k)], l_ref[at(j), at(k)], NT)
-                return carry
-
-            lax.fori_loop(k + 1, i + 1, update, 0)
-            return carry
-
-        lax.fori_loop(k + 1, 4, l_col, 0)
+        xs = split(xk)
+        for c in range(*steps):
+
+            @pl.when(k == c)
+            def _():
+                lo, hi = c * B, (c + 1) * B
+                if c > 0:
+                    w = dot_split(split(l_ref[lo:hi, :lo]), split(x_ref[:lo, :lo]), NN)
+                    x_ref[lo:hi, :lo] = -dot_split(xs, split(w), NN)
+                if c < 3:
+                    col = dot_split(split(s_ref[hi:, lo:hi]), xs)
+                    l_ref[hi:, lo:hi] = col
+                    col = split(col)
+                    s_ref[hi:, hi:] -= dot_split(col, col)
+
         return carry
 
     lax.fori_loop(steps[0], steps[1], step, 0)
@@ -229,7 +220,8 @@
     parity = lax.rem(front, 2)
     x = split(x_ref[...])
     panel_ref[...] = dot_split(split(a_ref[0, :, :N]), x)
-    top = split(dot_split(split(jnp.where(tile == 1, a_ref[0, :, :N], ahead_ref[...])), x))
+    raw = [ahead_ref[:, 32 * c : 32 * c + 32, :].reshape(N, B) for c in range(4)]
+    top = split(dot_split(split(jnp.concatenate(raw, axis=1)), x))
     b_ref[...] = jnp.zeros_like(b_ref)
     for i in range(4):
         rows = slice(i * B, (i + 1) * B)
@@ -257,11 +249,12 @@
 def corner(ids, cmap, front_vals, ahead, x, pp, pf):
     full = pl.BlockSpec((N, N), lambda i: (0, 0))
     piece = pl.BlockSpec((16, 104, B), lambda i: (0, 0, 0))
+    lead = pl.BlockSpec((16, B, B), lambda i: (0, 0, 0))
     return pl.pallas_call(
         corner_kernel,
         grid=(1,),
         out_shape=[SQUARE] + [jax.ShapeDtypeStruct((16, 104, B), F32)] * 2,
-        in_specs=[SMEM, SMEM, pl.BlockSpec((1, N, 2 * N), lambda i: (0, 0, 0)), full, full, full, full],
+        in_specs=[SMEM, SMEM, pl.BlockSpec((1, N, 2 * N), lambda i: (0, 0, 0)), lead, full, full, full],
         out_specs=[full, piece, piece],
         scratch_shapes=[pltpu.VMEM((2 * N, N), F32), pltpu.VMEM((1280, B), F32)],
         compiler_params=PARAMS,
@@ -275,7 +268,9 @@
     x = split(x_ref[...])
     tops = []
     for h in range(2):
-        raw = [top_ref[:, h, 32 * c : 32 * c + 32, :].reshape(N, B) for c in range(4)]
+        raw = [
+            top_ref[:, h * B + 32 * c : h * B + 32 * c + 32, :].reshape(N, B) for c in range(4)
+        ]
         tops.append(split(dot_split(split(jnp.concatenate(raw, axis=1)), x)))
     keep_ref[...] = jnp.zeros_like(keep_ref)
     send_ref[...] = jnp.zeros_like(send_ref)
@@ -288,14 +283,14 @@
 
         @pl.when(tile > 0)
         def _():
-            keep_ref[at(place), :] = jnp.where(parity == 1, first, second)
-            send_ref[at(place), :] = jnp.where(parity == 1, second, first)
+            keep_ref[at(place - 1), :] = jnp.where(parity == 1, first, second)
+            send_ref[at(place - 1), :] = jnp.where(parity == 1, second, first)
 
 
 def schur(ids, cmap, front_vals, panel, x, tops):
     return pl.pallas_call(
         schur_kernel,
-        out_shape=[jax.ShapeDtypeStruct((2 * N, N), F32)] * 2,
+        out_shape=[jax.ShapeDtypeStruct((6 * B, N), F32)] * 2,
         in_specs=[SMEM, SMEM, VMEM, VMEM, VMEM, VMEM],
         out_specs=[VMEM] * 2,
         compiler_params=PARAMS,
@@ -339,6 +334,41 @@
     )(ids, own, other, x, mine, theirs)
 
 
+def fan_tops_kernel(parts_ref, out_ref, sems):
+    copies = []
+    for t in range(16):
+        copies.append(
+            pltpu.make_async_copy(parts_ref.at[pl.ds(1, 2)], out_ref.at[t], sems.at[t])
+        )
+    for copy in copies:
+        copy.start()
+    for copy in copies:
+        copy.wait()
+
+
+def fan_corner_kernel(parts_ref, out_ref, piece_ref, sems):
+    piece_ref[:40, :] = parts_ref[1, :40, :]
+    piece_ref[40:, :] = parts_ref[1, 40:, :] + parts_ref[2, 40:, :]
+    copies = []
+    for t in range(16):
+        copies.append(pltpu.make_async_copy(piece_ref, out_ref.at[t], sems.at[t]))
+    for copy in copies:
+        copy.start()
+    for copy in copies:
+        copy.wait()
+
+
+def fanned(kernel, parts, shape, scratch):
+    return pl.pallas_call(
+        kernel,
+        out_shape=pltpu.HBM(shape, F32),
+        in_specs=[VMEM],
+        out_specs=pl.BlockSpec(memory_space=pltpu.HBM),
+        scratch_shapes=scratch + [pltpu.SemaphoreType.DMA((16,))],
+        compiler_params=PARAMS,
+    )(parts)
+
+
 def exchanged(x):
     return lax.all_to_all(x, "tile", 0, 0)
 
@@ -358,28 +388,33 @@
     parent_vals = parent_front[0]
 
     pieces = exchanged(spread(ids, child_front))
-    tops = lax.all_gather(pieces[1:3], "tile")
     pivot = gathered(pieces[0, :80])
-    columns, parents, pivot = lax.optimization_barrier((child_front[0, :, :N], parent_vals, pivot))
-    ahead = lax.ppermute(columns, "tile", [(1, 2)])
+    parents, pieces, pivot = lax.optimization_barrier((parent_vals, pieces, pivot))
     pivots_ahead = lax.ppermute(
         parents, ("front", "tile"), [(f * 16, f * 16 + 1) for f in range(1, 16, 2)]
     )
+    fan = fanned(fan_tops_kernel, pieces, (16, 2, B, B), [])
+    fan, pivot = lax.optimization_barrier((fan, pivot))
+    tops = exchanged(fan).reshape(16, 2 * B, B)
     child_x = inverse_whole(pivot)
     child_panel, keep, send = corner(
-        ids, child_map, child_front, ahead, child_x, pivots_ahead, parent_vals
+        ids, child_map, child_front, tops, child_x, pivots_ahead, parent_vals
     )
     parts = exchanged(keep + sibling(send))
-    piece = jnp.concatenate([parts[1, :40], parts[1, 40:] + parts[2, 40:]], axis=0)
-    mine = gathered(piece)
-    panel_later, _ = lax.optimization_barrier((child_panel, piece))
+    fan = fanned(fan_corner_kernel, parts, (16, 104, B), [pltpu.VMEM((104, B), F32)])
+    fan, panel_later = lax.optimization_barrier((fan, child_panel))
+    mine = exchanged(fan)
     keep, send = schur(ids, child_map, child_front, panel_later, child_x, tops)
+    send, mine = lax.optimization_barrier((send, mine))
     theirs = sibling(mine[:, :40])
+    own = keep + sibling(send)
     top_theirs = sibling(mine[:, 40:])
-    own = keep + sibling(send)
-    arrived = lax.ppermute(own[:N], "tile", [(i, i - 1) for i in range(1, 16)])
+    arrived = lax.ppermute(own[: 3 * B], "tile", [(i, i - 1) for i in range(1, 16)])
     x, s, l = inverse_first(ids, mine, theirs)
-    assembled, _ = lax.optimization_barrier((own[N:] + parent_vals + arrived, x))
+    assembled = (
+        parent_vals + jnp.pad(own[3 * B :], ((0, B), (0, 0))) + jnp.pad(arrived, ((B, 0), (0, 0)))
+    )
+    assembled, _ = lax.optimization_barrier((assembled, x))
     other = sibling(assembled)
     parent_x = inverse_last(x, s, l)
     result = parent_step(ids, assembled, other, parent_x, mine, top_theirs)

time: 184 us -> 166 us (0.902)
  between operations: 14.3 us -> 0.84 us
  Pallas kernels: 75.3 us -> 61.9 us
  starting transfers between devices: 7.7 us -> 15.9 us
  blocking collectives: 61.4 us -> 57.8 us
  waiting for transfers between devices: 17.1 us -> 19.7 us
    pallas_call x1, Pallas kernels: 25.8 us -> 18.8 us  [inverse_whole(): pl.pallas_call(whole_kernel, out_shape=SQUARE, in_specs=[VMEM], out_specs...]
    pallas_call x1, Pallas kernels: 20 us -> 14.8 us  [inverse_first(): pl.pallas_call(first_kernel, out_shape=[SQUARE] * 3, in_specs=[SMEM, VMEM...]
    unnamed x12 -> x16, local copies, waits for them, and re-layouts: 3.12 us -> 7.69 us
    all_to_all x1 -> x2, starting transfers between devices: 3.84 us -> 8.41 us  [exchanged(): return lax.all_to_all(x, 'tile', 0, 0)]
    ppermute x5, starting transfers between devices: 0.94 us -> 5.48 us  [sibling(): return lax.ppermute(x, 'front', [(i, i ^ 1) for i in range(16)])]
    all_to_all x3, blocking collectives: 61.4 us -> 57.8 us  [exchanged(): return lax.all_to_all(x, 'tile', 0, 0)]
    ppermute x5, waiting for transfers between devices: 2.22 us -> 5.48 us  [sibling(): return lax.ppermute(x, 'front', [(i, i ^ 1) for i in range(16)])]
    squeeze x2 -> x0, local copies, waits for them, and re-layouts: 2.27 us -> none  [the longest x1 2.26 us: local(): child_front[0, :, :N]]
  transfers between devices with their start and end apart: 10 -> 9, of which waited for: 3 -> 5; matrix products, arithmetic and copies ran while one was open for 2% -> 0% of each run, Pallas kernels for 32% -> 29%
where the time goes in v3:
time: 166 us; the launch traced here: 165 us
  Pallas kernels  61.9 us (37%)
  blocking collectives  57.8 us (35%)
  waiting for transfers between devices  19.7 us (12%)
  starting transfers between devices  15.9 us (10%)
  local copies, waits for them, and re-layouts  7.93 us (5%)
    all_to_all x3, blocking collectives, exchanged(): return lax.all_to_all(x, 'tile', 0, 0)  57.8 us
    pallas_call x1, Pallas kernels, inverse_whole(): pl.pallas_call(whole_kernel, out_shape=SQUARE, in_specs=[VMEM], out_specs...  18.8 us
    pallas_call x1, Pallas kernels, inverse_first(): pl.pallas_call(first_kernel, out_shape=[SQUARE] * 3, in_specs=[SMEM, VMEM...  14.8 us
    pallas_call x1, Pallas kernels, schur(): pl.pallas_call(schur_kernel, out_shape=[jax.ShapeDtypeStruct((6 * B, N),...  8.99 us
    all_to_all x2, waiting for transfers between devices, exchanged(): return lax.all_to_all(x, 'tile', 0, 0)  8.81 us
    all_to_all x2, starting transfers between devices, exchanged(): return lax.all_to_all(x, 'tile', 0, 0)  8.41 us
    unnamed x16, local copies, waits for them, and re-layouts  7.69 us
    pallas_call x1, Pallas kernels, corner(): pl.pallas_call(corner_kernel, grid=(1,), out_shape=[SQUARE] + [jax.ShapeD...  7.21 us
  transfers between devices with their start and end apart: 9, of which 5 were waited for; matrix products, arithmetic and copies ran while one was open for 0% of the time, Pallas kernels for 29%

profile of v3, /device:TPU:32, one launch (start us, length us, event | category | flops | bytes accessed | tf_op | source)
XLA Modules:
  0.0 164.8 jit_solution(15269271990942064466)
XLA Ops:
  0.6 0.1 pad_add_fusion.1.ids
  0.7 0.0 copy-start
  0.7 1.9 %copy-done = f32[1,512,1536]{2,1,0:T(8,128)S(1)} copy-done((f32[1,512,1536]{2,1,0:T(8,128)S(1)}, f32[1,512,1536]{2,1,0:T(8,128)}, u32[]{:S(2)}) %copy-start) | copy-done | bytes 3145752
  2.6 0.8 shard_map.50
  3.4 23.5 %all_to_all.25.parts_ref = f32[16,128,128]{2,1,0:T(8,128)S(1)} all-to-all(f32[16,128,128]{2,1,0:T(8,128)S(1)} %shard_map.50), channel_id=1, replica_groups=mesh['front'=16,'tile'=16] {'tile'}, dimensions={0} | all-to-all | bytes 2097152 | tf_op jit(solution)/shard_map/all_to_all | solution.py:373
  27.0 15.2 %all_to_all.26.a_ref = f32[16,80,128]{2,1,0:T(8,128)S(1)} all-to-all(f32[16,80,128]{2,1,0:T(8,128)S(1)} %broadcast_in_dim.14), channel_id=1, replica_groups=mesh['front'=16,'tile'=16] {'tile'}, dimensions={0} | all-to-all | bytes 1310720 | tf_op jit(solution)/shard_map/all_to_all | solution.py:373
  42.2 1.4 shard_map.51
  43.6 0.0 copy-start.1
  43.6 4.6 %all-to-all-start.2 = ((f32[16,2,128,128]{3,2,1,0:T(8,128)}), f32[16,2,128,128]{3,2,1,0:T(8,128)}, u32[]{:S(2)}, u32[]{:S(2)}) async-start(f32[16,2,128,128]{3,2,1,0:T(8,128)} %shard_map.51), calls=%async_computation.2 | async-start | bytes 4194304 | tf_op jit(solution)/shard_map/all_to_all | solution.py:373
  48.2 0.0 copy-done.1
  48.2 0.0 copy-start.3
  48.2 0.7 collective-permute-start
  49.0 18.8 %shard_map.52.x_ref = f32[512,512]{1,0:T(8,128)S(1)} custom-call(f32[16,80,128]{2,1,0:T(8,128)S(1)} %all_to_all.26.a_ref), custom_call_target="tpu_custom_call" | custom-call | flops 24999999488 | bytes 2097152 | tf_op jit(solution)/shard_map/pallas_call | solution.py:133
  67.8 0.0 copy-start.5
  67.8 1.0 copy-done.5
  68.8 0.0 collective-permute-done.pp_ref
  68.8 7.2 %all-to-all-done.2 = f32[16,2,128,128]{3,2,1,0:T(8,128)} async-done(((f32[16,2,128,128]{3,2,1,0:T(8,128)}), f32[16,2,128,128]{3,2,1,0:T(8,128)}, u32[]{:S(2)}, u32[]{:S(2)}) %all-to-all-start.2) | async-done | bytes 2097184 | tf_op jit(solution)/shard_map/all_to_all | solution.py:373
  76.0 0.0 copy-done.3
  76.0 0.0 copy-start.6
  76.0 1.2 copy-done.6
  77.2 7.2 %shard_map.53 = (f32[512,512]{1,0:T(8,128)}, f32[16,104,128]{2,1,0:T(8,128)S(1)}, f32[16,104,128]{2,1,0:T(8,128)S(1)}) custom-call(s32[2]{0:T(128)S(1)} %pad_add_fusion.1.ids, s32[16,60]{1,0:T(8,128)S(1)} %copy-done.3, f32[1,512,1536]{2,1,0:T(8,128)} %a_ref.5, f32[16,256,128]{2,1,0:T(8,128)} %bitcast.4.ahead_ref.top_ref, f32[512,512]{1,0:T(8,128)S(1)} %copy-done.6, ...), custom_call_target="tpu_custom_call" | custom-call | flops 3000000000 | bytes 2097152 | tf_op jit(solution)/shard_map/pallas_call | solution.py:253
  84.4 4.0 %collective-permute-start.1 = (f32[16,104,128]{2,1,0:T(8,128)S(1)}, f32[16,104,128]{2,1,0:T(8,128)S(1)}, u32[]{:S(2)}, u32[]{:S(2)}) collective-permute-start(f32[16,104,128]{2,1,0:T(8,128)S(1)} %get-tuple-element.27), channel_id=1, source_target_pairs={{0,16},{16,0},{32,48},{48,32},{64,80},{80,64},{96,112},{112,96},{1... | collective-permute-start | bytes 2555912 | tf_op jit(solution)/shard_map/ppermute | solution.py:381
  88.4 2.0 %collective-permute-done.1 = f32[16,104,128]{2,1,0:T(8,128)S(1)} collective-permute-done((f32[16,104,128]{2,1,0:T(8,128)S(1)}, f32[16,104,128]{2,1,0:T(8,128)S(1)}, u32[]{:S(2)}, u32[]{:S(2)}) %collective-permute-start.1) | collective-permute-done | bytes 852000 | tf_op jit(solution)/shard_map/ppermute | solution.py:381
  90.4 0.1 add.16
  90.5 19.0 %all_to_all.27.parts_ref = f32[16,104,128]{2,1,0:T(8,128)S(1)} all-to-all(f32[16,104,128]{2,1,0:T(8,128)S(1)} %add.16), channel_id=1, replica_groups=mesh['front'=16,'tile'=16] {'tile'}, dimensions={0} | all-to-all | bytes 1703936 | tf_op jit(solution)/shard_map/all_to_all | solution.py:373
  109.5 1.1 shard_map.54
  110.6 3.8 %all-to-all-start.4 = ((f32[16,104,128]{2,1,0:T(8,128)}), f32[16,104,128]{2,1,0:T(8,128)S(1)}, u32[]{:S(2)}, u32[]{:S(2)}) async-start(f32[16,104,128]{2,1,0:T(8,128)} %shard_map.54), calls=%async_computation.4 | async-start | bytes 1703936 | tf_op jit(solution)/shard_map/all_to_all | solution.py:373
  114.4 0.0 copy-start.4
  114.4 1.2 copy-done.4
  115.7 0.0 copy-start.7
  115.7 1.2 copy-done.7
  116.9 9.0 %shard_map.55 = (f32[768,512]{1,0:T(8,128)S(1)}, f32[768,512]{1,0:T(8,128)S(1)}) custom-call(s32[2]{0:T(128)S(1)} %pad_add_fusion.1.ids, s32[16,60]{1,0:T(8,128)S(1)} %copy-done.3, f32[1,512,1536]{2,1,0:T(8,128)} %a_ref.5, f32[512,512]{1,0:T(8,128)S(1)} %copy-done.4, f32[512,512]{1,0:T(8,128)S(1)} %copy-done.7, f32[16,256,128]{2,1,0:T(8,128)} %bitcast.4.ahead_ref.top_ref), custom_call_target="tpu_custom_call" | custom-call | flops 8000000000 | bytes 2097152 | tf_op jit(solution)/shard_map/pallas_call | solution.py:291
  125.9 0.0 copy-start.2
  125.9 1.2 copy-done.2
  127.0 1.6 all-to-all-done.4.mine_ref
  128.7 0.0 collective-permute-start.2
  128.7 0.6 collective-permute-start.4
  129.3 3.5 %collective-permute-done.2 = f32[768,512]{1,0:T(8,128)S(1)} collective-permute-done((f32[768,512]{1,0:T(8,128)}, f32[768,512]{1,0:T(8,128)S(1)}, u32[]{:S(2)}, u32[]{:S(2)}) %collective-permute-start.2) | collective-permute-done | bytes 1572896 | tf_op jit(solution)/shard_map/ppermute | solution.py:381
  132.8 0.3 add.17
  133.1 0.1 fusion
  133.2 1.3 collective-permute-start.3
  134.5 0.0 collective-permute-done.4.theirs_ref
  134.6 14.8 %shard_map.56 = (f32[512,512]{1,0:T(8,128)S(1)}, f32[512,512]{1,0:T(8,128)S(1)}, f32[512,512]{1,0:T(8,128)S(1)}) custom-call(s32[2]{0:T(128)S(1)} %pad_add_fusion.1.ids, f32[16,104,128]{2,1,0:T(8,128)S(1)} %all-to-all-done.4.mine_ref, f32[16,40,128]{2,1,0:T(8,128)S(1)} %collective-permute-done.4.theirs_ref), custom_call_target="tpu_custom_call" | custom-call | flops 20000000000 | bytes 2097152 | tf_op jit(solution)/shard_map/pallas_call | solution.py:145
  149.3 5.4 %collective-permute-done.3 = f32[384,512]{1,0:T(8,128)S(1)} collective-permute-done((f32[384,512]{1,0:T(8,128)S(1)}, f32[384,512]{1,0:T(8,128)S(1)}, u32[]{:S(2)}, u32[]{:S(2)}) %collective-permute-start.3) | collective-permute-done | bytes 786464 | tf_op jit(solution)/shard_map/ppermute | solution.py:412
  154.7 0.3 pad_add_fusion.own_ref
  155.0 0.1 collective-permute-start.5
  155.2 0.8 collective-permute-start.6
  156.0 4.4 %shard_map.57.x_ref = f32[512,512]{1,0:T(8,128)S(1)} custom-call(f32[512,512]{1,0:T(8,128)S(1)} %get-tuple-element.34.xin_ref, f32[512,512]{1,0:T(8,128)S(1)} %get-tuple-element.36.s_ref, f32[512,512]{1,0:T(8,128)S(1)} %get-tuple-element.37.l_ref), custom_call_target="tpu_custom_call" | custom-call | flops 6000000000 | bytes 2097152 | tf_op jit(solution)/shard_map/pallas_call | solution.py:157
  160.4 0.0 collective-permute-done.6.theirs_ref
  160.4 0.0 collective-permute-done.5.other_ref
  160.4 4.4 %shard_map.58 = f32[512,512]{1,0:T(8,128)} custom-call(s32[2]{0:T(128)S(1)} %pad_add_fusion.1.ids, f32[512,512]{1,0:T(8,128)S(1)} %pad_add_fusion.own_ref, f32[512,512]{1,0:T(8,128)S(1)} %collective-permute-done.5.other_ref, f32[512,512]{1,0:T(8,128)S(1)} %shard_map.57.x_ref, f32[16,104,128]{2,1,0:T(8,128)S(1)} %all-to-all-done.4.mine_ref, ...), custom_call_target="tpu_custom_call" | custom-call | flops 4000000000 | bytes 2097152 | tf_op jit(solution)/shard_map/pallas_call | solution.py:327
  (4 shorter events, 0.1 us)
Async XLA Ops:
  0.7 1.9 %copy-start = (f32[1,512,1536]{2,1,0:T(8,128)S(1)}, f32[1,512,1536]{2,1,0:T(8,128)}, u32[]{:S(2)}) copy-start(f32[1,512,1536]{2,1,0:T(8,128)} %a_ref.5) | copy-start | bytes 9437188
  43.6 4.6 %copy-start.1 = (f32[1,512,512]{2,1,0:T(8,128)S(1)}, f32[1,512,512]{2,1,0:T(8,128)}, u32[]{:S(2)}) copy-start(f32[1,512,512]{2,1,0:T(8,128)} %param.4) | copy-start | bytes 3145732
  43.6 32.3 %all-to-all-start.2 = ((f32[16,2,128,128]{3,2,1,0:T(8,128)}), f32[16,2,128,128]{3,2,1,0:T(8,128)}, u32[]{:S(2)}, u32[]{:S(2)}) async-start(f32[16,2,128,128]{3,2,1,0:T(8,128)} %shard_map.51), calls=%async_computation.2 | async-start | bytes 4194304 | tf_op jit(solution)/shard_map/all_to_all | solution.py:373
  48.2 27.7 %copy-start.3 = (s32[16,60]{1,0:T(8,128)S(1)}, s32[16,60]{1,0:T(8,128)}, u32[]{:S(2)}) copy-start(s32[16,60]{1,0:T(8,128)} %cmap.3) | copy-start | bytes 11524
  48.2 20.6 %collective-permute-start = (f32[512,512]{1,0:T(8,128)S(1)}, f32[512,512]{1,0:T(8,128)S(1)}, u32[]{:S(2)}, u32[]{:S(2)}) collective-permute-start(f32[512,512]{1,0:T(8,128)S(1)} %bitcast.9), channel_id=1, source_target_pairs={{16,17},{48,49},{80,81},{112,113},{144,145},{176,177},{208,209},{2... | collective-permute-start | bytes 3145736 | tf_op jit(solution)/shard_map/ppermute | solution.py:393
  67.8 1.0 copy-start.5
  76.0 1.2 copy-start.6
  84.4 6.0 %collective-permute-start.1 = (f32[16,104,128]{2,1,0:T(8,128)S(1)}, f32[16,104,128]{2,1,0:T(8,128)S(1)}, u32[]{:S(2)}, u32[]{:S(2)}) collective-permute-start(f32[16,104,128]{2,1,0:T(8,128)S(1)} %get-tuple-element.27), channel_id=1, source_target_pairs={{0,16},{16,0},{32,48},{48,32},{64,80},{80,64},{96,112},{112,96},{1... | collective-permute-start | bytes 2555912 | tf_op jit(solution)/shard_map/ppermute | solution.py:381
  110.6 18.1 %all-to-all-start.4 = ((f32[16,104,128]{2,1,0:T(8,128)}), f32[16,104,128]{2,1,0:T(8,128)S(1)}, u32[]{:S(2)}, u32[]{:S(2)}) async-start(f32[16,104,128]{2,1,0:T(8,128)} %shard_map.54), calls=%async_computation.4 | async-start | bytes 1703936 | tf_op jit(solution)/shard_map/all_to_all | solution.py:373
  114.4 1.2 copy-start.4
  115.7 1.2 copy-start.7
  125.9 1.2 copy-start.2
  128.7 4.1 %collective-permute-start.2 = (f32[768,512]{1,0:T(8,128)}, f32[768,512]{1,0:T(8,128)S(1)}, u32[]{:S(2)}, u32[]{:S(2)}) collective-permute-start(f32[768,512]{1,0:T(8,128)} %copy-done.2), channel_id=1, source_target_pairs={{0,16},{16,0},{32,48},{48,32},{64,80},{80,64},{96,112},{112,96},{1... | collective-permute-start | bytes 4718600 | tf_op jit(solution)/shard_map/ppermute | solution.py:381
  128.7 5.8 %collective-permute-start.4 = (f32[16,40,128]{2,1,0:T(8,128)S(1)}, f32[16,40,128]{2,1,0:T(8,128)S(1)}, u32[]{:S(2)}, u32[]{:S(2)}) collective-permute-start(f32[16,40,128]{2,1,0:T(8,128)S(1)} %slice.18), channel_id=1, source_target_pairs={{0,16},{16,0},{32,48},{48,32},{64,80},{80,64},{96,112},{112,96},{1... | collective-permute-start | bytes 983048 | tf_op jit(solution)/shard_map/ppermute | solution.py:381
  133.2 21.5 %collective-permute-start.3 = (f32[384,512]{1,0:T(8,128)S(1)}, f32[384,512]{1,0:T(8,128)S(1)}, u32[]{:S(2)}, u32[]{:S(2)}) collective-permute-start(f32[384,512]{1,0:T(8,128)S(1)} %get-tuple-element.39), channel_id=1, source_target_pairs={{1,0},{2,1},{3,2},{4,3},{5,4},{6,5},{7,6},{8,7},{9,8},{10,9},{11,1... | collective-permute-start | bytes 2359304 | tf_op jit(solution)/shard_map/ppermute | solution.py:412
  155.0 5.4 %collective-permute-start.5 = (f32[512,512]{1,0:T(8,128)S(1)}, f32[512,512]{1,0:T(8,128)S(1)}, u32[]{:S(2)}, u32[]{:S(2)}) collective-permute-start(f32[512,512]{1,0:T(8,128)S(1)} %pad_add_fusion.own_ref), channel_id=1, source_target_pairs={{0,16},{16,0},{32,48},{48,32},{64,80},{80,64},{96,112},{112,96},{1... | collective-permute-start | bytes 3145736 | tf_op jit(solution)/shard_map/ppermute | solution.py:381
  155.2 5.2 %collective-permute-start.6 = (f32[16,64,128]{2,1,0:T(8,128)S(1)}, f32[16,64,128]{2,1,0:T(8,128)S(1)}, u32[]{:S(2)}, u32[]{:S(2)}) collective-permute-start(f32[16,64,128]{2,1,0:T(8,128)S(1)} %slice.19), channel_id=1, source_target_pairs={{0,16},{16,0},{32,48},{48,32},{64,80},{80,64},{96,112},{112,96},{1... | collective-permute-start | bytes 1572872 | tf_op jit(solution)/shard_map/ppermute | solution.py:381

commit v4 on v3

--- a/solution.py
+++ b/solution.py
@@ -12,7 +12,7 @@
 F32 = jnp.float32
 VMEM = pl.BlockSpec(memory_space=pltpu.VMEM)
 SMEM = pl.BlockSpec(memory_space=pltpu.SMEM)
-PARAMS = pltpu.CompilerParams(vmem_limit_bytes=48 * 1024 * 1024)
+PARAMS = pltpu.CompilerParams(vmem_limit_bytes=40 * 1024 * 1024)
 
 
 def row_of(v, j):
@@ -49,13 +49,23 @@
             v = jnp.where(hit, vr * recip, v - scale * vr)
             xv = jnp.where(hit, xr * recip, xv - scale * xr)
         out.append(xf * lax.rsqrt(diag))
+        if p < 14:
+            rest = jnp.concatenate(left[p + 2 :], axis=0)
+            group = lax.broadcasted_iota(jnp.int32, rest.shape, 1) // 8
+            rest = split(jnp.where(group == p, rest, 0.0))
+            wide = [jnp.concatenate([v, xv], axis=1), jnp.zeros((120 - 8 * p, 2 * B), F32)]
+            if p > 0:
+                wide = [jnp.zeros((8 * p, 2 * B), F32)] + wide
+            both = dot_split(rest, split(jnp.concatenate(wide, axis=0)), NN)
         if p < 15:
-            w = [row_of(v, j) for j in range(8)]
-            xw = [row_of(xv, j) for j in range(8)]
-            for q in range(p + 1, 16):
-                c = [column_of(left[q], 8 * p + j) for j in range(8)]
-                left[q] = left[q] - total([c[j] * w[j] for j in range(8)])
-                right[q] = right[q] - total([c[j] * xw[j] for j in range(8)])
+            q = p + 1
+            c = [column_of(left[q], 8 * p + j) for j in range(8)]
+            left[q] = left[q] - total([c[j] * row_of(v, j) for j in range(8)])
+            right[q] = right[q] - total([c[j] * row_of(xv, j) for j in range(8)])
+            for q in range(p + 2, 16):
+                rows = slice(8 * (q - p - 2), 8 * (q - p - 1))
+                left[q] = left[q] - both[rows, :B]
+                right[q] = right[q] - both[rows, B:]
     return jnp.concatenate(out, axis=0)
 
 
@@ -102,10 +112,13 @@
         s_ref[i * B : (i + 1) * B, j * B : (j + 1) * B] = packed[b * B : (b + 1) * B, :]
 
 
-def whole_kernel(a_ref, x_ref, s_ref, l_ref):
+def whole_kernel(a_ref, out_ref, s_ref, l_ref, x_ref, sem):
     unpack(a_ref[...].reshape(1280, B), s_ref)
     x_ref[...] = jnp.zeros_like(x_ref)
     eliminate((0, 4), s_ref, l_ref, x_ref)
+    copy = pltpu.make_async_copy(x_ref, out_ref, sem)
+    copy.start()
+    copy.wait()
 
 
 def first_kernel(ids, mine_ref, theirs_ref, x_ref, s_ref, l_ref, p_ref):
@@ -123,6 +136,11 @@
 
 
 SQUARE = jax.ShapeDtypeStruct((N, N), F32)
+FAR = pl.BlockSpec(memory_space=pltpu.HBM)
+
+
+def far(x):
+    return pltpu.with_memory_space_constraint(x, pltpu.HBM)
 
 
 def cost(gflop):
@@ -132,10 +150,10 @@
 def inverse_whole(packed):
     return pl.pallas_call(
         whole_kernel,
-        out_shape=SQUARE,
+        out_shape=pltpu.HBM((N, N), F32),
         in_specs=[VMEM],
-        out_specs=VMEM,
-        scratch_shapes=[pltpu.VMEM((N, N), F32)] * 2,
+        out_specs=FAR,
+        scratch_shapes=[pltpu.VMEM((N, N), F32)] * 3 + [pltpu.SemaphoreType.DMA],
         compiler_params=PARAMS,
         cost_estimate=cost(25),
     )(packed)
@@ -149,7 +167,7 @@
         out_specs=[VMEM] * 3,
         scratch_shapes=[pltpu.VMEM((1280, B), F32)],
         compiler_params=PARAMS,
-        cost_estimate=cost(20),
+        cost_estimate=cost(1),
     )(ids, mine, theirs)
 
 
@@ -187,26 +205,25 @@
     @pl.when(ids[1] > 0)
     def _():
         for c in range(4):
-            out_ref[:, 32 * c : 32 * c + 32, :] = a_ref[0, :, c * B : (c + 1) * B].reshape(16, 32, B)
+            out_ref[:, 32 * c : 32 * c + 32, :] = a_ref[:, c * B : (c + 1) * B].reshape(16, 32, B)
 
     @pl.when(ids[1] == 0)
     def _():
         for b, (i, j) in enumerate(LOWER):
-            p_ref[b * B : (b + 1) * B, :] = symmetric(a_ref.at[0], i, j)
+            p_ref[b * B : (b + 1) * B, :] = symmetric(a_ref, i, j)
         out_ref[:, :80, :] = p_ref[...].reshape(16, 80, B)
         out_ref[:, 80:, :] = jnp.zeros((16, 48, B), F32)
 
 
-def spread(ids, front_vals):
+def spread(ids, columns):
     return pl.pallas_call(
         spread_kernel,
-        grid=(1,),
         out_shape=jax.ShapeDtypeStruct((16, B, B), F32),
-        in_specs=[SMEM, pl.BlockSpec((1, N, N), lambda i: (0, 0, 0))],
-        out_specs=pl.BlockSpec((16, B, B), lambda i: (0, 0, 0)),
+        in_specs=[SMEM, VMEM],
+        out_specs=VMEM,
         scratch_shapes=[pltpu.VMEM((1280, B), F32)],
         compiler_params=PARAMS,
-    )(ids, front_vals)
+    )(ids, columns)
 
 
 def place_of(cmap, front, tile, i):
@@ -214,27 +231,39 @@
 
 
 def corner_kernel(
-    ids, cmap, a_ref, ahead_ref, x_ref, pp_ref, pf_ref, panel_ref, keep_ref, send_ref, b_ref, p_ref
+    ids, cmap, a_far, top_ref, x_far, pf_far, panel_ref, keep_ref, send_ref,
+    a_ref, x_ref, pf_ref, b_ref, p_ref, sems,
 ):
+    copies = [
+        pltpu.make_async_copy(x_far, x_ref, sems.at[0]),
+        pltpu.make_async_copy(a_far.at[0, :, pl.ds(0, 2 * N)], a_ref, sems.at[1]),
+        pltpu.make_async_copy(pf_far, pf_ref, sems.at[2]),
+    ]
+    for copy in copies:
+        copy.start()
     front, tile = ids[0], ids[1]
     parity = lax.rem(front, 2)
+    raw = [top_ref[:, 32 * c : 32 * c + 32, :].reshape(N, B) for c in range(4)]
+    raw = split(jnp.concatenate(raw, axis=1))
+    copies[0].wait()
     x = split(x_ref[...])
-    panel_ref[...] = dot_split(split(a_ref[0, :, :N]), x)
-    raw = [ahead_ref[:, 32 * c : 32 * c + 32, :].reshape(N, B) for c in range(4)]
-    top = split(dot_split(split(jnp.concatenate(raw, axis=1)), x))
+    top = split(dot_split(raw, x))
+    copies[1].wait()
+    panel_ref[...] = dot_split(split(a_ref[:, :N]), x)
     b_ref[...] = jnp.zeros_like(b_ref)
     for i in range(4):
         rows = slice(i * B, (i + 1) * B)
-        first = a_ref[0, rows, N:] - dot_split(split(panel_ref[rows, :]), top)
+        first = a_ref[rows, N:] - dot_split(split(panel_ref[rows, :]), top)
 
         @pl.when(tile > 0)
         def _():
             b_ref[at(place_of(cmap, front, tile, i)), :] = first
 
-    @pl.when((tile == 1) & (parity == 1))
+    copies[2].wait()
+
+    @pl.when((tile <= 1) & (parity == 1))
     def _():
-        b_ref[:N, :] += pp_ref[...]
-        b_ref[N:, :] += pf_ref[...]
+        b_ref[pl.ds(pl.multiple_of(tile * N, N), N), :] += pf_ref[...]
 
     for b, (i, j) in enumerate(LOWER):
         p_ref[b * B : (b + 1) * B, :] = symmetric(b_ref, i, j)
@@ -246,25 +275,41 @@
             ref[:, 40 + 16 * c : 56 + 16 * c, :] = b_ref[rows, c * B : (c + 1) * B].reshape(16, 16, B)
 
 
-def corner(ids, cmap, front_vals, ahead, x, pp, pf):
-    full = pl.BlockSpec((N, N), lambda i: (0, 0))
-    piece = pl.BlockSpec((16, 104, B), lambda i: (0, 0, 0))
-    lead = pl.BlockSpec((16, B, B), lambda i: (0, 0, 0))
+def corner(ids, cmap, front_vals, tops, x, pf):
     return pl.pallas_call(
         corner_kernel,
-        grid=(1,),
         out_shape=[SQUARE] + [jax.ShapeDtypeStruct((16, 104, B), F32)] * 2,
-        in_specs=[SMEM, SMEM, pl.BlockSpec((1, N, 2 * N), lambda i: (0, 0, 0)), lead, full, full, full],
-        out_specs=[full, piece, piece],
-        scratch_shapes=[pltpu.VMEM((2 * N, N), F32), pltpu.VMEM((1280, B), F32)],
+        in_specs=[SMEM, SMEM, FAR, VMEM, FAR, FAR],
+        out_specs=[VMEM] * 3,
+        scratch_shapes=[
+            pltpu.VMEM((N, 2 * N), F32),
+            pltpu.VMEM((N, N), F32),
+            pltpu.VMEM((N, N), F32),
+            pltpu.VMEM((2 * N, N), F32),
+            pltpu.VMEM((1280, B), F32),
+            pltpu.SemaphoreType.DMA((3,)),
+        ],
         compiler_params=PARAMS,
         cost_estimate=cost(3),
-    )(ids, cmap, front_vals, ahead, x, pp, pf)
-
-
-def schur_kernel(ids, cmap, a_ref, panel_ref, x_ref, top_ref, keep_ref, send_ref):
+    )(ids, cmap, far(front_vals), tops, far(x), far(pf))
+
+
+def schur_kernel(
+    ids, cmap, a_far, panel_far, x_far, top_ref, keep_far, out_far,
+    a_ref, panel_ref, x_ref, keep_ref, send_ref, sems,
+):
+    copies = [
+        pltpu.make_async_copy(x_far, x_ref, sems.at[0]),
+        pltpu.make_async_copy(panel_far, panel_ref, sems.at[1]),
+        pltpu.make_async_copy(a_far.at[0, :, pl.ds(N, 2 * N)], a_ref, sems.at[2]),
+    ]
+    for copy in copies:
+        copy.start()
     front, tile = ids[0], ids[1]
     parity = lax.rem(front, 2)
+    keep_ref[...] = jnp.zeros_like(keep_ref)
+    send_ref[...] = jnp.zeros_like(send_ref)
+    copies[0].wait()
     x = split(x_ref[...])
     tops = []
     for h in range(2):
@@ -272,30 +317,80 @@
             top_ref[:, h * B + 32 * c : h * B + 32 * c + 32, :].reshape(N, B) for c in range(4)
         ]
         tops.append(split(dot_split(split(jnp.concatenate(raw, axis=1)), x)))
-    keep_ref[...] = jnp.zeros_like(keep_ref)
-    send_ref[...] = jnp.zeros_like(send_ref)
+    copies[1].wait()
+    copies[2].wait()
     for i in range(4):
         rows = slice(i * B, (i + 1) * B)
         panel = split(panel_ref[rows, :])
         place = place_of(cmap, front, tile, i)
-        first = a_ref[0, rows, N : 2 * N] - dot_split(panel, tops[0])
-        second = a_ref[0, rows, 2 * N :] - dot_split(panel, tops[1])
-
-        @pl.when(tile > 0)
+        first = a_ref[rows, :N] - dot_split(panel, tops[0])
+        second = a_ref[rows, N:] - dot_split(panel, tops[1])
+
+        @pl.when((tile > 0) & (parity == 1))
         def _():
-            keep_ref[at(place - 1), :] = jnp.where(parity == 1, first, second)
-            send_ref[at(place - 1), :] = jnp.where(parity == 1, second, first)
+            keep_ref[at(place - 1), :] = first
+            send_ref[at(place - 1), :] = second
+
+        @pl.when((tile > 0) & (parity == 0))
+        def _():
+            keep_ref[at(place - 1), :] = second
+            send_ref[at(place - 1), :] = first
+
+    copies = [
+        pltpu.make_async_copy(send_ref, out_far, sems.at[3]),
+        pltpu.make_async_copy(keep_ref, keep_far, sems.at[4]),
+    ]
+    for copy in copies:
+        copy.start()
+    for copy in copies:
+        copy.wait()
 
 
 def schur(ids, cmap, front_vals, panel, x, tops):
     return pl.pallas_call(
         schur_kernel,
-        out_shape=[jax.ShapeDtypeStruct((6 * B, N), F32)] * 2,
-        in_specs=[SMEM, SMEM, VMEM, VMEM, VMEM, VMEM],
-        out_specs=[VMEM] * 2,
+        out_shape=[pltpu.HBM((6 * B, N), F32)] * 2,
+        in_specs=[SMEM, SMEM, FAR, FAR, FAR, VMEM],
+        out_specs=[FAR, FAR],
+        scratch_shapes=[
+            pltpu.VMEM((N, 2 * N), F32),
+            pltpu.VMEM((N, N), F32),
+            pltpu.VMEM((N, N), F32),
+            pltpu.VMEM((6 * B, N), F32),
+            pltpu.VMEM((6 * B, N), F32),
+            pltpu.SemaphoreType.DMA((5,)),
+        ],
         compiler_params=PARAMS,
         cost_estimate=cost(8),
-    )(ids, cmap, front_vals, panel, x, tops)
+    )(ids, cmap, far(front_vals), far(panel), far(x), tops)
+
+
+def own_kernel(keep_far, recv_far, lower_ref, upper_ref, buf, sems):
+    copies = []
+    for h in range(2):
+        rows = pl.ds(h * 3 * B, 3 * B)
+        for n, ref in enumerate((keep_far, recv_far)):
+            copies.append(
+                pltpu.make_async_copy(ref.at[rows], buf.at[2 * h + n], sems.at[2 * h + n])
+            )
+    for copy in copies:
+        copy.start()
+    for h, ref in enumerate((lower_ref, upper_ref)):
+        copies[2 * h].wait()
+        copies[2 * h + 1].wait()
+        ref[...] = buf[2 * h] + buf[2 * h + 1]
+
+
+def own_halves(keep, recv):
+    return pl.pallas_call(
+        own_kernel,
+        out_shape=[jax.ShapeDtypeStruct((3 * B, N), F32)] * 2,
+        in_specs=[FAR, FAR],
+        out_specs=[VMEM, VMEM],
+        scratch_shapes=[pltpu.VMEM((4, 3 * B, N), F32), pltpu.SemaphoreType.DMA((4,))],
+        compiler_params=PARAMS,
+        cost_estimate=cost(1),
+    )(far(keep), far(recv))
 
 
 def parent_kernel(ids, own_ref, other_ref, x_ref, mine_ref, theirs_ref, out_ref):
@@ -347,7 +442,7 @@
 
 
 def fan_corner_kernel(parts_ref, out_ref, piece_ref, sems):
-    piece_ref[:40, :] = parts_ref[1, :40, :]
+    piece_ref[:40, :] = parts_ref[0, :40, :] + parts_ref[1, :40, :]
     piece_ref[40:, :] = parts_ref[1, 40:, :] + parts_ref[2, 40:, :]
     copies = []
     for t in range(16):
@@ -387,32 +482,28 @@
     ids = jnp.stack([front, tile]).astype(jnp.int32)
     parent_vals = parent_front[0]
 
-    pieces = exchanged(spread(ids, child_front))
+    pieces = exchanged(spread(ids, child_front[0, :, :N]))
     pivot = gathered(pieces[0, :80])
-    parents, pieces, pivot = lax.optimization_barrier((parent_vals, pieces, pivot))
-    pivots_ahead = lax.ppermute(
-        parents, ("front", "tile"), [(f * 16, f * 16 + 1) for f in range(1, 16, 2)]
-    )
+    pieces, pivot = lax.optimization_barrier((pieces, pivot))
     fan = fanned(fan_tops_kernel, pieces, (16, 2, B, B), [])
     fan, pivot = lax.optimization_barrier((fan, pivot))
     tops = exchanged(fan).reshape(16, 2 * B, B)
     child_x = inverse_whole(pivot)
-    child_panel, keep, send = corner(
-        ids, child_map, child_front, tops, child_x, pivots_ahead, parent_vals
-    )
-    parts = exchanged(keep + sibling(send))
+    child_panel, keep, send = corner(ids, child_map, child_front, tops, child_x, parent_vals)
+    summed, panel_later = lax.optimization_barrier((keep + sibling(send), child_panel))
+    parts = exchanged(summed)
+    keep, send = schur(ids, child_map, child_front, panel_later, child_x, tops)
+    send, parts = lax.optimization_barrier((send, parts))
     fan = fanned(fan_corner_kernel, parts, (16, 104, B), [pltpu.VMEM((104, B), F32)])
-    fan, panel_later = lax.optimization_barrier((fan, child_panel))
     mine = exchanged(fan)
-    keep, send = schur(ids, child_map, child_front, panel_later, child_x, tops)
-    send, mine = lax.optimization_barrier((send, mine))
+    lower, upper = own_halves(keep, sibling(send))
+    mine, lower = lax.optimization_barrier((mine, lower))
     theirs = sibling(mine[:, :40])
-    own = keep + sibling(send)
     top_theirs = sibling(mine[:, 40:])
-    arrived = lax.ppermute(own[: 3 * B], "tile", [(i, i - 1) for i in range(1, 16)])
+    arrived = lax.ppermute(lower, "tile", [(i, i - 1) for i in range(1, 16)])
     x, s, l = inverse_first(ids, mine, theirs)
     assembled = (
-        parent_vals + jnp.pad(own[3 * B :], ((0, B), (0, 0))) + jnp.pad(arrived, ((B, 0), (0, 0)))
+        parent_vals + jnp.pad(upper, ((0, B), (0, 0))) + jnp.pad(arrived, ((B, 0), (0, 0)))
     )
     assembled, _ = lax.optimization_barrier((assembled, x))
     other = sibling(assembled)

time: 166 us -> 157 us (0.946)
  waiting for transfers between devices: 19.7 us -> 39.7 us
  blocking collectives: 57.8 us -> 38.7 us
  local copies, waits for them, and re-layouts: 7.93 us -> 1.42 us
  starting transfers between devices: 15.9 us -> 13.9 us
    all_to_all x2 -> x3, waiting for transfers between devices: 8.81 us -> 30.8 us  [exchanged(): return lax.all_to_all(x, 'tile', 0, 0)]
    all_to_all x3 -> x2, blocking collectives: 57.8 us -> 38.7 us  [exchanged(): return lax.all_to_all(x, 'tile', 0, 0)]
    unnamed x16 -> x4, local copies, waits for them, and re-layouts: 7.69 us -> 0.01 us
    ppermute x5, starting transfers between devices: 5.48 us -> 0.86 us  [sibling(): return lax.ppermute(x, 'front', [(i, i ^ 1) for i in range(16)])]
    all_to_all x2 -> x3, starting transfers between devices: 8.41 us -> 11.6 us  [exchanged(): return lax.all_to_all(x, 'tile', 0, 0)]
    pallas_call x1, Pallas kernels: 14.8 us -> 12.7 us  [inverse_first(): pl.pallas_call(first_kernel, out_shape=[SQUARE] * 3, in_specs=[SMEM, VMEM...]
    pallas_call x4 -> x5, Pallas kernels: 35.8 us -> 37.3 us  [the longest x1 17.1 us: inverse_whole(): pl.pallas_call(whole_kernel, out_shape=pltpu.HBM((N, N), F32), in_specs=[...]
    ppermute x2 -> x1, waiting for transfers between devices: 5.4 us -> 4.97 us  [local(): arrived = lax.ppermute(lower, 'tile', [(i, i - 1) for i in range(1, 16)])]
  transfers between devices with their start and end apart: 9 -> 9, of which waited for: 5 -> 6; matrix products, arithmetic and copies ran while one was open for 0% -> 0% of each run, Pallas kernels for 29% -> 30%
where the time goes in v4:
time: 157 us; the launch traced here: 156 us
  Pallas kernels  60.5 us (39%)
  waiting for transfers between devices  39.7 us (25%)
  blocking collectives  38.7 us (25%)
  starting transfers between devices  13.9 us (9%)
    all_to_all x2, blocking collectives, exchanged(): return lax.all_to_all(x, 'tile', 0, 0)  38.7 us
    all_to_all x3, waiting for transfers between devices, exchanged(): return lax.all_to_all(x, 'tile', 0, 0)  30.8 us
    pallas_call x1, Pallas kernels, inverse_whole(): pl.pallas_call(whole_kernel, out_shape=pltpu.HBM((N, N), F32), in_specs=[...  17.1 us
    pallas_call x1, Pallas kernels, inverse_first(): pl.pallas_call(first_kernel, out_shape=[SQUARE] * 3, in_specs=[SMEM, VMEM...  12.7 us
    all_to_all x3, starting transfers between devices, exchanged(): return lax.all_to_all(x, 'tile', 0, 0)  11.6 us
    pallas_call x1, Pallas kernels, schur(): pl.pallas_call(schur_kernel, out_shape=[pltpu.HBM((6 * B, N), F32)] * 2,...  10.1 us
    pallas_call x1, Pallas kernels, corner(): pl.pallas_call(corner_kernel, out_shape=[SQUARE] + [jax.ShapeDtypeStruct(...  7.39 us
    ppermute x1, waiting for transfers between devices, local(): arrived = lax.ppermute(lower, 'tile', [(i, i - 1) for i in range(1, 16)])  4.97 us
  transfers between devices with their start and end apart: 9, of which 6 were waited for; matrix products, arithmetic and copies ran while one was open for 0% of the time, Pallas kernels for 30%

profile of v4, /device:TPU:32, one launch (start us, length us, event | category | flops | bytes accessed | tf_op | source)
XLA Modules:
  0.0 156.5 jit_solution(4047929420681173385)
XLA Ops:
  0.6 1.3 slice_bitcast_fusion.a_ref
  1.9 0.1 pad_add_fusion.1.ids
  2.0 0.8 shard_map.50
  2.8 23.5 %all_to_all.25.parts_ref = f32[16,128,128]{2,1,0:T(8,128)S(1)} all-to-all(f32[16,128,128]{2,1,0:T(8,128)S(1)} %shard_map.50), channel_id=1, replica_groups=mesh['front'=16,'tile'=16] {'tile'}, dimensions={0} | all-to-all | bytes 2097152 | tf_op jit(solution)/shard_map/all_to_all | solution.py:468
  26.4 15.2 %all_to_all.26.a_ref = f32[16,80,128]{2,1,0:T(8,128)S(1)} all-to-all(f32[16,80,128]{2,1,0:T(8,128)S(1)} %broadcast_in_dim.14), channel_id=1, replica_groups=mesh['front'=16,'tile'=16] {'tile'}, dimensions={0} | all-to-all | bytes 1310720 | tf_op jit(solution)/shard_map/all_to_all | solution.py:468
  41.6 1.5 shard_map.51
  43.1 3.7 %all-to-all-start.2 = ((f32[16,2,128,128]{3,2,1,0:T(8,128)}), f32[16,2,128,128]{3,2,1,0:T(8,128)S(1)}, u32[]{:S(2)}, u32[]{:S(2)}) async-start(f32[16,2,128,128]{3,2,1,0:T(8,128)} %shard_map.51), calls=%async_computation.2 | async-start | bytes 4194304 | tf_op jit(solution)/shard_map/all_to_all | solution.py:468
  46.8 0.0 copy-start
  46.8 17.1 %shard_map.52.x_far = f32[512,512]{1,0:T(8,128)} custom-call(f32[16,80,128]{2,1,0:T(8,128)S(1)} %all_to_all.26.a_ref), custom_call_target="tpu_custom_call" | custom-call | flops 24999999488 | bytes 2097152 | tf_op jit(solution)/shard_map/pallas_call | solution.py:151
  63.9 10.7 %all-to-all-done.2 = f32[16,2,128,128]{3,2,1,0:T(8,128)S(1)} async-done(((f32[16,2,128,128]{3,2,1,0:T(8,128)}), f32[16,2,128,128]{3,2,1,0:T(8,128)S(1)}, u32[]{:S(2)}, u32[]{:S(2)}) %all-to-all-start.2) | async-done | bytes 2097184 | tf_op jit(solution)/shard_map/all_to_all | solution.py:468
  74.6 0.0 copy-done
  74.6 7.4 %shard_map.53 = (f32[512,512]{1,0:T(8,128)}, f32[16,104,128]{2,1,0:T(8,128)S(1)}, f32[16,104,128]{2,1,0:T(8,128)S(1)}) custom-call(s32[2]{0:T(128)S(1)} %pad_add_fusion.1.ids, s32[16,60]{1,0:T(8,128)S(1)} %copy-done, f32[1,512,1536]{2,1,0:T(8,128)} %a_far.3, f32[16,256,128]{2,1,0:T(8,128)S(1)} %bitcast.11, f32[512,512]{1,0:T(8,128)} %shard_map.52.x_far, ...), custom_call_target="tpu_custom_call" | custom-call | flops 3000000000 | bytes 2097152 | tf_op jit(solution)/shard_map/pallas_call | solution.py:279
  82.0 0.1 collective-permute-start
  82.1 2.4 %collective-permute-done = f32[16,104,128]{2,1,0:T(8,128)S(1)} collective-permute-done((f32[16,104,128]{2,1,0:T(8,128)S(1)}, f32[16,104,128]{2,1,0:T(8,128)S(1)}, u32[]{:S(2)}, u32[]{:S(2)}) %collective-permute-start) | collective-permute-done | bytes 852000 | tf_op jit(solution)/shard_map/ppermute | solution.py:476
  84.5 1.0 add.13
  85.5 4.2 %all-to-all-start.3 = ((f32[16,104,128]{2,1,0:T(8,128)}), f32[16,104,128]{2,1,0:T(8,128)S(1)}, u32[]{:S(2)}, u32[]{:S(2)}) async-start(f32[16,104,128]{2,1,0:T(8,128)} %add.13), calls=%async_computation.3 | async-start | bytes 1703936 | tf_op jit(solution)/shard_map/all_to_all | solution.py:468
  89.7 10.1 %shard_map.54 = (f32[768,512]{1,0:T(8,128)}, f32[768,512]{1,0:T(8,128)}) custom-call(s32[2]{0:T(128)S(1)} %pad_add_fusion.1.ids, s32[16,60]{1,0:T(8,128)S(1)} %copy-done, f32[1,512,1536]{2,1,0:T(8,128)} %a_far.3, f32[512,512]{1,0:T(8,128)} %get-tuple-element.30.panel_far, f32[512,512]{1,0:T(8,128)} %shard_map.52.x_far, f32[16,256,128]{2,1,0:T(8,128)S(1)} %bitcast.12), custom_call_target="tpu_custom_call" | custom-call | flops 8000000000 | bytes 2097152 | tf_op jit(solution)/shard_map/pallas_call | solution.py:350
  99.8 5.6 %all-to-all-done.3.parts_ref = f32[16,104,128]{2,1,0:T(8,128)S(1)} async-done(((f32[16,104,128]{2,1,0:T(8,128)}), f32[16,104,128]{2,1,0:T(8,128)S(1)}, u32[]{:S(2)}, u32[]{:S(2)}) %all-to-all-start.3) | async-done | bytes 852000 | tf_op jit(solution)/shard_map/all_to_all | solution.py:468
  105.4 0.0 collective-permute-start.1
  105.4 1.0 shard_map.56
  106.5 3.6 %all-to-all-start.4 = ((f32[16,104,128]{2,1,0:T(8,128)}), f32[16,104,128]{2,1,0:T(8,128)S(1)}, u32[]{:S(2)}, u32[]{:S(2)}) async-start(f32[16,104,128]{2,1,0:T(8,128)} %shard_map.56), calls=%async_computation.4 | async-start | bytes 1703936 | tf_op jit(solution)/shard_map/all_to_all | solution.py:468
  110.1 0.0 collective-permute-done.1.recv_far
  110.1 2.0 %shard_map.55 = (f32[384,512]{1,0:T(8,128)S(1)}, f32[384,512]{1,0:T(8,128)S(1)}) custom-call(f32[768,512]{1,0:T(8,128)} %get-tuple-element.31.keep_far, f32[768,512]{1,0:T(8,128)} %collective-permute-done.1.recv_far), custom_call_target="tpu_custom_call" | custom-call | flops 1000000000 | bytes 2097152 | tf_op jit(solution)/shard_map/pallas_call | solution.py:385
  112.1 14.5 %all-to-all-done.4.mine_ref = f32[16,104,128]{2,1,0:T(8,128)S(1)} async-done(((f32[16,104,128]{2,1,0:T(8,128)}), f32[16,104,128]{2,1,0:T(8,128)S(1)}, u32[]{:S(2)}, u32[]{:S(2)}) %all-to-all-start.4) | async-done | bytes 852000 | tf_op jit(solution)/shard_map/all_to_all | solution.py:468
  126.6 0.0 copy-start.1
  126.6 1.4 collective-permute-start.2
  128.0 0.1 collective-permute-start.3
  128.1 1.6 %collective-permute-done.3.theirs_ref = f32[16,40,128]{2,1,0:T(8,128)S(1)} collective-permute-done((f32[16,40,128]{2,1,0:T(8,128)S(1)}, f32[16,40,128]{2,1,0:T(8,128)S(1)}, u32[]{:S(2)}, u32[]{:S(2)}) %collective-permute-start.3) | collective-permute-done | bytes 327712 | tf_op jit(solution)/shard_map/ppermute | solution.py:476
  129.7 12.7 %shard_map.57 = (f32[512,512]{1,0:T(8,128)S(1)}, f32[512,512]{1,0:T(8,128)S(1)}, f32[512,512]{1,0:T(8,128)S(1)}) custom-call(s32[2]{0:T(128)S(1)} %pad_add_fusion.1.ids, f32[16,104,128]{2,1,0:T(8,128)S(1)} %all-to-all-done.4.mine_ref, f32[16,40,128]{2,1,0:T(8,128)S(1)} %collective-permute-done.3.theirs_ref), custom_call_target="tpu_custom_call" | custom-call | flops 1000000000 | bytes 2097152 | tf_op jit(solution)/shard_map/pallas_call | solution.py:163
  142.5 5.0 %collective-permute-done.2 = f32[384,512]{1,0:T(8,128)S(1)} collective-permute-done((f32[384,512]{1,0:T(8,128)S(1)}, f32[384,512]{1,0:T(8,128)S(1)}, u32[]{:S(2)}, u32[]{:S(2)}) %collective-permute-start.2) | collective-permute-done | bytes 786464 | tf_op jit(solution)/shard_map/ppermute | solution.py:503
  147.5 0.0 copy-done.1
  147.5 0.3 pad_add_fusion.own_ref
  147.7 0.1 collective-permute-start.4
  147.9 0.6 collective-permute-start.5
  148.5 3.6 %shard_map.58.x_ref = f32[512,512]{1,0:T(8,128)S(1)} custom-call(f32[512,512]{1,0:T(8,128)S(1)} %get-tuple-element.40.xin_ref, f32[512,512]{1,0:T(8,128)S(1)} %get-tuple-element.42.s_ref, f32[512,512]{1,0:T(8,128)S(1)} %get-tuple-element.43.l_ref), custom_call_target="tpu_custom_call" | custom-call | flops 6000000000 | bytes 2097152 | tf_op jit(solution)/shard_map/pallas_call | solution.py:175
  152.0 0.0 collective-permute-done.5.theirs_ref
  152.1 0.0 collective-permute-done.4.other_ref
  152.1 4.4 %shard_map.59 = f32[512,512]{1,0:T(8,128)} custom-call(s32[2]{0:T(128)S(1)} %pad_add_fusion.1.ids, f32[512,512]{1,0:T(8,128)S(1)} %pad_add_fusion.own_ref, f32[512,512]{1,0:T(8,128)S(1)} %collective-permute-done.4.other_ref, f32[512,512]{1,0:T(8,128)S(1)} %shard_map.58.x_ref, f32[16,104,128]{2,1,0:T(8,128)S(1)} %all-to-all-done.4.mine_ref, ...), custom_call_target="tpu_custom_call" | custom-call | flops 4000000000 | bytes 2097152 | tf_op jit(solution)/shard_map/pallas_call | solution.py:422
  (4 shorter events, 0.1 us)
Async XLA Ops:
  43.1 31.6 %all-to-all-start.2 = ((f32[16,2,128,128]{3,2,1,0:T(8,128)}), f32[16,2,128,128]{3,2,1,0:T(8,128)S(1)}, u32[]{:S(2)}, u32[]{:S(2)}) async-start(f32[16,2,128,128]{3,2,1,0:T(8,128)} %shard_map.51), calls=%async_computation.2 | async-start | bytes 4194304 | tf_op jit(solution)/shard_map/all_to_all | solution.py:468
  46.8 27.8 %copy-start = (s32[16,60]{1,0:T(8,128)S(1)}, s32[16,60]{1,0:T(8,128)}, u32[]{:S(2)}) copy-start(s32[16,60]{1,0:T(8,128)} %cmap.3) | copy-start | bytes 11524
  82.0 2.5 %collective-permute-start = (f32[16,104,128]{2,1,0:T(8,128)S(1)}, f32[16,104,128]{2,1,0:T(8,128)S(1)}, u32[]{:S(2)}, u32[]{:S(2)}) collective-permute-start(f32[16,104,128]{2,1,0:T(8,128)S(1)} %get-tuple-element.29), channel_id=1, source_target_pairs={{0,16},{16,0},{32,48},{48,32},{64,80},{80,64},{96,112},{112,96},{1... | collective-permute-start | bytes 2555912 | tf_op jit(solution)/shard_map/ppermute | solution.py:476
  85.5 19.9 %all-to-all-start.3 = ((f32[16,104,128]{2,1,0:T(8,128)}), f32[16,104,128]{2,1,0:T(8,128)S(1)}, u32[]{:S(2)}, u32[]{:S(2)}) async-start(f32[16,104,128]{2,1,0:T(8,128)} %add.13), calls=%async_computation.3 | async-start | bytes 1703936 | tf_op jit(solution)/shard_map/all_to_all | solution.py:468
  105.4 4.7 %collective-permute-start.1 = (f32[768,512]{1,0:T(8,128)}, f32[768,512]{1,0:T(8,128)}, u32[]{:S(2)}, u32[]{:S(2)}) collective-permute-start(f32[768,512]{1,0:T(8,128)} %get-tuple-element.34), channel_id=1, source_target_pairs={{0,16},{16,0},{32,48},{48,32},{64,80},{80,64},{96,112},{112,96},{1... | collective-permute-start | bytes 4718600 | tf_op jit(solution)/shard_map/ppermute | solution.py:476
  106.5 20.1 %all-to-all-start.4 = ((f32[16,104,128]{2,1,0:T(8,128)}), f32[16,104,128]{2,1,0:T(8,128)S(1)}, u32[]{:S(2)}, u32[]{:S(2)}) async-start(f32[16,104,128]{2,1,0:T(8,128)} %shard_map.56), calls=%async_computation.4 | async-start | bytes 1703936 | tf_op jit(solution)/shard_map/all_to_all | solution.py:468
  126.6 20.9 %copy-start.1 = (f32[1,512,512]{2,1,0:T(8,128)S(1)}, f32[1,512,512]{2,1,0:T(8,128)}, u32[]{:S(2)}) copy-start(f32[1,512,512]{2,1,0:T(8,128)} %param.4) | copy-start | bytes 3145732
  126.6 20.9 %collective-permute-start.2 = (f32[384,512]{1,0:T(8,128)S(1)}, f32[384,512]{1,0:T(8,128)S(1)}, u32[]{:S(2)}, u32[]{:S(2)}) collective-permute-start(f32[384,512]{1,0:T(8,128)S(1)} %get-tuple-element.38), channel_id=1, source_target_pairs={{1,0},{2,1},{3,2},{4,3},{5,4},{6,5},{7,6},{8,7},{9,8},{10,9},{11,1... | collective-permute-start | bytes 2359304 | tf_op jit(solution)/shard_map/ppermute | solution.py:503
  128.0 1.7 %collective-permute-start.3 = (f32[16,40,128]{2,1,0:T(8,128)S(1)}, f32[16,40,128]{2,1,0:T(8,128)S(1)}, u32[]{:S(2)}, u32[]{:S(2)}) collective-permute-start(f32[16,40,128]{2,1,0:T(8,128)S(1)} %slice.14), channel_id=1, source_target_pairs={{0,16},{16,0},{32,48},{48,32},{64,80},{80,64},{96,112},{112,96},{1... | collective-permute-start | bytes 983048 | tf_op jit(solution)/shard_map/ppermute | solution.py:476
  147.7 4.3 %collective-permute-start.4 = (f32[512,512]{1,0:T(8,128)S(1)}, f32[512,512]{1,0:T(8,128)S(1)}, u32[]{:S(2)}, u32[]{:S(2)}) collective-permute-start(f32[512,512]{1,0:T(8,128)S(1)} %pad_add_fusion.own_ref), channel_id=1, source_target_pairs={{0,16},{16,0},{32,48},{48,32},{64,80},{80,64},{96,112},{112,96},{1... | collective-permute-start | bytes 3145736 | tf_op jit(solution)/shard_map/ppermute | solution.py:476
  147.9 4.2 %collective-permute-start.5 = (f32[16,64,128]{2,1,0:T(8,128)S(1)}, f32[16,64,128]{2,1,0:T(8,128)S(1)}, u32[]{:S(2)}, u32[]{:S(2)}) collective-permute-start(f32[16,64,128]{2,1,0:T(8,128)S(1)} %slice.15), channel_id=1, source_target_pairs={{0,16},{16,0},{32,48},{48,32},{64,80},{80,64},{96,112},{112,96},{1... | collective-permute-start | bytes 1572872 | tf_op jit(solution)/shard_map/ppermute | solution.py:476

commit v5 on v4

--- a/solution.py
+++ b/solution.py
@@ -201,7 +201,11 @@
     )
 
 
-def spread_kernel(ids, a_ref, out_ref, p_ref):
+def spread_kernel(ids, a_far, out_ref, a_ref, p_ref, sem):
+    copy = pltpu.make_async_copy(a_far.at[0, :, pl.ds(0, N)], a_ref, sem)
+    copy.start()
+    copy.wait()
+
     @pl.when(ids[1] > 0)
     def _():
         for c in range(4):
@@ -215,29 +219,61 @@
         out_ref[:, 80:, :] = jnp.zeros((16, 48, B), F32)
 
 
-def spread(ids, columns):
+def spread(ids, front_vals):
     return pl.pallas_call(
         spread_kernel,
         out_shape=jax.ShapeDtypeStruct((16, B, B), F32),
-        in_specs=[SMEM, VMEM],
+        in_specs=[SMEM, FAR],
         out_specs=VMEM,
-        scratch_shapes=[pltpu.VMEM((1280, B), F32)],
-        compiler_params=PARAMS,
-    )(ids, columns)
+        scratch_shapes=[
+            pltpu.VMEM((N, N), F32),
+            pltpu.VMEM((1280, B), F32),
+            pltpu.SemaphoreType.DMA,
+        ],
+        compiler_params=PARAMS,
+    )(ids, far(front_vals))
 
 
 def place_of(cmap, front, tile, i):
     return cmap[front, jnp.maximum(4 * tile - 4 + i, 0)] - 4 * (tile - 1)
 
 
+def panel_kernel(a_far, x_far, out_far, a_ref, x_ref, panel_ref, sems):
+    copies = [
+        pltpu.make_async_copy(x_far, x_ref, sems.at[0]),
+        pltpu.make_async_copy(a_far.at[0, :, pl.ds(0, N)], a_ref, sems.at[1]),
+    ]
+    for copy in copies:
+        copy.start()
+    for copy in copies:
+        copy.wait()
+    panel_ref[...] = dot_split(split(a_ref[...]), split(x_ref[...]))
+    copy = pltpu.make_async_copy(panel_ref, out_far, sems.at[2])
+    copy.start()
+    copy.wait()
+
+
+def panel_of(front_vals, x):
+    return pl.pallas_call(
+        panel_kernel,
+        out_shape=pltpu.HBM((N, N), F32),
+        in_specs=[FAR, FAR],
+        out_specs=FAR,
+        scratch_shapes=[pltpu.VMEM((N, N), F32)] * 3 + [pltpu.SemaphoreType.DMA((3,))],
+        compiler_params=PARAMS,
+        cost_estimate=cost(1),
+    )(far(front_vals), far(x))
+
+
 def corner_kernel(
-    ids, cmap, a_far, top_ref, x_far, pf_far, panel_ref, keep_ref, send_ref,
-    a_ref, x_ref, pf_ref, b_ref, p_ref, sems,
+    ids, cmap, a_far, panel_far, top_ref, x_far, pf_far, keep_ref, send_ref,
+    a_ref, panel_ref, x_ref, pf_ref, b_ref, p_ref, sems,
 ):
     copies = [
         pltpu.make_async_copy(x_far, x_ref, sems.at[0]),
-        pltpu.make_async_copy(a_far.at[0, :, pl.ds(0, 2 * N)], a_ref, sems.at[1]),
-        pltpu.make_async_copy(pf_far, pf_ref, sems.at[2]),
+        pltpu.make_async_copy(panel_far, panel_ref, sems.at[1]),
+        pltpu.make_async_copy(a_far.at[0, :, pl.ds(N, N)], a_ref, sems.at[2]),
+        pltpu.make_async_copy(pf_far, pf_ref, sems.at[3]),
     ]
     for copy in copies:
         copy.start()
@@ -246,20 +282,19 @@
     raw = [top_ref[:, 32 * c : 32 * c + 32, :].reshape(N, B) for c in range(4)]
     raw = split(jnp.concatenate(raw, axis=1))
     copies[0].wait()
-    x = split(x_ref[...])
-    top = split(dot_split(raw, x))
+    top = split(dot_split(raw, split(x_ref[...])))
     copies[1].wait()
-    panel_ref[...] = dot_split(split(a_ref[:, :N]), x)
+    copies[2].wait()
     b_ref[...] = jnp.zeros_like(b_ref)
     for i in range(4):
         rows = slice(i * B, (i + 1) * B)
-        first = a_ref[rows, N:] - dot_split(split(panel_ref[rows, :]), top)
+        first = a_ref[rows, :] - dot_split(split(panel_ref[rows, :]), top)
 
         @pl.when(tile > 0)
         def _():
             b_ref[at(place_of(cmap, front, tile, i)), :] = first
 
-    copies[2].wait()
+    copies[3].wait()
 
     @pl.when((tile <= 1) & (parity == 1))
     def _():
@@ -275,23 +310,21 @@
             ref[:, 40 + 16 * c : 56 + 16 * c, :] = b_ref[rows, c * B : (c + 1) * B].reshape(16, 16, B)
 
 
-def corner(ids, cmap, front_vals, tops, x, pf):
+def corner(ids, cmap, front_vals, panel, tops, x, pf):
     return pl.pallas_call(
         corner_kernel,
-        out_shape=[SQUARE] + [jax.ShapeDtypeStruct((16, 104, B), F32)] * 2,
-        in_specs=[SMEM, SMEM, FAR, VMEM, FAR, FAR],
-        out_specs=[VMEM] * 3,
-        scratch_shapes=[
-            pltpu.VMEM((N, 2 * N), F32),
-            pltpu.VMEM((N, N), F32),
-            pltpu.VMEM((N, N), F32),
+        out_shape=[jax.ShapeDtypeStruct((16, 104, B), F32)] * 2,
+        in_specs=[SMEM, SMEM, FAR, FAR, VMEM, FAR, FAR],
+        out_specs=[VMEM] * 2,
+        scratch_shapes=[pltpu.VMEM((N, N), F32)] * 4
+        + [
             pltpu.VMEM((2 * N, N), F32),
             pltpu.VMEM((1280, B), F32),
-            pltpu.SemaphoreType.DMA((3,)),
+            pltpu.SemaphoreType.DMA((4,)),
         ],
         compiler_params=PARAMS,
         cost_estimate=cost(3),
-    )(ids, cmap, far(front_vals), tops, far(x), far(pf))
+    )(ids, cmap, far(front_vals), far(panel), tops, far(x), far(pf))
 
 
 def schur_kernel(
@@ -482,14 +515,15 @@
     ids = jnp.stack([front, tile]).astype(jnp.int32)
     parent_vals = parent_front[0]
 
-    pieces = exchanged(spread(ids, child_front[0, :, :N]))
+    pieces = exchanged(spread(ids, child_front))
     pivot = gathered(pieces[0, :80])
     pieces, pivot = lax.optimization_barrier((pieces, pivot))
     fan = fanned(fan_tops_kernel, pieces, (16, 2, B, B), [])
     fan, pivot = lax.optimization_barrier((fan, pivot))
     tops = exchanged(fan).reshape(16, 2 * B, B)
     child_x = inverse_whole(pivot)
-    child_panel, keep, send = corner(ids, child_map, child_front, tops, child_x, parent_vals)
+    child_panel = panel_of(child_front, child_x)
+    keep, send = corner(ids, child_map, child_front, child_panel, tops, child_x, parent_vals)
     summed, panel_later = lax.optimization_barrier((keep + sibling(send), child_panel))
     parts = exchanged(summed)
     keep, send = schur(ids, child_map, child_front, panel_later, child_x, tops)
@@ -497,7 +531,7 @@
     fan = fanned(fan_corner_kernel, parts, (16, 104, B), [pltpu.VMEM((104, B), F32)])
     mine = exchanged(fan)
     lower, upper = own_halves(keep, sibling(send))
-    mine, lower = lax.optimization_barrier((mine, lower))
+    mine, _ = lax.optimization_barrier((mine, lower))
     theirs = sibling(mine[:, :40])
     top_theirs = sibling(mine[:, 40:])
     arrived = lax.ppermute(lower, "tile", [(i, i - 1) for i in range(1, 16)])

time: 157 us -> 150 us (0.955)
  waiting for transfers between devices: 39.7 us -> 29.7 us
  Pallas kernels: 60.5 us -> 63.9 us
    all_to_all x3, waiting for transfers between devices: 30.8 us -> 25.8 us  [exchanged(): return lax.all_to_all(x, 'tile', 0, 0)]
    ppermute x1, waiting for transfers between devices: 4.97 us -> 0.01 us  [local(): arrived = lax.ppermute(lower, 'tile', [(i, i - 1) for i in range(1, 16)])]
    pallas_call x1 -> x2, Pallas kernels: 7.39 us -> 9.53 us  [the longest x1 5.97 us: corner(): pl.pallas_call(corner_kernel, out_shape=[jax.ShapeDtypeStruct((16, 104, B...]
  transfers between devices with their start and end apart: 9 -> 9, of which waited for: 6 -> 5; matrix products, arithmetic and copies ran while one was open for 0% -> 0% of each run, Pallas kernels for 30% -> 33%
where the time goes in v5:
time: 150 us
  Pallas kernels  63.9 us (43%)
  blocking collectives  38.7 us (26%)
  waiting for transfers between devices  29.7 us (20%)
  starting transfers between devices  13.9 us (9%)
  other arithmetic  2.53 us (2%)
    all_to_all x2, blocking collectives, exchanged(): return lax.all_to_all(x, 'tile', 0, 0)  38.7 us
    all_to_all x3, waiting for transfers between devices, exchanged(): return lax.all_to_all(x, 'tile', 0, 0)  25.8 us
    pallas_call x1, Pallas kernels, inverse_whole(): pl.pallas_call(whole_kernel, out_shape=pltpu.HBM((N, N), F32), in_specs=[...  17.1 us
    pallas_call x1, Pallas kernels, inverse_first(): pl.pallas_call(first_kernel, out_shape=[SQUARE] * 3, in_specs=[SMEM, VMEM...  12.7 us
    all_to_all x3, starting transfers between devices, exchanged(): return lax.all_to_all(x, 'tile', 0, 0)  11.6 us
    pallas_call x1, Pallas kernels, schur(): pl.pallas_call(schur_kernel, out_shape=[pltpu.HBM((6 * B, N), F32)] * 2,...  10.1 us
    pallas_call x1, Pallas kernels, corner(): pl.pallas_call(corner_kernel, out_shape=[jax.ShapeDtypeStruct((16, 104, B...  5.97 us
    pallas_call x1, Pallas kernels, parent_step(): pl.pallas_call(parent_kernel, out_shape=SQUARE, in_specs=[SMEM] + [VMEM]...  4.41 us
  transfers between devices with their start and end apart: 9, of which 5 were waited for; matrix products, arithmetic and copies ran while one was open for 0% of the time, Pallas kernels for 33%

profile of v5, /device:TPU:32, one launch (start us, length us, event | category | flops | bytes accessed | tf_op | source)
XLA Modules:
  0.0 149.8 jit_solution(8694646883688091142)
XLA Ops:
  0.6 0.1 pad_add_fusion.1.ids
  0.7 2.0 %shard_map.50 = f32[16,128,128]{2,1,0:T(8,128)S(1)} custom-call(s32[2]{0:T(128)S(1)} %pad_add_fusion.1.ids, f32[1,512,1536]{2,1,0:T(8,128)} %a_far.7), custom_call_target="tpu_custom_call" | custom-call | tf_op jit(solution)/shard_map/pallas_call | solution.py:223
  2.7 23.5 %all_to_all.25.parts_ref = f32[16,128,128]{2,1,0:T(8,128)S(1)} all-to-all(f32[16,128,128]{2,1,0:T(8,128)S(1)} %shard_map.50), channel_id=1, replica_groups=mesh['front'=16,'tile'=16] {'tile'}, dimensions={0} | all-to-all | bytes 2097152 | tf_op jit(solution)/shard_map/all_to_all | solution.py:501
  26.3 15.2 %all_to_all.26.a_ref = f32[16,80,128]{2,1,0:T(8,128)S(1)} all-to-all(f32[16,80,128]{2,1,0:T(8,128)S(1)} %broadcast_in_dim.14), channel_id=1, replica_groups=mesh['front'=16,'tile'=16] {'tile'}, dimensions={0} | all-to-all | bytes 1310720 | tf_op jit(solution)/shard_map/all_to_all | solution.py:501
  41.5 1.5 shard_map.51
  43.0 3.7 %all-to-all-start.2 = ((f32[16,2,128,128]{3,2,1,0:T(8,128)}), f32[16,2,128,128]{3,2,1,0:T(8,128)S(1)}, u32[]{:S(2)}, u32[]{:S(2)}) async-start(f32[16,2,128,128]{3,2,1,0:T(8,128)} %shard_map.51), calls=%async_computation.2 | async-start | bytes 4194304 | tf_op jit(solution)/shard_map/all_to_all | solution.py:501
  46.7 17.1 %shard_map.52.x_far = f32[512,512]{1,0:T(8,128)} custom-call(f32[16,80,128]{2,1,0:T(8,128)S(1)} %all_to_all.26.a_ref), custom_call_target="tpu_custom_call" | custom-call | flops 24999999488 | bytes 2097152 | tf_op jit(solution)/shard_map/pallas_call | solution.py:151
  63.8 0.0 copy-start
  63.8 3.6 %shard_map.53.panel_far = f32[512,512]{1,0:T(8,128)} custom-call(f32[1,512,1536]{2,1,0:T(8,128)} %a_far.7, f32[512,512]{1,0:T(8,128)} %shard_map.52.x_far), custom_call_target="tpu_custom_call" | custom-call | flops 1000000000 | bytes 2097152 | tf_op jit(solution)/shard_map/pallas_call | solution.py:257
  67.4 7.1 %all-to-all-done.2 = f32[16,2,128,128]{3,2,1,0:T(8,128)S(1)} async-done(((f32[16,2,128,128]{3,2,1,0:T(8,128)}), f32[16,2,128,128]{3,2,1,0:T(8,128)S(1)}, u32[]{:S(2)}, u32[]{:S(2)}) %all-to-all-start.2) | async-done | bytes 2097184 | tf_op jit(solution)/shard_map/all_to_all | solution.py:501
  74.6 0.0 copy-done
  74.6 6.0 %shard_map.54 = (f32[16,104,128]{2,1,0:T(8,128)S(1)}, f32[16,104,128]{2,1,0:T(8,128)S(1)}) custom-call(s32[2]{0:T(128)S(1)} %pad_add_fusion.1.ids, s32[16,60]{1,0:T(8,128)S(1)} %copy-done, f32[1,512,1536]{2,1,0:T(8,128)} %a_far.7, f32[512,512]{1,0:T(8,128)} %shard_map.53.panel_far, f32[16,256,128]{2,1,0:T(8,128)S(1)} %bitcast.9, ...), custom_call_target="tpu_custom_call" | custom-call | flops 3000000000 | bytes 2097152 | tf_op jit(solution)/shard_map/pallas_call | solution.py:314
  80.5 0.1 collective-permute-start
  80.6 2.4 %collective-permute-done = f32[16,104,128]{2,1,0:T(8,128)S(1)} collective-permute-done((f32[16,104,128]{2,1,0:T(8,128)S(1)}, f32[16,104,128]{2,1,0:T(8,128)S(1)}, u32[]{:S(2)}, u32[]{:S(2)}) %collective-permute-start) | collective-permute-done | bytes 852000 | tf_op jit(solution)/shard_map/ppermute | solution.py:509
  83.0 1.0 add.13
  84.0 4.2 %all-to-all-start.3 = ((f32[16,104,128]{2,1,0:T(8,128)}), f32[16,104,128]{2,1,0:T(8,128)S(1)}, u32[]{:S(2)}, u32[]{:S(2)}) async-start(f32[16,104,128]{2,1,0:T(8,128)} %add.13), calls=%async_computation.3 | async-start | bytes 1703936 | tf_op jit(solution)/shard_map/all_to_all | solution.py:501
  88.3 10.1 %shard_map.55 = (f32[768,512]{1,0:T(8,128)}, f32[768,512]{1,0:T(8,128)}) custom-call(s32[2]{0:T(128)S(1)} %pad_add_fusion.1.ids, s32[16,60]{1,0:T(8,128)S(1)} %copy-done, f32[1,512,1536]{2,1,0:T(8,128)} %a_far.7, f32[512,512]{1,0:T(8,128)} %shard_map.53.panel_far, f32[512,512]{1,0:T(8,128)} %shard_map.52.x_far, f32[16,256,128]{2,1,0:T(8,128)S(1)} %bitcast.10), custom_call_target="tpu_custom_call" | custom-call | flops 8000000000 | bytes 2097152 | tf_op jit(solution)/shard_map/pallas_call | solution.py:383
  98.4 5.6 %all-to-all-done.3.parts_ref = f32[16,104,128]{2,1,0:T(8,128)S(1)} async-done(((f32[16,104,128]{2,1,0:T(8,128)}), f32[16,104,128]{2,1,0:T(8,128)S(1)}, u32[]{:S(2)}, u32[]{:S(2)}) %all-to-all-start.3) | async-done | bytes 852000 | tf_op jit(solution)/shard_map/all_to_all | solution.py:501
  104.0 0.0 collective-permute-start.1
  104.0 1.0 shard_map.57
  105.0 3.6 %all-to-all-start.4 = ((f32[16,104,128]{2,1,0:T(8,128)}), f32[16,104,128]{2,1,0:T(8,128)S(1)}, u32[]{:S(2)}, u32[]{:S(2)}) async-start(f32[16,104,128]{2,1,0:T(8,128)} %shard_map.57), calls=%async_computation.4 | async-start | bytes 1703936 | tf_op jit(solution)/shard_map/all_to_all | solution.py:501
  108.6 0.0 collective-permute-done.1.recv_far
  108.7 2.0 %shard_map.56 = (f32[384,512]{1,0:T(8,128)S(1)}, f32[384,512]{1,0:T(8,128)S(1)}) custom-call(f32[768,512]{1,0:T(8,128)} %get-tuple-element.28.keep_far, f32[768,512]{1,0:T(8,128)} %collective-permute-done.1.recv_far), custom_call_target="tpu_custom_call" | custom-call | flops 1000000000 | bytes 2097152 | tf_op jit(solution)/shard_map/pallas_call | solution.py:418
  110.6 0.0 copy-start.1
  110.6 1.4 collective-permute-start.2
  112.1 13.0 %all-to-all-done.4.mine_ref = f32[16,104,128]{2,1,0:T(8,128)S(1)} async-done(((f32[16,104,128]{2,1,0:T(8,128)}), f32[16,104,128]{2,1,0:T(8,128)S(1)}, u32[]{:S(2)}, u32[]{:S(2)}) %all-to-all-start.4) | async-done | bytes 852000 | tf_op jit(solution)/shard_map/all_to_all | solution.py:501
  125.1 0.1 collective-permute-start.3
  125.2 1.6 %collective-permute-done.3.theirs_ref = f32[16,40,128]{2,1,0:T(8,128)S(1)} collective-permute-done((f32[16,40,128]{2,1,0:T(8,128)S(1)}, f32[16,40,128]{2,1,0:T(8,128)S(1)}, u32[]{:S(2)}, u32[]{:S(2)}) %collective-permute-start.3) | collective-permute-done | bytes 327712 | tf_op jit(solution)/shard_map/ppermute | solution.py:509
  126.8 12.7 %shard_map.58 = (f32[512,512]{1,0:T(8,128)S(1)}, f32[512,512]{1,0:T(8,128)S(1)}, f32[512,512]{1,0:T(8,128)S(1)}) custom-call(s32[2]{0:T(128)S(1)} %pad_add_fusion.1.ids, f32[16,104,128]{2,1,0:T(8,128)S(1)} %all-to-all-done.4.mine_ref, f32[16,40,128]{2,1,0:T(8,128)S(1)} %collective-permute-done.3.theirs_ref), custom_call_target="tpu_custom_call" | custom-call | flops 1000000000 | bytes 2097152 | tf_op jit(solution)/shard_map/pallas_call | solution.py:163
  139.6 0.0 collective-permute-done.2
  139.6 0.0 copy-done.1
  139.6 1.4 pad_add_fusion.own_ref
  141.1 0.2 collective-permute-start.4
  141.3 0.5 collective-permute-start.5
  141.8 3.6 %shard_map.59.x_ref = f32[512,512]{1,0:T(8,128)S(1)} custom-call(f32[512,512]{1,0:T(8,128)S(1)} %get-tuple-element.36.xin_ref, f32[512,512]{1,0:T(8,128)S(1)} %get-tuple-element.38.s_ref, f32[512,512]{1,0:T(8,128)S(1)} %get-tuple-element.39.l_ref), custom_call_target="tpu_custom_call" | custom-call | flops 6000000000 | bytes 2097152 | tf_op jit(solution)/shard_map/pallas_call | solution.py:175
  145.4 0.0 collective-permute-done.5.theirs_ref
  145.4 0.0 collective-permute-done.4.other_ref
  145.4 4.4 %shard_map.60 = f32[512,512]{1,0:T(8,128)} custom-call(s32[2]{0:T(128)S(1)} %pad_add_fusion.1.ids, f32[512,512]{1,0:T(8,128)S(1)} %pad_add_fusion.own_ref, f32[512,512]{1,0:T(8,128)S(1)} %collective-permute-done.4.other_ref, f32[512,512]{1,0:T(8,128)S(1)} %shard_map.59.x_ref, f32[16,104,128]{2,1,0:T(8,128)S(1)} %all-to-all-done.4.mine_ref, ...), custom_call_target="tpu_custom_call" | custom-call | flops 4000000000 | bytes 2097152 | tf_op jit(solution)/shard_map/pallas_call | solution.py:455
  (4 shorter events, 0.1 us)
Async XLA Ops:
  43.0 31.6 %all-to-all-start.2 = ((f32[16,2,128,128]{3,2,1,0:T(8,128)}), f32[16,2,128,128]{3,2,1,0:T(8,128)S(1)}, u32[]{:S(2)}, u32[]{:S(2)}) async-start(f32[16,2,128,128]{3,2,1,0:T(8,128)} %shard_map.51), calls=%async_computation.2 | async-start | bytes 4194304 | tf_op jit(solution)/shard_map/all_to_all | solution.py:501
  63.8 10.7 %copy-start = (s32[16,60]{1,0:T(8,128)S(1)}, s32[16,60]{1,0:T(8,128)}, u32[]{:S(2)}) copy-start(s32[16,60]{1,0:T(8,128)} %cmap.3) | copy-start | bytes 11524
  80.5 2.5 %collective-permute-start = (f32[16,104,128]{2,1,0:T(8,128)S(1)}, f32[16,104,128]{2,1,0:T(8,128)S(1)}, u32[]{:S(2)}, u32[]{:S(2)}) collective-permute-start(f32[16,104,128]{2,1,0:T(8,128)S(1)} %get-tuple-element.26), channel_id=1, source_target_pairs={{0,16},{16,0},{32,48},{48,32},{64,80},{80,64},{96,112},{112,96},{1... | collective-permute-start | bytes 2555912 | tf_op jit(solution)/shard_map/ppermute | solution.py:509
  84.0 19.9 %all-to-all-start.3 = ((f32[16,104,128]{2,1,0:T(8,128)}), f32[16,104,128]{2,1,0:T(8,128)S(1)}, u32[]{:S(2)}, u32[]{:S(2)}) async-start(f32[16,104,128]{2,1,0:T(8,128)} %add.13), calls=%async_computation.3 | async-start | bytes 1703936 | tf_op jit(solution)/shard_map/all_to_all | solution.py:501
  104.0 4.7 %collective-permute-start.1 = (f32[768,512]{1,0:T(8,128)}, f32[768,512]{1,0:T(8,128)}, u32[]{:S(2)}, u32[]{:S(2)}) collective-permute-start(f32[768,512]{1,0:T(8,128)} %get-tuple-element.31), channel_id=1, source_target_pairs={{0,16},{16,0},{32,48},{48,32},{64,80},{80,64},{96,112},{112,96},{1... | collective-permute-start | bytes 4718600 | tf_op jit(solution)/shard_map/ppermute | solution.py:509
  105.0 20.1 %all-to-all-start.4 = ((f32[16,104,128]{2,1,0:T(8,128)}), f32[16,104,128]{2,1,0:T(8,128)S(1)}, u32[]{:S(2)}, u32[]{:S(2)}) async-start(f32[16,104,128]{2,1,0:T(8,128)} %shard_map.57), calls=%async_computation.4 | async-start | bytes 1703936 | tf_op jit(solution)/shard_map/all_to_all | solution.py:501
  110.6 29.0 %copy-start.1 = (f32[1,512,512]{2,1,0:T(8,128)S(1)}, f32[1,512,512]{2,1,0:T(8,128)}, u32[]{:S(2)}) copy-start(f32[1,512,512]{2,1,0:T(8,128)} %param.4) | copy-start | bytes 3145732
  110.6 29.0 %collective-permute-start.2 = (f32[384,512]{1,0:T(8,128)S(1)}, f32[384,512]{1,0:T(8,128)}, u32[]{:S(2)}, u32[]{:S(2)}) collective-permute-start(f32[384,512]{1,0:T(8,128)S(1)} %get-tuple-element.33), channel_id=1, source_target_pairs={{1,0},{2,1},{3,2},{4,3},{5,4},{6,5},{7,6},{8,7},{9,8},{10,9},{11,1... | collective-permute-start | bytes 2359304 | tf_op jit(solution)/shard_map/ppermute | solution.py:537
  125.1 1.7 %collective-permute-start.3 = (f32[16,40,128]{2,1,0:T(8,128)S(1)}, f32[16,40,128]{2,1,0:T(8,128)S(1)}, u32[]{:S(2)}, u32[]{:S(2)}) collective-permute-start(f32[16,40,128]{2,1,0:T(8,128)S(1)} %slice.10), channel_id=1, source_target_pairs={{0,16},{16,0},{32,48},{48,32},{64,80},{80,64},{96,112},{112,96},{1... | collective-permute-start | bytes 983048 | tf_op jit(solution)/shard_map/ppermute | solution.py:509
  141.1 4.3 %collective-permute-start.4 = (f32[512,512]{1,0:T(8,128)S(1)}, f32[512,512]{1,0:T(8,128)S(1)}, u32[]{:S(2)}, u32[]{:S(2)}) collective-permute-start(f32[512,512]{1,0:T(8,128)S(1)} %pad_add_fusion.own_ref), channel_id=1, source_target_pairs={{0,16},{16,0},{32,48},{48,32},{64,80},{80,64},{96,112},{112,96},{1... | collective-permute-start | bytes 3145736 | tf_op jit(solution)/shard_map/ppermute | solution.py:509
  141.3 4.0 %collective-permute-start.5 = (f32[16,64,128]{2,1,0:T(8,128)S(1)}, f32[16,64,128]{2,1,0:T(8,128)S(1)}, u32[]{:S(2)}, u32[]{:S(2)}) collective-permute-start(f32[16,64,128]{2,1,0:T(8,128)S(1)} %slice.11), channel_id=1, source_target_pairs={{0,16},{16,0},{32,48},{48,32},{64,80},{80,64},{96,112},{112,96},{1... | collective-permute-start | bytes 1572872 | tf_op jit(solution)/shard_map/ppermute | solution.py:509

commit v6 on v5

--- a/solution.py
+++ b/solution.py
@@ -116,9 +116,7 @@
     unpack(a_ref[...].reshape(1280, B), s_ref)
     x_ref[...] = jnp.zeros_like(x_ref)
     eliminate((0, 4), s_ref, l_ref, x_ref)
-    copy = pltpu.make_async_copy(x_ref, out_ref, sem)
-    copy.start()
-    copy.wait()
+    wait_for(*start_copies([(x_ref, out_ref)], sem))
 
 
 def first_kernel(ids, mine_ref, theirs_ref, x_ref, s_ref, l_ref, p_ref):
@@ -139,6 +137,31 @@
 FAR = pl.BlockSpec(memory_space=pltpu.HBM)
 
 
+PARTS = 4
+
+
+def start_copies(pairs, sems, first=0):
+    groups = []
+    for n, (src, dst) in enumerate(pairs):
+        step = dst.shape[0] // PARTS
+        group = []
+        for p in range(PARTS):
+            rows = pl.ds(p * step, step)
+            sem = sems.at[first + n * PARTS + p]
+            group.append(pltpu.make_async_copy(src.at[rows], dst.at[rows], sem))
+        groups.append(group)
+    for group in groups:
+        for copy in group:
+            copy.start()
+    return groups
+
+
+def wait_for(*groups):
+    for group in groups:
+        for copy in group:
+            copy.wait()
+
+
 def far(x):
     return pltpu.with_memory_space_constraint(x, pltpu.HBM)
 
@@ -153,7 +176,7 @@
         out_shape=pltpu.HBM((N, N), F32),
         in_specs=[VMEM],
         out_specs=FAR,
-        scratch_shapes=[pltpu.VMEM((N, N), F32)] * 3 + [pltpu.SemaphoreType.DMA],
+        scratch_shapes=[pltpu.VMEM((N, N), F32)] * 3 + [pltpu.SemaphoreType.DMA((PARTS,))],
         compiler_params=PARAMS,
         cost_estimate=cost(25),
     )(packed)
@@ -202,9 +225,7 @@
 
 
 def spread_kernel(ids, a_far, out_ref, a_ref, p_ref, sem):
-    copy = pltpu.make_async_copy(a_far.at[0, :, pl.ds(0, N)], a_ref, sem)
-    copy.start()
-    copy.wait()
+    wait_for(*start_copies([(a_far.at[0, :, pl.ds(0, N)], a_ref)], sem))
 
     @pl.when(ids[1] > 0)
     def _():
@@ -228,7 +249,7 @@
         scratch_shapes=[
             pltpu.VMEM((N, N), F32),
             pltpu.VMEM((1280, B), F32),
-            pltpu.SemaphoreType.DMA,
+            pltpu.SemaphoreType.DMA((PARTS,)),
         ],
         compiler_params=PARAMS,
     )(ids, far(front_vals))
@@ -239,18 +260,10 @@
 
 
 def panel_kernel(a_far, x_far, out_far, a_ref, x_ref, panel_ref, sems):
-    copies = [
-        pltpu.make_async_copy(x_far, x_ref, sems.at[0]),
-        pltpu.make_async_copy(a_far.at[0, :, pl.ds(0, N)], a_ref, sems.at[1]),
-    ]
-    for copy in copies:
-        copy.start()
-    for copy in copies:
-        copy.wait()
+    pairs = [(x_far, x_ref), (a_far.at[0, :, pl.ds(0, N)], a_ref)]
+    wait_for(*start_copies(pairs, sems))
     panel_ref[...] = dot_split(split(a_ref[...]), split(x_ref[...]))
-    copy = pltpu.make_async_copy(panel_ref, out_far, sems.at[2])
-    copy.start()
-    copy.wait()
+    wait_for(*start_copies([(panel_ref, out_far)], sems, 2 * PARTS))
 
 
 def panel_of(front_vals, x):
@@ -259,7 +272,7 @@
         out_shape=pltpu.HBM((N, N), F32),
         in_specs=[FAR, FAR],
         out_specs=FAR,
-        scratch_shapes=[pltpu.VMEM((N, N), F32)] * 3 + [pltpu.SemaphoreType.DMA((3,))],
+        scratch_shapes=[pltpu.VMEM((N, N), F32)] * 3 + [pltpu.SemaphoreType.DMA((3 * PARTS,))],
         compiler_params=PARAMS,
         cost_estimate=cost(1),
     )(far(front_vals), far(x))
@@ -269,22 +282,22 @@
     ids, cmap, a_far, panel_far, top_ref, x_far, pf_far, keep_ref, send_ref,
     a_ref, panel_ref, x_ref, pf_ref, b_ref, p_ref, sems,
 ):
-    copies = [
-        pltpu.make_async_copy(x_far, x_ref, sems.at[0]),
-        pltpu.make_async_copy(panel_far, panel_ref, sems.at[1]),
-        pltpu.make_async_copy(a_far.at[0, :, pl.ds(N, N)], a_ref, sems.at[2]),
-        pltpu.make_async_copy(pf_far, pf_ref, sems.at[3]),
-    ]
-    for copy in copies:
-        copy.start()
+    copies = start_copies(
+        [
+            (x_far, x_ref),
+            (panel_far, panel_ref),
+            (a_far.at[0, :, pl.ds(N, N)], a_ref),
+            (pf_far, pf_ref),
+        ],
+        sems,
+    )
     front, tile = ids[0], ids[1]
     parity = lax.rem(front, 2)
     raw = [top_ref[:, 32 * c : 32 * c + 32, :].reshape(N, B) for c in range(4)]
     raw = split(jnp.concatenate(raw, axis=1))
-    copies[0].wait()
+    wait_for(copies[0])
     top = split(dot_split(raw, split(x_ref[...])))
-    copies[1].wait()
-    copies[2].wait()
+    wait_for(*copies[1:3])
     b_ref[...] = jnp.zeros_like(b_ref)
     for i in range(4):
         rows = slice(i * B, (i + 1) * B)
@@ -294,7 +307,7 @@
         def _():
             b_ref[at(place_of(cmap, front, tile, i)), :] = first
 
-    copies[3].wait()
+    wait_for(copies[3])
 
     @pl.when((tile <= 1) & (parity == 1))
     def _():
@@ -320,7 +333,7 @@
         + [
             pltpu.VMEM((2 * N, N), F32),
             pltpu.VMEM((1280, B), F32),
-            pltpu.SemaphoreType.DMA((4,)),
+            pltpu.SemaphoreType.DMA((4 * PARTS,)),
         ],
         compiler_params=PARAMS,
         cost_estimate=cost(3),
@@ -331,52 +344,38 @@
     ids, cmap, a_far, panel_far, x_far, top_ref, keep_far, out_far,
     a_ref, panel_ref, x_ref, keep_ref, send_ref, sems,
 ):
-    copies = [
-        pltpu.make_async_copy(x_far, x_ref, sems.at[0]),
-        pltpu.make_async_copy(panel_far, panel_ref, sems.at[1]),
-        pltpu.make_async_copy(a_far.at[0, :, pl.ds(N, 2 * N)], a_ref, sems.at[2]),
-    ]
-    for copy in copies:
-        copy.start()
+    copies = start_copies(
+        [(x_far, x_ref), (panel_far, panel_ref), (a_far.at[0, :, pl.ds(N, 2 * N)], a_ref)], sems
+    )
     front, tile = ids[0], ids[1]
     parity = lax.rem(front, 2)
     keep_ref[...] = jnp.zeros_like(keep_ref)
     send_ref[...] = jnp.zeros_like(send_ref)
-    copies[0].wait()
+    wait_for(copies[0])
     x = split(x_ref[...])
-    tops = []
-    for h in range(2):
+    out = []
+    for h, half, ref, target in (
+        (0, parity, send_ref, out_far),
+        (1, 1 - parity, keep_ref, keep_far),
+    ):
         raw = [
-            top_ref[:, h * B + 32 * c : h * B + 32 * c + 32, :].reshape(N, B) for c in range(4)
+            top_ref[:, pl.ds(pl.multiple_of(half * B + 32 * c, 32), 32), :].reshape(N, B)
+            for c in range(4)
         ]
-        tops.append(split(dot_split(split(jnp.concatenate(raw, axis=1)), x)))
-    copies[1].wait()
-    copies[2].wait()
-    for i in range(4):
-        rows = slice(i * B, (i + 1) * B)
-        panel = split(panel_ref[rows, :])
-        place = place_of(cmap, front, tile, i)
-        first = a_ref[rows, :N] - dot_split(panel, tops[0])
-        second = a_ref[rows, N:] - dot_split(panel, tops[1])
-
-        @pl.when((tile > 0) & (parity == 1))
-        def _():
-            keep_ref[at(place - 1), :] = first
-            send_ref[at(place - 1), :] = second
-
-        @pl.when((tile > 0) & (parity == 0))
-        def _():
-            keep_ref[at(place - 1), :] = second
-            send_ref[at(place - 1), :] = first
-
-    copies = [
-        pltpu.make_async_copy(send_ref, out_far, sems.at[3]),
-        pltpu.make_async_copy(keep_ref, keep_far, sems.at[4]),
-    ]
-    for copy in copies:
-        copy.start()
-    for copy in copies:
-        copy.wait()
+        top = split(dot_split(split(jnp.concatenate(raw, axis=1)), x))
+        if h == 0:
+            wait_for(*copies[1:])
+        for i in range(4):
+            rows = slice(i * B, (i + 1) * B)
+            rest = a_ref[rows, pl.ds(pl.multiple_of(half * N, N), N)]
+            rest = rest - dot_split(split(panel_ref[rows, :]), top)
+
+            @pl.when(tile > 0)
+            def _():
+                ref[at(place_of(cmap, front, tile, i) - 1), :] = rest
+
+        out += start_copies([(ref, target)], sems, (3 + h) * PARTS)
+    wait_for(*out)
 
 
 def schur(ids, cmap, front_vals, panel, x, tops):
@@ -391,14 +390,14 @@
             pltpu.VMEM((N, N), F32),
             pltpu.VMEM((6 * B, N), F32),
             pltpu.VMEM((6 * B, N), F32),
-            pltpu.SemaphoreType.DMA((5,)),
+            pltpu.SemaphoreType.DMA((5 * PARTS,)),
         ],
         compiler_params=PARAMS,
         cost_estimate=cost(8),
     )(ids, cmap, far(front_vals), far(panel), far(x), tops)
 
 
-def own_kernel(keep_far, recv_far, lower_ref, upper_ref, buf, sems):
+def own_kernel(keep_far, recv_far, pf_far, lower_ref, base_ref, buf, pf_ref, sems):
     copies = []
     for h in range(2):
         rows = pl.ds(h * 3 * B, 3 * B)
@@ -406,24 +405,33 @@
             copies.append(
                 pltpu.make_async_copy(ref.at[rows], buf.at[2 * h + n], sems.at[2 * h + n])
             )
+    copies.append(pltpu.make_async_copy(pf_far, pf_ref, sems.at[4]))
     for copy in copies:
         copy.start()
-    for h, ref in enumerate((lower_ref, upper_ref)):
-        copies[2 * h].wait()
-        copies[2 * h + 1].wait()
-        ref[...] = buf[2 * h] + buf[2 * h + 1]
-
-
-def own_halves(keep, recv):
+    copies[0].wait()
+    copies[1].wait()
+    lower_ref[...] = buf[0] + buf[1]
+    copies[2].wait()
+    copies[3].wait()
+    copies[4].wait()
+    base_ref[: 3 * B, :] = pf_ref[: 3 * B, :] + buf[2] + buf[3]
+    base_ref[3 * B :, :] = pf_ref[3 * B :, :]
+
+
+def own_halves(keep, recv, pf):
     return pl.pallas_call(
         own_kernel,
-        out_shape=[jax.ShapeDtypeStruct((3 * B, N), F32)] * 2,
-        in_specs=[FAR, FAR],
+        out_shape=[jax.ShapeDtypeStruct((3 * B, N), F32), SQUARE],
+        in_specs=[FAR] * 3,
         out_specs=[VMEM, VMEM],
-        scratch_shapes=[pltpu.VMEM((4, 3 * B, N), F32), pltpu.SemaphoreType.DMA((4,))],
+        scratch_shapes=[
+            pltpu.VMEM((4, 3 * B, N), F32),
+            pltpu.VMEM((N, N), F32),
+            pltpu.SemaphoreType.DMA((5,)),
+        ],
         compiler_params=PARAMS,
         cost_estimate=cost(1),
-    )(far(keep), far(recv))
+    )(far(keep), far(recv), far(pf))
 
 
 def parent_kernel(ids, own_ref, other_ref, x_ref, mine_ref, theirs_ref, out_ref):
@@ -530,15 +538,13 @@
     send, parts = lax.optimization_barrier((send, parts))
     fan = fanned(fan_corner_kernel, parts, (16, 104, B), [pltpu.VMEM((104, B), F32)])
     mine = exchanged(fan)
-    lower, upper = own_halves(keep, sibling(send))
+    lower, base = own_halves(keep, sibling(send), parent_vals)
     mine, _ = lax.optimization_barrier((mine, lower))
     theirs = sibling(mine[:, :40])
     top_theirs = sibling(mine[:, 40:])
     arrived = lax.ppermute(lower, "tile", [(i, i - 1) for i in range(1, 16)])
     x, s, l = inverse_first(ids, mine, theirs)
-    assembled = (
-        parent_vals + jnp.pad(upper, ((0, B), (0, 0))) + jnp.pad(arrived, ((B, 0), (0, 0)))
-    )
+    assembled = jnp.concatenate([base[:B], base[B:] + arrived], axis=0)
     assembled, _ = lax.optimization_barrier((assembled, x))
     other = sibling(assembled)
     parent_x = inverse_last(x, s, l)

time: 150 us -> 149 us (level)
  transfers between devices with their start and end apart: 9 -> 9, of which waited for: 5 -> 5; matrix products, arithmetic and copies ran while one was open for 0% -> 0% of each run, Pallas kernels for 33% -> 34%
where the time goes in v6:
time: 149 us
  Pallas kernels  64.7 us (43%)
  blocking collectives  38.7 us (26%)
  waiting for transfers between devices  29.1 us (20%)
  starting transfers between devices  13.7 us (9%)
    all_to_all x2, blocking collectives, exchanged(): return lax.all_to_all(x, 'tile', 0, 0)  38.7 us
    all_to_all x3, waiting for transfers between devices, exchanged(): return lax.all_to_all(x, 'tile', 0, 0)  25.1 us
    pallas_call x1, Pallas kernels, inverse_whole(): pl.pallas_call(whole_kernel, out_shape=pltpu.HBM((N, N), F32), in_specs=[...  17.1 us
    pallas_call x1, Pallas kernels, inverse_first(): pl.pallas_call(first_kernel, out_shape=[SQUARE] * 3, in_specs=[SMEM, VMEM...  12.7 us
    all_to_all x3, starting transfers between devices, exchanged(): return lax.all_to_all(x, 'tile', 0, 0)  11.6 us
    pallas_call x1, Pallas kernels, schur(): pl.pallas_call(schur_kernel, out_shape=[pltpu.HBM((6 * B, N), F32)] * 2,...  10.4 us
    pallas_call x1, Pallas kernels, corner(): pl.pallas_call(corner_kernel, out_shape=[jax.ShapeDtypeStruct((16, 104, B...  6.03 us
    pallas_call x1, Pallas kernels, parent_step(): pl.pallas_call(parent_kernel, out_shape=SQUARE, in_specs=[SMEM] + [VMEM]...  4.39 us
  transfers between devices with their start and end apart: 9, of which 5 were waited for; matrix products, arithmetic and copies ran while one was open for 0% of the time, Pallas kernels for 34%

profile of v6, /device:TPU:32, one launch (start us, length us, event | category | flops | bytes accessed | tf_op | source)
XLA Modules:
  0.0 148.6 jit_solution(8853841488827452461)
XLA Ops:
  0.6 0.1 pad_add_fusion.ids
  0.7 2.0 %shard_map.50 = f32[16,128,128]{2,1,0:T(8,128)S(1)} custom-call(s32[2]{0:T(128)S(1)} %pad_add_fusion.ids, f32[1,512,1536]{2,1,0:T(8,128)} %a_far.7), custom_call_target="tpu_custom_call" | custom-call | tf_op jit(solution)/shard_map/pallas_call | solution.py:244
  2.7 23.5 %all_to_all.25.parts_ref = f32[16,128,128]{2,1,0:T(8,128)S(1)} all-to-all(f32[16,128,128]{2,1,0:T(8,128)S(1)} %shard_map.50), channel_id=1, replica_groups=mesh['front'=16,'tile'=16] {'tile'}, dimensions={0} | all-to-all | bytes 2097152 | tf_op jit(solution)/shard_map/all_to_all | solution.py:509
  26.3 15.2 %all_to_all.26.a_ref = f32[16,80,128]{2,1,0:T(8,128)S(1)} all-to-all(f32[16,80,128]{2,1,0:T(8,128)S(1)} %broadcast_in_dim.14), channel_id=1, replica_groups=mesh['front'=16,'tile'=16] {'tile'}, dimensions={0} | all-to-all | bytes 1310720 | tf_op jit(solution)/shard_map/all_to_all | solution.py:509
  41.5 1.5 shard_map.51
  43.0 3.7 %all-to-all-start.2 = ((f32[16,2,128,128]{3,2,1,0:T(8,128)}), f32[16,2,128,128]{3,2,1,0:T(8,128)S(1)}, u32[]{:S(2)}, u32[]{:S(2)}) async-start(f32[16,2,128,128]{3,2,1,0:T(8,128)} %shard_map.51), calls=%async_computation.2 | async-start | bytes 4194304 | tf_op jit(solution)/shard_map/all_to_all | solution.py:509
  46.7 17.1 %shard_map.52.x_far = f32[512,512]{1,0:T(8,128)} custom-call(f32[16,80,128]{2,1,0:T(8,128)S(1)} %all_to_all.26.a_ref), custom_call_target="tpu_custom_call" | custom-call | flops 24999999488 | bytes 2097152 | tf_op jit(solution)/shard_map/pallas_call | solution.py:174
  63.8 0.0 copy-start
  63.8 3.6 %shard_map.53.panel_far = f32[512,512]{1,0:T(8,128)} custom-call(f32[1,512,1536]{2,1,0:T(8,128)} %a_far.7, f32[512,512]{1,0:T(8,128)} %shard_map.52.x_far), custom_call_target="tpu_custom_call" | custom-call | flops 1000000000 | bytes 2097152 | tf_op jit(solution)/shard_map/pallas_call | solution.py:270
  67.4 7.1 %all-to-all-done.2 = f32[16,2,128,128]{3,2,1,0:T(8,128)S(1)} async-done(((f32[16,2,128,128]{3,2,1,0:T(8,128)}), f32[16,2,128,128]{3,2,1,0:T(8,128)S(1)}, u32[]{:S(2)}, u32[]{:S(2)}) %all-to-all-start.2) | async-done | bytes 2097184 | tf_op jit(solution)/shard_map/all_to_all | solution.py:509
  74.5 0.0 copy-done
  74.5 6.0 %shard_map.54 = (f32[16,104,128]{2,1,0:T(8,128)S(1)}, f32[16,104,128]{2,1,0:T(8,128)S(1)}) custom-call(s32[2]{0:T(128)S(1)} %pad_add_fusion.ids, s32[16,60]{1,0:T(8,128)S(1)} %copy-done, f32[1,512,1536]{2,1,0:T(8,128)} %a_far.7, f32[512,512]{1,0:T(8,128)} %shard_map.53.panel_far, f32[16,256,128]{2,1,0:T(8,128)S(1)} %bitcast.8, f32[512,512]{1,0:T(8,128)} %shard_map.52.x_far, ...), custom_call_target="tpu_custom_call" | custom-call | flops 3000000000 | bytes 2097152 | tf_op jit(solution)/shard_map/pallas_call | solution.py:327
  80.6 0.1 collective-permute-start
  80.7 2.4 %collective-permute-done = f32[16,104,128]{2,1,0:T(8,128)S(1)} collective-permute-done((f32[16,104,128]{2,1,0:T(8,128)S(1)}, f32[16,104,128]{2,1,0:T(8,128)S(1)}, u32[]{:S(2)}, u32[]{:S(2)}) %collective-permute-start) | collective-permute-done | bytes 852000 | tf_op jit(solution)/shard_map/ppermute | solution.py:517
  83.1 1.0 add.6
  84.1 4.2 %all-to-all-start.3 = ((f32[16,104,128]{2,1,0:T(8,128)}), f32[16,104,128]{2,1,0:T(8,128)S(1)}, u32[]{:S(2)}, u32[]{:S(2)}) async-start(f32[16,104,128]{2,1,0:T(8,128)} %add.6), calls=%async_computation.3 | async-start | bytes 1703936 | tf_op jit(solution)/shard_map/all_to_all | solution.py:509
  88.3 10.4 %shard_map.55 = (f32[768,512]{1,0:T(8,128)}, f32[768,512]{1,0:T(8,128)}) custom-call(s32[2]{0:T(128)S(1)} %pad_add_fusion.ids, s32[16,60]{1,0:T(8,128)S(1)} %copy-done, f32[1,512,1536]{2,1,0:T(8,128)} %a_far.7, f32[512,512]{1,0:T(8,128)} %shard_map.53.panel_far, f32[512,512]{1,0:T(8,128)} %shard_map.52.x_far, f32[16,256,128]{2,1,0:T(8,128)S(1)} %bitcast.9), custom_call_target="tpu_custom_call" | custom-call | flops 8000000000 | bytes 2097152 | tf_op jit(solution)/shard_map/pallas_call | solution.py:382
  98.7 5.2 %all-to-all-done.3.parts_ref = f32[16,104,128]{2,1,0:T(8,128)S(1)} async-done(((f32[16,104,128]{2,1,0:T(8,128)}), f32[16,104,128]{2,1,0:T(8,128)S(1)}, u32[]{:S(2)}, u32[]{:S(2)}) %all-to-all-start.3) | async-done | bytes 852000 | tf_op jit(solution)/shard_map/all_to_all | solution.py:509
  104.0 0.0 collective-permute-start.1
  104.0 1.0 shard_map.57
  105.0 3.6 %all-to-all-start.4 = ((f32[16,104,128]{2,1,0:T(8,128)}), f32[16,104,128]{2,1,0:T(8,128)S(1)}, u32[]{:S(2)}, u32[]{:S(2)}) async-start(f32[16,104,128]{2,1,0:T(8,128)} %shard_map.57), calls=%async_computation.4 | async-start | bytes 1703936 | tf_op jit(solution)/shard_map/all_to_all | solution.py:509
  108.7 0.0 collective-permute-done.1.recv_far
  108.7 2.4 %shard_map.56 = (f32[384,512]{1,0:T(8,128)S(1)}, f32[512,512]{1,0:T(8,128)S(1)}) custom-call(f32[768,512]{1,0:T(8,128)} %get-tuple-element.28.keep_far, f32[768,512]{1,0:T(8,128)} %collective-permute-done.1.recv_far, f32[512,512]{1,0:T(8,128)} %bitcast.12), custom_call_target="tpu_custom_call" | custom-call | flops 1000000000 | bytes 2097152 | tf_op jit(solution)/shard_map/pallas_call | solution.py:422
  111.0 1.3 collective-permute-start.2
  112.3 12.8 %all-to-all-done.4.mine_ref = f32[16,104,128]{2,1,0:T(8,128)S(1)} async-done(((f32[16,104,128]{2,1,0:T(8,128)}), f32[16,104,128]{2,1,0:T(8,128)S(1)}, u32[]{:S(2)}, u32[]{:S(2)}) %all-to-all-start.4) | async-done | bytes 852000 | tf_op jit(solution)/shard_map/all_to_all | solution.py:509
  125.1 0.1 collective-permute-start.3
  125.3 1.6 %collective-permute-done.3.theirs_ref = f32[16,40,128]{2,1,0:T(8,128)S(1)} collective-permute-done((f32[16,40,128]{2,1,0:T(8,128)S(1)}, f32[16,40,128]{2,1,0:T(8,128)S(1)}, u32[]{:S(2)}, u32[]{:S(2)}) %collective-permute-start.3) | collective-permute-done | bytes 327712 | tf_op jit(solution)/shard_map/ppermute | solution.py:517
  126.8 12.7 %shard_map.58 = (f32[512,512]{1,0:T(8,128)S(1)}, f32[512,512]{1,0:T(8,128)S(1)}, f32[512,512]{1,0:T(8,128)S(1)}) custom-call(s32[2]{0:T(128)S(1)} %pad_add_fusion.ids, f32[16,104,128]{2,1,0:T(8,128)S(1)} %all-to-all-done.4.mine_ref, f32[16,40,128]{2,1,0:T(8,128)S(1)} %collective-permute-done.3.theirs_ref), custom_call_target="tpu_custom_call" | custom-call | flops 1000000000 | bytes 2097152 | tf_op jit(solution)/shard_map/pallas_call | solution.py:186
  139.6 0.0 collective-permute-done.2
  139.6 0.1 slice_add_fusion
  139.8 0.1 pad_maximum_fusion.own_ref
  139.8 0.2 collective-permute-start.4
  140.1 0.5 collective-permute-start.5
  140.6 3.6 %shard_map.59.x_ref = f32[512,512]{1,0:T(8,128)S(1)} custom-call(f32[512,512]{1,0:T(8,128)S(1)} %get-tuple-element.36.xin_ref, f32[512,512]{1,0:T(8,128)S(1)} %get-tuple-element.38.s_ref, f32[512,512]{1,0:T(8,128)S(1)} %get-tuple-element.39.l_ref), custom_call_target="tpu_custom_call" | custom-call | flops 6000000000 | bytes 2097152 | tf_op jit(solution)/shard_map/pallas_call | solution.py:198
  144.1 0.0 collective-permute-done.5.theirs_ref
  144.1 0.0 collective-permute-done.4.other_ref
  144.2 4.4 %shard_map.60 = f32[512,512]{1,0:T(8,128)} custom-call(s32[2]{0:T(128)S(1)} %pad_add_fusion.ids, f32[512,512]{1,0:T(8,128)S(1)} %pad_maximum_fusion.own_ref, f32[512,512]{1,0:T(8,128)S(1)} %collective-permute-done.4.other_ref, f32[512,512]{1,0:T(8,128)S(1)} %shard_map.59.x_ref, f32[16,104,128]{2,1,0:T(8,128)S(1)} %all-to-all-done.4.mine_ref, ...), custom_call_target="tpu_custom_call" | custom-call | flops 4000000000 | bytes 2097152 | tf_op jit(solution)/shard_map/pallas_call | solution.py:463
  (5 shorter events, 0.1 us)
Async XLA Ops:
  43.0 31.6 %all-to-all-start.2 = ((f32[16,2,128,128]{3,2,1,0:T(8,128)}), f32[16,2,128,128]{3,2,1,0:T(8,128)S(1)}, u32[]{:S(2)}, u32[]{:S(2)}) async-start(f32[16,2,128,128]{3,2,1,0:T(8,128)} %shard_map.51), calls=%async_computation.2 | async-start | bytes 4194304 | tf_op jit(solution)/shard_map/all_to_all | solution.py:509
  63.8 10.7 %copy-start = (s32[16,60]{1,0:T(8,128)S(1)}, s32[16,60]{1,0:T(8,128)}, u32[]{:S(2)}) copy-start(s32[16,60]{1,0:T(8,128)} %cmap.3) | copy-start | bytes 11524
  80.6 2.5 %collective-permute-start = (f32[16,104,128]{2,1,0:T(8,128)S(1)}, f32[16,104,128]{2,1,0:T(8,128)S(1)}, u32[]{:S(2)}, u32[]{:S(2)}) collective-permute-start(f32[16,104,128]{2,1,0:T(8,128)S(1)} %get-tuple-element.26), channel_id=1, source_target_pairs={{0,16},{16,0},{32,48},{48,32},{64,80},{80,64},{96,112},{112,96},{1... | collective-permute-start | bytes 2555912 | tf_op jit(solution)/shard_map/ppermute | solution.py:517
  84.1 19.9 %all-to-all-start.3 = ((f32[16,104,128]{2,1,0:T(8,128)}), f32[16,104,128]{2,1,0:T(8,128)S(1)}, u32[]{:S(2)}, u32[]{:S(2)}) async-start(f32[16,104,128]{2,1,0:T(8,128)} %add.6), calls=%async_computation.3 | async-start | bytes 1703936 | tf_op jit(solution)/shard_map/all_to_all | solution.py:509
  104.0 4.7 %collective-permute-start.1 = (f32[768,512]{1,0:T(8,128)}, f32[768,512]{1,0:T(8,128)}, u32[]{:S(2)}, u32[]{:S(2)}) collective-permute-start(f32[768,512]{1,0:T(8,128)} %get-tuple-element.31), channel_id=1, source_target_pairs={{0,16},{16,0},{32,48},{48,32},{64,80},{80,64},{96,112},{112,96},{1... | collective-permute-start | bytes 4718600 | tf_op jit(solution)/shard_map/ppermute | solution.py:517
  105.0 20.1 %all-to-all-start.4 = ((f32[16,104,128]{2,1,0:T(8,128)}), f32[16,104,128]{2,1,0:T(8,128)S(1)}, u32[]{:S(2)}, u32[]{:S(2)}) async-start(f32[16,104,128]{2,1,0:T(8,128)} %shard_map.57), calls=%async_computation.4 | async-start | bytes 1703936 | tf_op jit(solution)/shard_map/all_to_all | solution.py:509
  111.0 28.6 %collective-permute-start.2 = (f32[384,512]{1,0:T(8,128)S(1)}, f32[384,512]{1,0:T(8,128)S(1)}, u32[]{:S(2)}, u32[]{:S(2)}) collective-permute-start(f32[384,512]{1,0:T(8,128)S(1)} %get-tuple-element.33), channel_id=1, source_target_pairs={{1,0},{2,1},{3,2},{4,3},{5,4},{6,5},{7,6},{8,7},{9,8},{10,9},{11,1... | collective-permute-start | bytes 2359304 | tf_op jit(solution)/shard_map/ppermute | solution.py:545
  125.1 1.7 %collective-permute-start.3 = (f32[16,40,128]{2,1,0:T(8,128)S(1)}, f32[16,40,128]{2,1,0:T(8,128)S(1)}, u32[]{:S(2)}, u32[]{:S(2)}) collective-permute-start(f32[16,40,128]{2,1,0:T(8,128)S(1)} %slice.18), channel_id=1, source_target_pairs={{0,16},{16,0},{32,48},{48,32},{64,80},{80,64},{96,112},{112,96},{1... | collective-permute-start | bytes 983048 | tf_op jit(solution)/shard_map/ppermute | solution.py:517
  139.8 4.3 %collective-permute-start.4 = (f32[512,512]{1,0:T(8,128)S(1)}, f32[512,512]{1,0:T(8,128)S(1)}, u32[]{:S(2)}, u32[]{:S(2)}) collective-permute-start(f32[512,512]{1,0:T(8,128)S(1)} %pad_maximum_fusion.own_ref), channel_id=1, source_target_pairs={{0,16},{16,0},{32,48},{48,32},{64,80},{80,64},{96,112},{112,96},{1... | collective-permute-start | bytes 3145736 | tf_op jit(solution)/shard_map/ppermute | solution.py:517
  140.1 4.0 %collective-permute-start.5 = (f32[16,64,128]{2,1,0:T(8,128)S(1)}, f32[16,64,128]{2,1,0:T(8,128)S(1)}, u32[]{:S(2)}, u32[]{:S(2)}) collective-permute-start(f32[16,64,128]{2,1,0:T(8,128)S(1)} %slice.19), channel_id=1, source_target_pairs={{0,16},{16,0},{32,48},{48,32},{64,80},{80,64},{96,112},{112,96},{1... | collective-permute-start | bytes 1572872 | tf_op jit(solution)/shard_map/ppermute | solution.py:517

commit v7 on v6

--- a/solution.py
+++ b/solution.py
@@ -7,6 +7,7 @@
 
 B = 128
 N = 512
+NEAR = 2
 NT = ((1,), (1,))
 NN = ((1,), (0,))
 F32 = jnp.float32
@@ -49,23 +50,25 @@
             v = jnp.where(hit, vr * recip, v - scale * vr)
             xv = jnp.where(hit, xr * recip, xv - scale * xr)
         out.append(xf * lax.rsqrt(diag))
-        if p < 14:
-            rest = jnp.concatenate(left[p + 2 :], axis=0)
+        near = min(p + NEAR, 15)
+        if near < 15:
+            rest = jnp.concatenate(left[near + 1 :], axis=0)
             group = lax.broadcasted_iota(jnp.int32, rest.shape, 1) // 8
             rest = split(jnp.where(group == p, rest, 0.0))
             wide = [jnp.concatenate([v, xv], axis=1), jnp.zeros((120 - 8 * p, 2 * B), F32)]
             if p > 0:
                 wide = [jnp.zeros((8 * p, 2 * B), F32)] + wide
             both = dot_split(rest, split(jnp.concatenate(wide, axis=0)), NN)
-        if p < 15:
-            q = p + 1
+        w = [row_of(v, j) for j in range(8)]
+        xw = [row_of(xv, j) for j in range(8)]
+        for q in range(p + 1, near + 1):
             c = [column_of(left[q], 8 * p + j) for j in range(8)]
-            left[q] = left[q] - total([c[j] * row_of(v, j) for j in range(8)])
-            right[q] = right[q] - total([c[j] * row_of(xv, j) for j in range(8)])
-            for q in range(p + 2, 16):
-                rows = slice(8 * (q - p - 2), 8 * (q - p - 1))
-                left[q] = left[q] - both[rows, :B]
-                right[q] = right[q] - both[rows, B:]
+            left[q] = left[q] - total([c[j] * w[j] for j in range(8)])
+            right[q] = right[q] - total([c[j] * xw[j] for j in range(8)])
+        for q in range(near + 1, 16):
+            rows = slice(8 * (q - near - 1), 8 * (q - near))
+            left[q] = left[q] - both[rows, :B]
+            right[q] = right[q] - both[rows, B:]
     return jnp.concatenate(out, axis=0)
 
 
@@ -224,18 +227,27 @@
     )
 
 
-def spread_kernel(ids, a_far, out_ref, a_ref, p_ref, sem):
-    wait_for(*start_copies([(a_far.at[0, :, pl.ds(0, N)], a_ref)], sem))
-
-    @pl.when(ids[1] > 0)
-    def _():
-        for c in range(4):
-            out_ref[:, 32 * c : 32 * c + 32, :] = a_ref[:, c * B : (c + 1) * B].reshape(16, 32, B)
+def spread_kernel(ids, a_far, out_ref, a_ref, p_ref, sems):
+    copies = []
+    for c in range(4):
+        copy = pltpu.make_async_copy(a_far.at[0, :, pl.ds(c * B, B)], a_ref.at[c], sems.at[c])
+        copy.start()
+        copies.append(copy)
+
+    def block(i, j):
+        return a_ref[j, i * B : (i + 1) * B, :]
+
+    for c, copy in enumerate(copies):
+        copy.wait()
+
+        @pl.when(ids[1] > 0)
+        def _():
+            out_ref[:, 32 * c : 32 * c + 32, :] = a_ref[c].reshape(16, 32, B)
 
     @pl.when(ids[1] == 0)
     def _():
         for b, (i, j) in enumerate(LOWER):
-            p_ref[b * B : (b + 1) * B, :] = symmetric(a_ref, i, j)
+            p_ref[b * B : (b + 1) * B, :] = 0.5 * (block(i, j) + block(j, i).T)
         out_ref[:, :80, :] = p_ref[...].reshape(16, 80, B)
         out_ref[:, 80:, :] = jnp.zeros((16, 48, B), F32)
 
@@ -247,9 +259,9 @@
         in_specs=[SMEM, FAR],
         out_specs=VMEM,
         scratch_shapes=[
-            pltpu.VMEM((N, N), F32),
+            pltpu.VMEM((4, N, B), F32),
             pltpu.VMEM((1280, B), F32),
-            pltpu.SemaphoreType.DMA((PARTS,)),
+            pltpu.SemaphoreType.DMA((4,)),
         ],
         compiler_params=PARAMS,
     )(ids, far(front_vals))
@@ -342,7 +354,7 @@
 
 def schur_kernel(
     ids, cmap, a_far, panel_far, x_far, top_ref, keep_far, out_far,
-    a_ref, panel_ref, x_ref, keep_ref, send_ref, sems,
+    a_ref, panel_ref, x_ref, keep_ref, send_ref, ph_ref, pl_ref, sems,
 ):
     copies = start_copies(
         [(x_far, x_ref), (panel_far, panel_ref), (a_far.at[0, :, pl.ds(N, 2 * N)], a_ref)], sems
@@ -365,10 +377,11 @@
         top = split(dot_split(split(jnp.concatenate(raw, axis=1)), x))
         if h == 0:
             wait_for(*copies[1:])
+            ph_ref[...], pl_ref[...] = split(panel_ref[...])
         for i in range(4):
             rows = slice(i * B, (i + 1) * B)
             rest = a_ref[rows, pl.ds(pl.multiple_of(half * N, N), N)]
-            rest = rest - dot_split(split(panel_ref[rows, :]), top)
+            rest = rest - dot_split((ph_ref[rows, :], pl_ref[rows, :]), top)
 
             @pl.when(tile > 0)
             def _():
@@ -390,6 +403,8 @@
             pltpu.VMEM((N, N), F32),
             pltpu.VMEM((6 * B, N), F32),
             pltpu.VMEM((6 * B, N), F32),
+            pltpu.VMEM((N, N), jnp.bfloat16),
+            pltpu.VMEM((N, N), jnp.bfloat16),
             pltpu.SemaphoreType.DMA((5 * PARTS,)),
         ],
         compiler_params=PARAMS,

time: 149 us -> 148 us (level)
  no operation moved by 1% of the time
where the time goes in v7:
time: 148 us
  Pallas kernels  63.7 us (43%)
  blocking collectives  38.7 us (26%)
  waiting for transfers between devices  29.5 us (20%)
  starting transfers between devices  13.7 us (9%)
    all_to_all x2, blocking collectives, exchanged(): return lax.all_to_all(x, 'tile', 0, 0)  38.7 us
    all_to_all x3, waiting for transfers between devices, exchanged(): return lax.all_to_all(x, 'tile', 0, 0)  25.6 us
    pallas_call x1, Pallas kernels, inverse_whole(): pl.pallas_call(whole_kernel, out_shape=pltpu.HBM((N, N), F32), in_specs=[...  16.5 us
    pallas_call x1, Pallas kernels, inverse_first(): pl.pallas_call(first_kernel, out_shape=[SQUARE] * 3, in_specs=[SMEM, VMEM...  12.3 us
    all_to_all x3, starting transfers between devices, exchanged(): return lax.all_to_all(x, 'tile', 0, 0)  11.6 us
    pallas_call x1, Pallas kernels, schur(): pl.pallas_call(schur_kernel, out_shape=[pltpu.HBM((6 * B, N), F32)] * 2,...  10.5 us
    pallas_call x1, Pallas kernels, corner(): pl.pallas_call(corner_kernel, out_shape=[jax.ShapeDtypeStruct((16, 104, B...  6.03 us
    pallas_call x1, Pallas kernels, parent_step(): pl.pallas_call(parent_kernel, out_shape=SQUARE, in_specs=[SMEM] + [VMEM]...  4.39 us
  transfers between devices with their start and end apart: 9, of which 5 were waited for; matrix products, arithmetic and copies ran while one was open for 0% of the time, Pallas kernels for 34%

profile of v7, /device:TPU:32, one launch (start us, length us, event | category | flops | bytes accessed | tf_op | source)
XLA Modules:
  0.0 147.9 jit_solution(15548134926647841002)
XLA Ops:
  0.6 0.1 pad_add_fusion.ids
  0.7 2.0 %shard_map.50 = f32[16,128,128]{2,1,0:T(8,128)S(1)} custom-call(s32[2]{0:T(128)S(1)} %pad_add_fusion.ids, f32[1,512,1536]{2,1,0:T(8,128)} %a_far.7), custom_call_target="tpu_custom_call" | custom-call | tf_op jit(solution)/shard_map/pallas_call | solution.py:256
  2.7 23.5 %all_to_all.25.parts_ref = f32[16,128,128]{2,1,0:T(8,128)S(1)} all-to-all(f32[16,128,128]{2,1,0:T(8,128)S(1)} %shard_map.50), channel_id=1, replica_groups=mesh['front'=16,'tile'=16] {'tile'}, dimensions={0} | all-to-all | bytes 2097152 | tf_op jit(solution)/shard_map/all_to_all | solution.py:524
  26.2 15.2 %all_to_all.26.a_ref = f32[16,80,128]{2,1,0:T(8,128)S(1)} all-to-all(f32[16,80,128]{2,1,0:T(8,128)S(1)} %broadcast_in_dim.14), channel_id=1, replica_groups=mesh['front'=16,'tile'=16] {'tile'}, dimensions={0} | all-to-all | bytes 1310720 | tf_op jit(solution)/shard_map/all_to_all | solution.py:524
  41.5 1.5 shard_map.51
  42.9 3.7 %all-to-all-start.2 = ((f32[16,2,128,128]{3,2,1,0:T(8,128)}), f32[16,2,128,128]{3,2,1,0:T(8,128)S(1)}, u32[]{:S(2)}, u32[]{:S(2)}) async-start(f32[16,2,128,128]{3,2,1,0:T(8,128)} %shard_map.51), calls=%async_computation.2 | async-start | bytes 4194304 | tf_op jit(solution)/shard_map/all_to_all | solution.py:524
  46.7 16.5 %shard_map.52.x_far = f32[512,512]{1,0:T(8,128)} custom-call(f32[16,80,128]{2,1,0:T(8,128)S(1)} %all_to_all.26.a_ref), custom_call_target="tpu_custom_call" | custom-call | flops 24999999488 | bytes 2097152 | tf_op jit(solution)/shard_map/pallas_call | solution.py:177
  63.2 0.0 copy-start
  63.2 3.6 %shard_map.53.panel_far = f32[512,512]{1,0:T(8,128)} custom-call(f32[1,512,1536]{2,1,0:T(8,128)} %a_far.7, f32[512,512]{1,0:T(8,128)} %shard_map.52.x_far), custom_call_target="tpu_custom_call" | custom-call | flops 1000000000 | bytes 2097152 | tf_op jit(solution)/shard_map/pallas_call | solution.py:282
  66.8 7.7 %all-to-all-done.2 = f32[16,2,128,128]{3,2,1,0:T(8,128)S(1)} async-done(((f32[16,2,128,128]{3,2,1,0:T(8,128)}), f32[16,2,128,128]{3,2,1,0:T(8,128)S(1)}, u32[]{:S(2)}, u32[]{:S(2)}) %all-to-all-start.2) | async-done | bytes 2097184 | tf_op jit(solution)/shard_map/all_to_all | solution.py:524
  74.5 0.0 copy-done
  74.5 6.0 %shard_map.54 = (f32[16,104,128]{2,1,0:T(8,128)S(1)}, f32[16,104,128]{2,1,0:T(8,128)S(1)}) custom-call(s32[2]{0:T(128)S(1)} %pad_add_fusion.ids, s32[16,60]{1,0:T(8,128)S(1)} %copy-done, f32[1,512,1536]{2,1,0:T(8,128)} %a_far.7, f32[512,512]{1,0:T(8,128)} %shard_map.53.panel_far, f32[16,256,128]{2,1,0:T(8,128)S(1)} %bitcast.8, f32[512,512]{1,0:T(8,128)} %shard_map.52.x_far, ...), custom_call_target="tpu_custom_call" | custom-call | flops 3000000000 | bytes 2097152 | tf_op jit(solution)/shard_map/pallas_call | solution.py:339
  80.5 0.1 collective-permute-start
  80.6 2.4 %collective-permute-done = f32[16,104,128]{2,1,0:T(8,128)S(1)} collective-permute-done((f32[16,104,128]{2,1,0:T(8,128)S(1)}, f32[16,104,128]{2,1,0:T(8,128)S(1)}, u32[]{:S(2)}, u32[]{:S(2)}) %collective-permute-start) | collective-permute-done | bytes 852000 | tf_op jit(solution)/shard_map/ppermute | solution.py:532
  83.0 1.0 add.6
  84.0 4.2 %all-to-all-start.3 = ((f32[16,104,128]{2,1,0:T(8,128)}), f32[16,104,128]{2,1,0:T(8,128)S(1)}, u32[]{:S(2)}, u32[]{:S(2)}) async-start(f32[16,104,128]{2,1,0:T(8,128)} %add.6), calls=%async_computation.3 | async-start | bytes 1703936 | tf_op jit(solution)/shard_map/all_to_all | solution.py:524
  88.2 10.5 %shard_map.55 = (f32[768,512]{1,0:T(8,128)}, f32[768,512]{1,0:T(8,128)}) custom-call(s32[2]{0:T(128)S(1)} %pad_add_fusion.ids, s32[16,60]{1,0:T(8,128)S(1)} %copy-done, f32[1,512,1536]{2,1,0:T(8,128)} %a_far.7, f32[512,512]{1,0:T(8,128)} %shard_map.53.panel_far, f32[512,512]{1,0:T(8,128)} %shard_map.52.x_far, f32[16,256,128]{2,1,0:T(8,128)S(1)} %bitcast.9), custom_call_target="tpu_custom_call" | custom-call | flops 8000000000 | bytes 2097152 | tf_op jit(solution)/shard_map/pallas_call | solution.py:395
  98.8 5.1 %all-to-all-done.3.parts_ref = f32[16,104,128]{2,1,0:T(8,128)S(1)} async-done(((f32[16,104,128]{2,1,0:T(8,128)}), f32[16,104,128]{2,1,0:T(8,128)S(1)}, u32[]{:S(2)}, u32[]{:S(2)}) %all-to-all-start.3) | async-done | bytes 852000 | tf_op jit(solution)/shard_map/all_to_all | solution.py:524
  103.9 0.0 collective-permute-start.1
  103.9 1.0 shard_map.57
  105.0 3.6 %all-to-all-start.4 = ((f32[16,104,128]{2,1,0:T(8,128)}), f32[16,104,128]{2,1,0:T(8,128)S(1)}, u32[]{:S(2)}, u32[]{:S(2)}) async-start(f32[16,104,128]{2,1,0:T(8,128)} %shard_map.57), calls=%async_computation.4 | async-start | bytes 1703936 | tf_op jit(solution)/shard_map/all_to_all | solution.py:524
  108.6 0.0 collective-permute-done.1.recv_far
  108.6 2.4 %shard_map.56 = (f32[384,512]{1,0:T(8,128)S(1)}, f32[512,512]{1,0:T(8,128)S(1)}) custom-call(f32[768,512]{1,0:T(8,128)} %get-tuple-element.28.keep_far, f32[768,512]{1,0:T(8,128)} %collective-permute-done.1.recv_far, f32[512,512]{1,0:T(8,128)} %bitcast.12), custom_call_target="tpu_custom_call" | custom-call | flops 1000000000 | bytes 2097152 | tf_op jit(solution)/shard_map/pallas_call | solution.py:437
  111.0 1.3 collective-permute-start.2
  112.3 12.8 %all-to-all-done.4.mine_ref = f32[16,104,128]{2,1,0:T(8,128)S(1)} async-done(((f32[16,104,128]{2,1,0:T(8,128)}), f32[16,104,128]{2,1,0:T(8,128)S(1)}, u32[]{:S(2)}, u32[]{:S(2)}) %all-to-all-start.4) | async-done | bytes 852000 | tf_op jit(solution)/shard_map/all_to_all | solution.py:524
  125.1 0.1 collective-permute-start.3
  125.2 1.6 %collective-permute-done.3.theirs_ref = f32[16,40,128]{2,1,0:T(8,128)S(1)} collective-permute-done((f32[16,40,128]{2,1,0:T(8,128)S(1)}, f32[16,40,128]{2,1,0:T(8,128)S(1)}, u32[]{:S(2)}, u32[]{:S(2)}) %collective-permute-start.3) | collective-permute-done | bytes 327712 | tf_op jit(solution)/shard_map/ppermute | solution.py:532
  126.8 12.3 %shard_map.58 = (f32[512,512]{1,0:T(8,128)S(1)}, f32[512,512]{1,0:T(8,128)S(1)}, f32[512,512]{1,0:T(8,128)S(1)}) custom-call(s32[2]{0:T(128)S(1)} %pad_add_fusion.ids, f32[16,104,128]{2,1,0:T(8,128)S(1)} %all-to-all-done.4.mine_ref, f32[16,40,128]{2,1,0:T(8,128)S(1)} %collective-permute-done.3.theirs_ref), custom_call_target="tpu_custom_call" | custom-call | flops 1000000000 | bytes 2097152 | tf_op jit(solution)/shard_map/pallas_call | solution.py:189
  139.1 0.0 collective-permute-done.2
  139.1 0.1 slice_add_fusion
  139.3 0.1 pad_maximum_fusion.own_ref
  139.4 0.2 collective-permute-start.4
  139.6 0.5 collective-permute-start.5
  140.1 3.4 %shard_map.59.x_ref = f32[512,512]{1,0:T(8,128)S(1)} custom-call(f32[512,512]{1,0:T(8,128)S(1)} %get-tuple-element.36.xin_ref, f32[512,512]{1,0:T(8,128)S(1)} %get-tuple-element.38.s_ref, f32[512,512]{1,0:T(8,128)S(1)} %get-tuple-element.39.l_ref), custom_call_target="tpu_custom_call" | custom-call | flops 6000000000 | bytes 2097152 | tf_op jit(solution)/shard_map/pallas_call | solution.py:201
  143.5 0.0 collective-permute-done.5.theirs_ref
  143.5 0.0 collective-permute-done.4.other_ref
  143.5 4.4 %shard_map.60 = f32[512,512]{1,0:T(8,128)} custom-call(s32[2]{0:T(128)S(1)} %pad_add_fusion.ids, f32[512,512]{1,0:T(8,128)S(1)} %pad_maximum_fusion.own_ref, f32[512,512]{1,0:T(8,128)S(1)} %collective-permute-done.4.other_ref, f32[512,512]{1,0:T(8,128)S(1)} %shard_map.59.x_ref, f32[16,104,128]{2,1,0:T(8,128)S(1)} %all-to-all-done.4.mine_ref, ...), custom_call_target="tpu_custom_call" | custom-call | flops 4000000000 | bytes 2097152 | tf_op jit(solution)/shard_map/pallas_call | solution.py:478
  (5 shorter events, 0.1 us)
Async XLA Ops:
  42.9 31.6 %all-to-all-start.2 = ((f32[16,2,128,128]{3,2,1,0:T(8,128)}), f32[16,2,128,128]{3,2,1,0:T(8,128)S(1)}, u32[]{:S(2)}, u32[]{:S(2)}) async-start(f32[16,2,128,128]{3,2,1,0:T(8,128)} %shard_map.51), calls=%async_computation.2 | async-start | bytes 4194304 | tf_op jit(solution)/shard_map/all_to_all | solution.py:524
  63.2 11.3 %copy-start = (s32[16,60]{1,0:T(8,128)S(1)}, s32[16,60]{1,0:T(8,128)}, u32[]{:S(2)}) copy-start(s32[16,60]{1,0:T(8,128)} %cmap.3) | copy-start | bytes 11524
  80.5 2.5 %collective-permute-start = (f32[16,104,128]{2,1,0:T(8,128)S(1)}, f32[16,104,128]{2,1,0:T(8,128)S(1)}, u32[]{:S(2)}, u32[]{:S(2)}) collective-permute-start(f32[16,104,128]{2,1,0:T(8,128)S(1)} %get-tuple-element.26), channel_id=1, source_target_pairs={{0,16},{16,0},{32,48},{48,32},{64,80},{80,64},{96,112},{112,96},{1... | collective-permute-start | bytes 2555912 | tf_op jit(solution)/shard_map/ppermute | solution.py:532
  84.0 19.9 %all-to-all-start.3 = ((f32[16,104,128]{2,1,0:T(8,128)}), f32[16,104,128]{2,1,0:T(8,128)S(1)}, u32[]{:S(2)}, u32[]{:S(2)}) async-start(f32[16,104,128]{2,1,0:T(8,128)} %add.6), calls=%async_computation.3 | async-start | bytes 1703936 | tf_op jit(solution)/shard_map/all_to_all | solution.py:524
  103.9 4.7 %collective-permute-start.1 = (f32[768,512]{1,0:T(8,128)}, f32[768,512]{1,0:T(8,128)}, u32[]{:S(2)}, u32[]{:S(2)}) collective-permute-start(f32[768,512]{1,0:T(8,128)} %get-tuple-element.31), channel_id=1, source_target_pairs={{0,16},{16,0},{32,48},{48,32},{64,80},{80,64},{96,112},{112,96},{1... | collective-permute-start | bytes 4718600 | tf_op jit(solution)/shard_map/ppermute | solution.py:532
  105.0 20.1 %all-to-all-start.4 = ((f32[16,104,128]{2,1,0:T(8,128)}), f32[16,104,128]{2,1,0:T(8,128)S(1)}, u32[]{:S(2)}, u32[]{:S(2)}) async-start(f32[16,104,128]{2,1,0:T(8,128)} %shard_map.57), calls=%async_computation.4 | async-start | bytes 1703936 | tf_op jit(solution)/shard_map/all_to_all | solution.py:524
  111.0 28.1 %collective-permute-start.2 = (f32[384,512]{1,0:T(8,128)S(1)}, f32[384,512]{1,0:T(8,128)S(1)}, u32[]{:S(2)}, u32[]{:S(2)}) collective-permute-start(f32[384,512]{1,0:T(8,128)S(1)} %get-tuple-element.33), channel_id=1, source_target_pairs={{1,0},{2,1},{3,2},{4,3},{5,4},{6,5},{7,6},{8,7},{9,8},{10,9},{11,1... | collective-permute-start | bytes 2359304 | tf_op jit(solution)/shard_map/ppermute | solution.py:560
  125.1 1.7 %collective-permute-start.3 = (f32[16,40,128]{2,1,0:T(8,128)S(1)}, f32[16,40,128]{2,1,0:T(8,128)S(1)}, u32[]{:S(2)}, u32[]{:S(2)}) collective-permute-start(f32[16,40,128]{2,1,0:T(8,128)S(1)} %slice.18), channel_id=1, source_target_pairs={{0,16},{16,0},{32,48},{48,32},{64,80},{80,64},{96,112},{112,96},{1... | collective-permute-start | bytes 983048 | tf_op jit(solution)/shard_map/ppermute | solution.py:532
  139.4 4.1 %collective-permute-start.4 = (f32[512,512]{1,0:T(8,128)S(1)}, f32[512,512]{1,0:T(8,128)S(1)}, u32[]{:S(2)}, u32[]{:S(2)}) collective-permute-start(f32[512,512]{1,0:T(8,128)S(1)} %pad_maximum_fusion.own_ref), channel_id=1, source_target_pairs={{0,16},{16,0},{32,48},{48,32},{64,80},{80,64},{96,112},{112,96},{1... | collective-permute-start | bytes 3145736 | tf_op jit(solution)/shard_map/ppermute | solution.py:532
  139.6 3.8 %collective-permute-start.5 = (f32[16,64,128]{2,1,0:T(8,128)S(1)}, f32[16,64,128]{2,1,0:T(8,128)S(1)}, u32[]{:S(2)}, u32[]{:S(2)}) collective-permute-start(f32[16,64,128]{2,1,0:T(8,128)S(1)} %slice.19), channel_id=1, source_target_pairs={{0,16},{16,0},{32,48},{48,32},{64,80},{80,64},{96,112},{112,96},{1... | collective-permute-start | bytes 1572872 | tf_op jit(solution)/shard_map/ppermute | solution.py:532
